TPU v7x, 128 devices: a whole 4x4x4 slice. The times are simulated.
128 devices in a mesh: batch: 16 (over x, y), proto: 8 (over z, core).
Axes of the slice: x: 4, y: 4, z: 4, core: 2. Of those that a mesh axis runs over, the one named last changes fastest.
Arguments:
- features: bfloat16 [10, 1024, 256], P(None, 'batch'), may hold values from -6 to 6
- teacher_logits: bfloat16 [2, 1024, 65536], P(None, 'batch', 'proto'), may hold values from -12 to 12
- directions: bfloat16 [256, 65536], P(None, 'proto'), may hold values from -0.375 to 0.375
- center: float32 [65536], P('proto'), may hold values from -3 to 3
Outputs:
- grad_features: float32 [10, 1024, 256], P(None, 'batch')
- grad_directions: float32 [256, 65536], P('batch', 'proto')
- new_center: float32 [65536], P('proto')
All inputs are finite; a program needn't handle non-finite values.
Results may differ from a plain program's by a relative error of at most 0.0003.
The roundings to bfloat16 on the way count: a program that leaves them out, or rounds other values in their place, can miss the bound.
Values sent between devices are 32-bit elements; how exact they have to be, the bound alone decides.
No kernel may reach another device: no remote copies, remote signals or barrier semaphores. Data moves between devices by JAX's collectives and lax.ppermute only.
A program may use at most 128 MiB of HBM per device.

v0:
```python
import jax
import jax.numpy as jnp
from jax import lax
from jax.sharding import PartitionSpec as P


def on_device(features, teacher_logits, directions, center):
    num_global = teacher_logits.shape[0]
    crops = features.shape[0]
    num_local = crops - num_global
    images = features.shape[1] * lax.axis_size("batch")
    dim = features.shape[2]
    dirs = directions.astype(jnp.float32)
    col_norm = jnp.sqrt(jnp.sum(dirs * dirs, axis=0) + 1e-06)
    weight = dirs / col_norm
    weight_b = weight.astype(jnp.bfloat16)
    zf = features.astype(jnp.float32)
    inv_norm = 1.0 / jnp.sqrt(jnp.sum(zf * zf, axis=-1, keepdims=True) + 1e-06)
    unit = zf * inv_norm
    unit_b = unit.astype(jnp.bfloat16)
    scores = jnp.einsum("cbd,dp->cbp", unit_b, weight_b, preferred_element_type=jnp.float32) / 0.1
    tscores = (teacher_logits.astype(jnp.float32) - center) / 0.04
    col_local = jnp.sum(teacher_logits.astype(jnp.float32), axis=(0, 1))
    col_sums = lax.psum(col_local, "batch")
    s_loc = jnp.max(scores, axis=-1, keepdims=True)
    t_loc = jnp.max(tscores, axis=-1, keepdims=True)
    s_top, t_top = lax.pmax((s_loc, t_loc), "proto")
    s_exp = jnp.exp(scores - s_top)
    t_exp = jnp.exp(tscores - t_top)
    s_tot, t_tot = lax.psum(
        (jnp.sum(s_exp, axis=-1, keepdims=True), jnp.sum(t_exp, axis=-1, keepdims=True)), "proto"
    )
    student = s_exp / s_tot
    teacher = t_exp / t_tot
    both = teacher[0] + teacher[1]
    target = jnp.concatenate(
        [teacher[1][None], teacher[0][None], jnp.broadcast_to(both, (num_local,) + both.shape)],
        axis=0,
    )
    counts = jnp.concatenate(
        [jnp.ones((num_global,), jnp.float32), 2.0 * jnp.ones((num_local,), jnp.float32)]
    )
    scale = 1.0 / (0.1 * 18.0 * images)
    grad_b = ((counts[:, None, None] * student - target) * scale).astype(jnp.bfloat16)
    grad_part = jnp.einsum("cbp,dp->cbd", grad_b, weight_b, preferred_element_type=jnp.float32)
    grad_unit = lax.psum(grad_part, "proto")
    grad_features = (
        grad_unit - unit * jnp.sum(grad_unit * unit, axis=-1, keepdims=True)
    ) * inv_norm
    my_rows = dim // lax.axis_size("batch")
    row_start = lax.axis_index("batch") * my_rows
    weight_mine = lax.dynamic_slice_in_dim(weight, row_start, my_rows, 0)
    full_local = jnp.einsum("cbd,cbp->dp", unit_b, grad_b, preferred_element_type=jnp.float32)
    grad_all = lax.psum(full_local, "batch")
    dots = jnp.sum(grad_all * weight, axis=0)
    grad_mine = lax.dynamic_slice_in_dim(grad_all, row_start, my_rows, 0)
    grad_directions = (grad_mine - weight_mine * dots) / col_norm
    new_center = 0.9 * center + 0.1 * col_sums / (2.0 * images)
    return (grad_features, grad_directions, new_center)


def solution(mesh):
    in_specs = (P(None, "batch", None), P(None, "batch", "proto"), P(None, "proto"), P("proto"))
    out_specs = (P(None, "batch", None), P("batch", "proto"), P("proto"))
    return jax.shard_map(
        on_device, mesh=mesh, in_specs=in_specs, out_specs=out_specs, check_vma=False
    )
```

profile of v0, /device:TPU:0, one launch (start us, length us, event | category | flops | bytes accessed | tf_op | source)
XLA Modules:
  0.0 315.6 jit_solution(2027969032225067304)
XLA Ops:
  7.2 0.0 all-reduce.5.cloned.1.call-start
  7.2 3.1 fusion.4
  10.3 1.1 fusion.24
  11.4 0.0 copy-start.1
  11.5 0.0 copy-start.4
  11.5 12.4 %multiply_reduce_fusion = (f32[10,64]{1,0:T(8,128)S(1)}, f32[10,64,8192]{2,1,0:T(8,128)}) fusion(f32[8192]{0:T(1024)S(1)} %add_sqrt_fusion, bf16[256,8192]{1,0:T(8,128)(2,1)} %param.6, bf16[10,64,256]{2,1,0:T(8,128)(2,1)} %param.4, f32[10,64]{1,0:T(8,128)S(1)} %add_rsqrt_fusion), kind=kOutput, calls=%fused_computation.5 | convolution fusion | flops 2701622784 | bytes 25531392 | tf_op jit(solution)/shard_map/cbd,dp->cbp/dot_general | solution.py:21
  23.8 0.0 copy-done.1
  23.8 0.0 copy-done.4
  23.9 0.7 fusion.7
  24.5 16.4 %all-reduce.1 = (f32[2,64]{1,0:T(2,128)S(1)}, f32[10,64]{1,0:T(8,128)S(1)}) all-reduce(f32[2,64]{1,0:T(2,128)S(1)} %fusion.7, f32[10,64]{1,0:T(8,128)S(1)} %get-tuple-element.14), channel_id=1, replica_groups=mesh['batch'=16,'proto'=8] {'proto'}, use_global_device_ids=true, to_apply=%region_7.0 | all-reduce | flops 768 | bytes 6144 | tf_op jit(solution)/shard_map/pmax | solution.py:27
  40.9 1.7 convert_reduce_fusion
  42.6 9.3 %fusion.3 = f32[10,64]{1,0:T(8,128)S(1)} fusion(f32[10,64,8192]{2,1,0:T(8,128)} %get-tuple-element.15, f32[10,64]{1,0:T(8,128)S(1)} %get-tuple-element.8), kind=kLoop, calls=%fused_computation.6 | loop fusion | flops 15728000 | bytes 20976640 | tf_op jit(solution)/shard_map/reduce_sum | solution.py:31
  52.0 13.1 %all-reduce = (f32[2,64]{1,0:T(2,128)S(1)}, f32[10,64]{1,0:T(8,128)S(1)}) all-reduce(f32[2,64]{1,0:T(2,128)S(1)} %get-tuple-element.4, f32[10,64]{1,0:T(8,128)S(1)} %fusion.3), channel_id=1, replica_groups=mesh['batch'=16,'proto'=8] {'proto'}, use_global_device_ids=true, to_apply=%region_9.0 | all-reduce | flops 768 | bytes 6144 | tf_op jit(solution)/shard_map/psum | solution.py:30
  65.0 1.0 fusion.9
  66.0 0.6 fusion.28
  66.7 0.0 copy-start.5
  66.7 7.9 %broadcast_in_dim.25 = f32[8,64,8192]{2,1,0:T(8,128)} broadcast(f32[64,8192]{1,0:T(8,128)S(1)} %get-tuple-element.12), dimensions={1,2} | broadcast | bytes 18874368 | tf_op jit(solution)/shard_map/broadcast_in_dim | solution.py:37
  74.6 0.0 copy-done.5
  74.6 0.0 copy-start.2
  74.6 14.2 %fusion.2 = bf16[10,64,8192]{2,1,0:T(8,128)(2,1)S(1)} fusion(f32[8,64,8192]{2,1,0:T(8,128)} %broadcast_in_dim.25, f32[1,64,8192]{2,1,0:T(8,128)S(1)} %get-tuple-element.13, f32[1,64,8192]{2,1,0:T(8,128)S(1)} %get-tuple-element.11, f32[10,64,8192]{2,1,0:T(8,128)} %get-tuple-element.15, f32[10,64]{1,0:T(8,128)S(1)} %get-tuple-element.6, ...), kind=kLoop, calls=%fused_computation.3 | loop fusion | flops 47185920 | bytes 52433960 | tf_op jit(solution)/shard_map/convert_element_type | solution.py:44
  88.8 0.0 copy-start
  88.8 4.0 %copy-done = bf16[10,64,8192]{2,1,0:T(8,128)(2,1)} copy-done((bf16[10,64,8192]{2,1,0:T(8,128)(2,1)}, bf16[10,64,8192]{2,1,0:T(8,128)(2,1)S(1)}, u32[]{:S(2)}) %copy-start) | copy-done | bytes 10485784
  92.8 0.0 copy-done.2
  92.8 0.0 copy-start.3
  92.8 3.7 %fusion.11 = f32[10,64,256]{2,1,0:T(8,128)} fusion(bf16[10,64,8192]{2,1,0:T(8,128)(2,1)S(1)} %fusion.2, bf16[256,8192]{1,0:T(8,128)(2,1)S(1)} %copy-done.2, f32[8192]{0:T(1024)S(1)} %add_sqrt_fusion), kind=kOutput, calls=%fused_computation.20 | convolution fusion | flops 2690646016 | bytes 15368192 | tf_op jit(solution)/shard_map/cbp,dp->cbd/dot_general | solution.py:45
  96.5 0.0 all-reduce.5.cloned.1.call-update
  96.5 0.0 all-reduce.7.cloned.1.call-start
  96.6 0.0 copy-done.3
  96.6 9.9 %convolution_bitcast_fusion = f32[256,8192]{1,0:T(8,128)} fusion(bf16[10,64,8192]{2,1,0:T(8,128)(2,1)} %copy-done, bf16[10,64,256]{2,1,0:T(8,128)(2,1)S(1)} %copy-done.3, f32[10,64]{1,0:T(8,128)S(1)} %add_rsqrt_fusion), kind=kOutput, calls=%fused_computation.7 | convolution fusion | flops 2684846080 | bytes 19204608 | tf_op jit(solution)/shard_map/cbd,cbp->dp/dot_general | solution.py:53
  106.5 0.0 all-reduce.7.cloned.1.call-update
  106.5 75.1 %psum.39 = f32[8192]{0:T(1024)S(1)} all-reduce(f32[8192]{0:T(1024)S(1)} %get-tuple-element.3), channel_id=1, replica_groups=mesh['batch'=16,'proto'=8] {'batch'}, use_global_device_ids=true, to_apply=%region_15.0 | all-reduce | flops 8192 | bytes 65536 | tf_op jit(solution)/shard_map/psum | solution.py:24
  181.6 0.6 multiply_add_fusion
  182.2 0.0 all-reduce.5.cloned.1.call-done
  182.2 5.4 %fusion.19 = f32[10,64,256]{2,1,0:T(8,128)} fusion(f32[10,64,256]{2,1,0:T(8,128)} %all-reduce.5.cloned.1.call-done, bf16[10,64,256]{2,1,0:T(8,128)(2,1)S(1)} %copy-done.3, f32[10,64]{1,0:T(8,128)S(1)} %add_rsqrt_fusion), kind=kOutput, calls=%fused_computation.29 | output fusion | flops 1311615 | bytes 1640960 | tf_op jit(solution)/shard_map/mul | solution.py:48
  187.6 113.6 %all-reduce.7.cloned.1.call-done = f32[256,8192]{1,0:T(8,128)} async-done(((f32[256,8192]{1,0:T(8,128)}), f32[256,8192]{1,0:T(8,128)}) %all-reduce.7.cloned.1.call-update) | async-done | bytes 8388624 | tf_op jit(solution)/shard_map/psum | solution.py:54
  301.2 5.6 %multiply_reduce_fusion.1 = (f32[8192]{0:T(1024)S(1)}, f32[256,8192]{1,0:T(8,128)S(1)}) fusion(f32[256,8192]{1,0:T(8,128)} %all-reduce.7.cloned.1.call-done, f32[8192]{0:T(1024)S(1)} %add_sqrt_fusion, bf16[256,8192]{1,0:T(8,128)(2,1)} %param.6), kind=kLoop, calls=%fused_computation.11 | loop fusion | flops 8380416 | bytes 21037056 | tf_op jit(solution)/shard_map/reduce_sum | solution.py:55
  306.8 1.9 subtract_divide_fusion
  (2 shorter events, 0.0 us)
Async XLA Ops:
  7.2 175.0 %all-reduce.5.cloned.1.call-start = ((), (), s32[]{:S(2)}) async-start(), calls=%async_computation | async-start | bytes 1310720 | tf_op jit(solution)/shard_map/psum | solution.py:46
  11.4 12.4 %copy-start.1 = (bf16[2,64,8192]{2,1,0:T(8,128)(2,1)S(1)}, bf16[2,64,8192]{2,1,0:T(8,128)(2,1)}, u32[]{:S(2)}) copy-start(bf16[2,64,8192]{2,1,0:T(8,128)(2,1)} %param.5) | copy-start | bytes 6291460
  11.5 12.4 %copy-start.4 = (f32[8192]{0:T(1024)S(1)}, f32[8192]{0:T(1024)}, u32[]{:S(2)}) copy-start(f32[8192]{0:T(1024)} %param.7) | copy-start | bytes 98308
  66.7 7.9 %copy-start.5 = (f32[10]{0:T(128)S(1)}, f32[10]{0:T(128)}, u32[]{:S(2)}) copy-start(f32[10]{0:T(128)} %constant.14.clone.1) | copy-start | bytes 124
  74.6 18.2 %copy-start.2 = (bf16[256,8192]{1,0:T(8,128)(2,1)S(1)}, bf16[256,8192]{1,0:T(8,128)(2,1)}, u32[]{:S(2)}) copy-start(bf16[256,8192]{1,0:T(8,128)(2,1)} %param.6) | copy-start | bytes 12582916
  88.8 4.0 %copy-start = (bf16[10,64,8192]{2,1,0:T(8,128)(2,1)}, bf16[10,64,8192]{2,1,0:T(8,128)(2,1)S(1)}, u32[]{:S(2)}) copy-start(bf16[10,64,8192]{2,1,0:T(8,128)(2,1)S(1)} %fusion.2) | copy-start | bytes 31457284
  92.8 3.8 %copy-start.3 = (bf16[10,64,256]{2,1,0:T(8,128)(2,1)S(1)}, bf16[10,64,256]{2,1,0:T(8,128)(2,1)}, u32[]{:S(2)}) copy-start(bf16[10,64,256]{2,1,0:T(8,128)(2,1)} %param.4) | copy-start | bytes 983044
  96.5 204.6 %all-reduce.7.cloned.1.call-start = ((), (), s32[]{:S(2)}) async-start(), calls=%async_computation.1 | async-start | bytes 16777216 | tf_op jit(solution)/shard_map/psum | solution.py:54
Sparse Core Ops, SparseCore 0:
  96.7 60.6 all-reduce.4
  160.9 140.2 all-reduce.6
where the time goes:
time: 316 us
  waiting for transfers between devices  114 us (36%)
  blocking collectives  105 us (33%)
  other arithmetic  45.3 us (14%)
  matrix products  26 us (8%)
  between operations  14.2 us (4%)
  local copies, waits for them, and re-layouts  11.9 us (4%)
    psum x1, waiting for transfers between devices, on_device(): grad_all = lax.psum(full_local, 'batch')  114 us
    psum x1, blocking collectives, on_device(): col_sums = lax.psum(col_local, 'batch')  75.1 us
    pmax x1, blocking collectives, on_device(): s_top, t_top = lax.pmax((s_loc, t_loc), 'proto')  16.4 us
    convert_element_type x1, other arithmetic, on_device(): ((counts[:, None, None] * student - target) * scale).astype(jnp.bfloat16)  14.2 us
    psum x1, blocking collectives, on_device(): lax.psum((jnp.sum(s_exp, axis=-1, keepdims=True), jnp.sum(t_exp, axis=-1,...  13.1 us
    dot_general x1, matrix products, on_device(): jnp.einsum('cbd,dp->cbp', unit_b, weight_b, preferred_element_type=jnp.fl...  12.4 us
    dot_general x1, matrix products, on_device(): jnp.einsum('cbd,cbp->dp', unit_b, grad_b, preferred_element_type=jnp.floa...  9.87 us
    reduce_sum x1, other arithmetic, on_device(): jnp.sum(s_exp, axis=-1, keepdims=True)  9.33 us
  transfers between devices with their start and end apart: 2, of which 1 were waited for; matrix products, arithmetic and copies ran while one was open for 5% of the time, Pallas kernels for 0%

commit v1 on v0

v1 whole, which is shorter than its diff:
```python
import functools
import math

import jax
import jax.numpy as jnp
from jax import lax
from jax.experimental import pallas as pl
from jax.experimental.pallas import tpu as pltpu
from jax.sharding import PartitionSpec as P

F32 = jnp.float32
BF16 = jnp.bfloat16
LOG2E = math.log2(math.e)
STUDENT_C = 10.0 * LOG2E
TEACHER_C = 25.0 * LOG2E
EPS = 1e-06
VMEM = 56 * 1024 * 1024
CHUNKS = 2
STAT_TILE = 1024
TILE = 256


def stats_kernel(
    f_ref, dir_ref, t_ref, c_ref, ub_ref, inv_ref, colsum_ref, stat_ref, sacc, macc, tacc
):
    step = pl.program_id(0)
    rows = f_ref.shape[0]

    @pl.when(step == 0)
    def _():
        zf = f_ref[...].astype(F32)
        inv = 1.0 / jnp.sqrt(jnp.sum(zf * zf, axis=-1, keepdims=True) + EPS)
        ub_ref[...] = (zf * inv).astype(BF16)
        sacc[...] = jnp.zeros_like(sacc)
        macc[...] = jnp.full_like(macc, -1e30)
        tacc[...] = jnp.zeros_like(tacc)

    d = dir_ref[...].astype(F32)
    inv_col = 1.0 / jnp.sqrt(jnp.sum(d * d, axis=0, keepdims=True) + EPS)
    inv_ref[...] = inv_col
    wb = (d * inv_col).astype(BF16)
    width = d.shape[1]
    ub = ub_ref[...]
    for k in range(width // TILE):
        s = jnp.dot(ub, wb[:, k * TILE : (k + 1) * TILE], preferred_element_type=F32)
        e = jnp.exp2(s * STUDENT_C)
        part = e[:, :128]
        for m in range(1, TILE // 128):
            part += e[:, m * 128 : (m + 1) * 128]
        sacc[...] += part
    t = t_ref[...].astype(F32)
    colsum_ref[...] = jnp.sum(t, axis=0, keepdims=True)
    diff = t - c_ref[...]
    lanes = [diff[:, m * 128 : (m + 1) * 128] for m in range(width // 128)]
    old = macc[...]
    top = functools.reduce(jnp.maximum, lanes, old)
    total = tacc[...] * jnp.exp2((old - top) * TEACHER_C)
    for lane in lanes:
        total += jnp.exp2((lane - top) * TEACHER_C)
    macc[...] = top
    tacc[...] = total

    @pl.when(step == pl.num_programs(0) - 1)
    def _():
        stat_ref[...] = jnp.zeros_like(stat_ref)
        for r in range(rows // 128):
            stat_ref[r : r + 1, :] = jnp.sum(
                sacc[r * 128 : (r + 1) * 128, :].T, axis=0, keepdims=True
            )
        tops = macc[...].T
        best = jnp.max(tops, axis=0, keepdims=True)
        stat_ref[5:6, :] = best
        stat_ref[6:7, :] = jnp.sum(
            tacc[...].T * jnp.exp2((tops - best) * TEACHER_C), axis=0, keepdims=True
        )


def grad_kernel(images, place, stat_ref, f_ref, ub_ref, *refs):
    first = place[3] == 0
    del first
    (dirs, invs, teach, cents) = (refs[0:4], refs[4:8], refs[8:12], refs[12:16])
    (before_ref, xp, xm, xk, yp, ym, yk, after_ref, keep_ref, send_ref) = refs[16:26]
    (utx, uty, tflat, arow, brow, mrow, acc, gbuf, wbuf) = refs[26:35]
    step = pl.program_id(0)
    x, y, core = place[0], place[1], place[2]
    rows = ub_ref.shape[0]
    img = rows // 10
    scale = 1.0 / (0.1 * 18.0 * images)

    def block_of(xr, yr):
        return pl.multiple_of(lax.rem(x + xr, 4) * 64 + lax.rem(y + yr, 4) * 16, 16)

    @pl.when(step == 0)
    def _():
        tflat[...] = ub_ref[...].T
        for a in range(4):
            for b in range(4):
                at = (a * 4 + b) * 16
                utx[at : at + 16, :] = tflat[pl.ds(block_of(a, b), 16), :]
                uty[at : at + 16, :] = tflat[pl.ds(block_of(b, a), 16), :]
        stat = stat_ref[...]
        sums = jnp.sum(stat, axis=0)
        top = jnp.max(stat[:, 5:6, :], axis=0)
        ttot = jnp.sum(stat[:, 6:7, :] * jnp.exp2((stat[:, 5:6, :] - top) * TEACHER_C), axis=0)
        packed = jnp.concatenate([sums[0:5], top, ttot, jnp.zeros((121, 128), F32)], axis=0).T
        for r in range(5):
            arow[r * 128 : (r + 1) * 128, :] = jnp.broadcast_to(
                scale / packed[:, r : r + 1], (128, 128)
            )
        arow[2 * img :, :] = 2.0 * arow[2 * img :, :]
        mrow[...] = jnp.broadcast_to(packed[:, 5:6], (128, 128))
        brow[...] = jnp.broadcast_to(scale / packed[:, 6:7], (128, 128))
        acc[...] = before_ref[...]

    ub = ub_ref[...]
    for q in range(4):
        cols = slice(q * TILE, (q + 1) * TILE)
        inv = invs[q][...]
        wb = (dirs[q][...].astype(F32) * inv).astype(BF16)
        wbuf[:, cols] = wb
        s = jnp.dot(ub, wb, preferred_element_type=F32)
        for m in range(TILE // 128):
            lane = slice(m * 128, (m + 1) * 128)
            diff = teach[q][:, lane].astype(F32) - cents[q][:, lane]
            t = jnp.exp2((diff - mrow[...]) * TEACHER_C) * brow[...]
            t0, t1 = t[:img], t[img:]
            both = t0 + t1
            for j in range(10):
                r = slice(j * img, (j + 1) * img)
                target = t1 if j == 0 else t0 if j == 1 else both
                g = jnp.exp2(s[r, lane] * STUDENT_C) * arow[r, :] - target
                gbuf[r, q * TILE + m * 128 : q * TILE + (m + 1) * 128] = g.astype(BF16)
        ut = utx if q < 2 else uty
        gw = jnp.dot(ut[...], gbuf[:, cols], preferred_element_type=F32)
        weights = []
        dots = jnp.zeros((1, TILE), F32)
        for a in range(4):
            for b in range(4):
                at = (a * 4 + b) * 16
                start = block_of(a, b) if q < 2 else block_of(b, a)
                w = dirs[q][pl.ds(start, 16), :].astype(F32) * inv
                weights.append(w)
                dots += jnp.sum(gw[at : at + 16] * w, axis=0, keepdims=True)
        plus, minus, kept = (xp, xm, xk) if q < 2 else (yp, ym, yk)
        even = q % 2 == 0
        where = (
            [(kept, 128), (kept, 0), (plus, 0), (minus, 64)]
            if even
            else [(kept, 192), (plus, 64), (minus, 0), (kept, 64)]
        )
        for a in range(4):
            ref, base = where[a]
            for b in range(4):
                at = (a * 4 + b) * 16
                ref[base + b * 16 : base + (b + 1) * 16, :] = (
                    gw[at : at + 16] - weights[a * 4 + b] * dots
                ) * inv
    acc[...] += lax.dot_general(
        gbuf[...], wbuf[...], (((1,), (1,)), ((), ())), preferred_element_type=F32
    )

    @pl.when(step == pl.num_programs(0) - 1)
    def _():
        g = acc[...]
        after_ref[...] = g
        zf = f_ref[...].astype(F32)
        inv = 1.0 / jnp.sqrt(jnp.sum(zf * zf, axis=-1, keepdims=True) + EPS)
        unit = zf * inv
        acc[...] = (g - unit * jnp.sum(g * unit, axis=-1, keepdims=True)) * inv
        half = rows // 2
        keep_ref[...] = acc[pl.ds(pl.multiple_of(core * half, 8), half), :]
        send_ref[...] = acc[pl.ds(pl.multiple_of((1 - core) * half, 8), half), :]


def stats_call(f, dirs, teach, center):
    rows, dim = f.shape
    protos = dirs.shape[1]
    trows = teach.shape[0]
    whole = lambda i: (0, 0)
    tile = lambda i: (0, i)
    return pl.pallas_call(
        stats_kernel,
        grid=(protos // STAT_TILE,),
        in_specs=[
            pl.BlockSpec((rows, dim), whole),
            pl.BlockSpec((dim, STAT_TILE), tile),
            pl.BlockSpec((trows, STAT_TILE), tile),
            pl.BlockSpec((1, STAT_TILE), tile),
        ],
        out_specs=[
            pl.BlockSpec((rows, dim), whole),
            pl.BlockSpec((1, STAT_TILE), tile),
            pl.BlockSpec((1, STAT_TILE), tile),
            pl.BlockSpec((8, 128), whole),
        ],
        out_shape=[
            jax.ShapeDtypeStruct((rows, dim), BF16),
            jax.ShapeDtypeStruct((1, protos), F32),
            jax.ShapeDtypeStruct((1, protos), F32),
            jax.ShapeDtypeStruct((8, 128), F32),
        ],
        scratch_shapes=[
            pltpu.VMEM((rows, 128), F32),
            pltpu.VMEM((trows, 128), F32),
            pltpu.VMEM((trows, 128), F32),
        ],
        compiler_params=pltpu.CompilerParams(
            dimension_semantics=("arbitrary",), vmem_limit_bytes=VMEM
        ),
        cost_estimate=pl.CostEstimate(
            flops=2 * rows * dim * protos,
            bytes_accessed=2 * (dim + trows) * protos,
            transcendentals=(rows + trows) * protos,
        ),
        name="stats",
    )(f, dirs, teach, center)


def grad_call(images, chunk, place, stat, f, ub, dirs, inv, teach, center, before):
    rows, dim = f.shape
    protos = dirs.shape[1]
    trows = teach.shape[0]
    quarter = protos // 4
    part = quarter // CHUNKS
    steps = part // TILE
    whole = lambda i, p: (0, 0)
    tile = lambda i, p: (0, i)

    def at(q):
        base = (q * quarter + chunk * part) // TILE
        return lambda i, p: (0, base + i)

    spread = lambda height: [pl.BlockSpec((height, TILE), at(q)) for q in range(4)]
    half = rows // 2
    out = lambda height: jax.ShapeDtypeStruct((height, part), F32)
    return pl.pallas_call(
        functools.partial(grad_kernel, images),
        grid_spec=pltpu.PrefetchScalarGridSpec(
            num_scalar_prefetch=1,
            grid=(steps,),
            in_specs=[
                pl.BlockSpec((8, 8, 128), lambda i, p: (0, 0, 0)),
                pl.BlockSpec((rows, dim), whole),
                pl.BlockSpec((rows, dim), whole),
            ]
            + spread(dim)
            + spread(1)
            + spread(trows)
            + spread(1)
            + [pl.BlockSpec((rows, dim), whole)],
            out_specs=[
                pl.BlockSpec((128, TILE), tile),
                pl.BlockSpec((128, TILE), tile),
                pl.BlockSpec((256, TILE), tile),
                pl.BlockSpec((128, TILE), tile),
                pl.BlockSpec((128, TILE), tile),
                pl.BlockSpec((256, TILE), tile),
                pl.BlockSpec((rows, dim), whole),
                pl.BlockSpec((half, dim), whole),
                pl.BlockSpec((half, dim), whole),
            ],
            scratch_shapes=[
                pltpu.VMEM((dim, rows), BF16),
                pltpu.VMEM((dim, rows), BF16),
                pltpu.VMEM((dim, rows), BF16),
                pltpu.VMEM((rows, 128), F32),
                pltpu.VMEM((trows, 128), F32),
                pltpu.VMEM((trows, 128), F32),
                pltpu.VMEM((rows, dim), F32),
                pltpu.VMEM((rows, 4 * TILE), BF16),
                pltpu.VMEM((dim, 4 * TILE), BF16),
            ],
        ),
        out_shape=[out(128), out(128), out(256), out(128), out(128), out(256)]
        + [
            jax.ShapeDtypeStruct((rows, dim), F32),
            jax.ShapeDtypeStruct((half, dim), F32),
            jax.ShapeDtypeStruct((half, dim), F32),
        ],
        compiler_params=pltpu.CompilerParams(
            dimension_semantics=("arbitrary",), vmem_limit_bytes=VMEM
        ),
        cost_estimate=pl.CostEstimate(
            flops=6 * rows * dim * protos // CHUNKS,
            bytes_accessed=(2 * (dim + trows) + 4 * dim) * protos // CHUNKS,
            transcendentals=(rows + trows) * protos // CHUNKS,
        ),
        name="grads",
    )(place, stat, f, ub, *([dirs] * 4), *([inv] * 4), *([teach] * 4), *([center] * 4), before)


def shift_x(d):
    return [(x * 4 + y, ((x + d) % 4) * 4 + y) for x in range(4) for y in range(4)]


def shift_y(d):
    return [(x * 4 + y, x * 4 + (y + d) % 4) for x in range(4) for y in range(4)]


def ring(plus, minus, kept, shift):
    n = plus.shape[0] // 2
    up = lax.ppermute(plus, "batch", shift(1))
    down = lax.ppermute(minus, "batch", shift(-1))
    up2 = lax.ppermute(up[:n] + kept[:n], "batch", shift(1))
    down2 = lax.ppermute(down[:n] + kept[n : 2 * n], "batch", shift(-1))
    first = kept[2 * n : 3 * n] + down[n:] + up2
    second = kept[3 * n :] + up[n:] + down2
    return first, second


def second_ring(first, second, shift):
    n = first.shape[0] // 4
    f = [first[n * k : n * (k + 1)] for k in range(4)]
    s = [second[n * k : n * (k + 1)] for k in range(4)]
    plus = jnp.concatenate([f[2], s[1]], axis=0)
    minus = jnp.concatenate([s[2], f[3]], axis=0)
    kept = jnp.concatenate([f[1], s[3], f[0], s[0]], axis=0)
    return ring(plus, minus, kept, shift)


def on_device(features, teacher_logits, directions, center):
    crops, img, dim = features.shape
    images = img * lax.axis_size("batch")
    protos = directions.shape[1]
    rows = crops * img
    f = features.reshape(rows, dim)
    teach = teacher_logits.reshape(-1, protos)
    cent = center.reshape(1, protos)
    b, p = lax.axis_index("batch"), lax.axis_index("proto")
    place = jnp.stack([b // 4, b % 4, p % 2, 0]).astype(jnp.int32)
    ub, inv, colsum, stat = stats_call(f, directions, teach, cent)
    col_sums = lax.psum(colsum.reshape(protos), "batch")
    new_center = 0.9 * center + 0.1 * col_sums / (2.0 * images)
    stats = lax.all_to_all(jnp.broadcast_to(stat, (8, 8, 128)), "proto", 0, 0)
    before = jnp.zeros((rows, dim), F32)
    pieces = [[] for _ in range(4)]
    for chunk in range(CHUNKS):
        xp, xm, xk, yp, ym, yk, before, keep, send = grad_call(
            images, chunk, place, stats, f, ub, directions, inv, teach, cent, before
        )
        out_x = second_ring(*ring(xp, xm, xk, shift_x), shift_y)
        out_y = second_ring(*ring(yp, ym, yk, shift_y), shift_x)
        for q, piece in enumerate(out_x + out_y):
            pieces[q].append(piece)
    grad_directions = jnp.concatenate([part for row in pieces for part in row], axis=1)
    total = keep + lax.ppermute(send, "proto", [(i, i ^ 1) for i in range(8)])
    total = total + lax.ppermute(total, "proto", [(i, i ^ 2) for i in range(8)])
    total = total + lax.ppermute(total, "proto", [(i, 6 - 2 * (i // 2) + i % 2) for i in range(8)])
    other = lax.ppermute(total, "proto", [(i, i ^ 1) for i in range(8)])
    even = p % 2 == 0
    grad_features = jnp.concatenate(
        [jnp.where(even, total, other), jnp.where(even, other, total)], axis=0
    ).reshape(crops, img, dim)
    return (grad_features, grad_directions, new_center)


def solution(mesh):
    in_specs = (P(None, "batch", None), P(None, "batch", "proto"), P(None, "proto"), P("proto"))
    out_specs = (P(None, "batch", None), P("batch", "proto"), P("proto"))
    return jax.shard_map(
        on_device, mesh=mesh, in_specs=in_specs, out_specs=out_specs, check_vma=False
    )
```

time: 316 us -> 215 us (0.68)
  waiting for transfers between devices: 114 us -> 52.3 us
  starting transfers between devices: 0.08 us -> 42.6 us
  other arithmetic: 45.3 us -> 8.01 us
  Pallas kernels: 0 us -> 33 us
  blocking collectives: 105 us -> 74.5 us
  matrix products: 26 us -> 0 us
  between operations: 14.2 us -> 1.15 us
  local copies, waits for them, and re-layouts: 11.9 us -> 3.07 us
    psum x2 -> x0, waiting for transfers between devices: 114 us -> none  [the longest x1 114 us: on_device(): grad_all = lax.psum(full_local, 'batch')]
    ppermute x0 -> x36, waiting for transfers between devices: none -> 47.5 us  [the longest x8 19.5 us: ring(): up = lax.ppermute(plus, 'batch', shift(1))]
    ppermute x0 -> x36, starting transfers between devices: none -> 37.2 us  [the longest x8 15.3 us: ring(): down2 = lax.ppermute(down[:n] + kept[n:2 * n], 'batch', shift(-1))]
    pallas_call x0 -> x3, Pallas kernels: none -> 33 us  [the longest x2 22.9 us: grad_call(): pl.pallas_call(functools.partial(grad_kernel, images), grid_spec=pltpu.Pr...]
    dot_general x3 -> x0, matrix products: 26 us -> none  [the longest x1 12.4 us: on_device(): jnp.einsum('cbd,dp->cbp', unit_b, weight_b, preferred_element_type=jnp.fl...]
    reduce_sum x5 -> x0, other arithmetic: 20.8 us -> none  [the longest x1 9.33 us: on_device(): jnp.sum(s_exp, axis=-1, keepdims=True)]
    pmax x1 -> x0, blocking collectives: 16.4 us -> none  [on_device(): s_top, t_top = lax.pmax((s_loc, t_loc), 'proto')]
    convert_element_type x1 -> x0, other arithmetic: 14.2 us -> none  [on_device(): ((counts[:, None, None] * student - target) * scale).astype(jnp.bfloat16)]
  transfers between devices with their start and end apart: 2 -> 37, of which waited for: 1 -> 16; matrix products, arithmetic and copies ran while one was open for 5% -> 4% of each run, Pallas kernels for 0% -> 5%
where the time goes in v1:
time: 215 us
  blocking collectives  74.5 us (35%)
  waiting for transfers between devices  52.3 us (24%)
  starting transfers between devices  42.6 us (20%)
  Pallas kernels  33 us (15%)
  other arithmetic  8.01 us (4%)
  local copies, waits for them, and re-layouts  3.07 us (1%)
    psum x1, blocking collectives, on_device(): col_sums = lax.psum(colsum.reshape(protos), 'batch')  74.5 us
    pallas_call x2, Pallas kernels, grad_call(): pl.pallas_call(functools.partial(grad_kernel, images), grid_spec=pltpu.Pr...  22.9 us
    ppermute x8, waiting for transfers between devices, ring(): up = lax.ppermute(plus, 'batch', shift(1))  19.5 us
    ppermute x8, waiting for transfers between devices, ring(): up2 = lax.ppermute(up[:n] + kept[:n], 'batch', shift(1))  16.4 us
    ppermute x8, starting transfers between devices, ring(): down2 = lax.ppermute(down[:n] + kept[n:2 * n], 'batch', shift(-1))  15.3 us
    ppermute x8, starting transfers between devices, ring(): down = lax.ppermute(minus, 'batch', shift(-1))  14.1 us
    pallas_call x1, Pallas kernels, stats_call(): pl.pallas_call(stats_kernel, grid=(protos // STAT_TILE,), in_specs=[pl.Bl...  10.1 us
    ppermute x8, waiting for transfers between devices, ring(): down = lax.ppermute(minus, 'batch', shift(-1))  7.09 us
  transfers between devices with their start and end apart: 37, of which 16 were waited for; matrix products, arithmetic and copies ran while one was open for 4% of the time, Pallas kernels for 5%

profile of v1, /device:TPU:0, one launch (start us, length us, event | category | flops | bytes accessed | tf_op | source)
XLA Modules:
  0.0 214.6 jit_solution(16211666237746576020)
XLA Ops:
  0.6 10.1 %stats.1 = (bf16[640,256]{1,0:T(8,128)(2,1)}, f32[1,8192]{1,0:T(1,128)}, f32[1,8192]{1,0:T(1,128)}, f32[8,128]{1,0:T(8,128)}) custom-call(bf16[640,256]{1,0:T(8,128)(2,1)} %bitcast.26, bf16[256,8192]{1,0:T(8,128)(2,1)} %refs_3_.3, bf16[128,8192]{1,0:T(8,128)(2,1)} %bitcast.8, f32[1,8192]{1,0:T(1,128)} %bitcast.17), custom_call_target="tpu_custom_call" | custom-call | flops 2684354560 | bytes 6291456 | tf_op jit(solution)/shard_map/stats/pallas_call | solution.py:181
  10.7 1.3 broadcast_in_dim.6
  12.0 5.4 %all-to-all-start = ((f32[8,8,128]{2,1,0:T(8,128)}), f32[8,8,128]{2,1,0:T(8,128)S(1)}, u32[]{:S(2)}, u32[]{:S(2)}) async-start(f32[8,8,128]{2,1,0:T(8,128)} %broadcast_in_dim.6), calls=%async_computation | async-start | bytes 65536 | tf_op jit(solution)/shard_map/all_to_all | solution.py:334
  17.4 0.6 pad_add_fusion.place
  18.0 4.9 %all-to-all-done.stat_ref = f32[8,8,128]{2,1,0:T(8,128)S(1)} async-done(((f32[8,8,128]{2,1,0:T(8,128)}), f32[8,8,128]{2,1,0:T(8,128)S(1)}, u32[]{:S(2)}, u32[]{:S(2)}) %all-to-all-start) | async-done | bytes 32800 | tf_op jit(solution)/shard_map/all_to_all | solution.py:334
  22.9 0.9 broadcast_in_dim.7.refs_16_
  23.8 11.3 %grads.2 = (f32[128,1024]{1,0:T(8,128)}, f32[128,1024]{1,0:T(8,128)}, f32[256,1024]{1,0:T(8,128)}, f32[128,1024]{1,0:T(8,128)}, f32[128,1024]{1,0:T(8,128)}, /*i...) custom-call(s32[4]{0:T(128)} %pad_add_fusion.place, f32[8,8,128]{2,1,0:T(8,128)} %copy-done.5, ...), custom_call_target="tpu_custom_call" | custom-call | flops 4026531840 | bytes 7340032 | tf_op jit(solution)/shard_map/grads/pallas_call | solution.py:236
  35.1 2.8 %collective-permute-start.4 = (f32[128,1024]{1,0:T(8,128)}, f32[128,1024]{1,0:T(8,128)S(1)}, u32[]{:S(2)}, u32[]{:S(2)}) collective-permute-start(f32[128,1024]{1,0:T(8,128)} %get-tuple-element.29), channel_id=1, source_target_pairs={{0,96},{8,104},{16,112},{24,120},{32,0},{40,8},{48,16},{56,24},{64... | collective-permute-start | bytes 1572872 | tf_op jit(solution)/shard_map/ppermute | solution.py:303
  37.9 11.5 %grads.3 = (f32[128,1024]{1,0:T(8,128)}, f32[128,1024]{1,0:T(8,128)}, f32[256,1024]{1,0:T(8,128)}, f32[128,1024]{1,0:T(8,128)}, f32[128,1024]{1,0:T(8,128)}, /*i...) custom-call(s32[4]{0:T(128)} %pad_add_fusion.place, f32[8,8,128]{2,1,0:T(8,128)} %copy-done.5, ...), custom_call_target="tpu_custom_call" | custom-call | flops 4026531840 | bytes 7340032 | tf_op jit(solution)/shard_map/grads/pallas_call | solution.py:236
  49.5 0.1 collective-permute-start
  49.6 3.1 %collective-permute-start.20 = (f32[128,1024]{1,0:T(8,128)}, f32[128,1024]{1,0:T(8,128)}, u32[]{:S(2)}, u32[]{:S(2)}) collective-permute-start(f32[128,1024]{1,0:T(8,128)} %get-tuple-element.35), channel_id=1, source_target_pairs={{0,24},{8,0},{16,8},{24,16},{32,56},{40,32},{48,40},{56,48},{64,88... | collective-permute-start | bytes 1572872 | tf_op jit(solution)/shard_map/ppermute | solution.py:303
  52.7 74.5 %psum.7 = f32[8192]{0:T(1024)S(1)} all-reduce(f32[8192]{0:T(1024)S(1)} %bitcast.30), channel_id=1, replica_groups=mesh['batch'=16,'proto'=8] {'batch'}, use_global_device_ids=true, to_apply=%region_0.1 | all-reduce | flops 8192 | bytes 65536 | tf_op jit(solution)/shard_map/psum | solution.py:332
  127.2 0.6 multiply_add_fusion
  127.8 2.0 collective-permute-start.5
  129.8 1.0 add.169
  130.9 3.3 %collective-permute-start.27 = (f32[128,1024]{1,0:T(8,128)}, f32[128,1024]{1,0:T(8,128)S(1)}, u32[]{:S(2)}, u32[]{:S(2)}) collective-permute-start(f32[128,1024]{1,0:T(8,128)} %get-tuple-element.38), channel_id=1, source_target_pairs={{0,24},{8,0},{16,8},{24,16},{32,56},{40,32},{48,40},{56,48},{64,88... | collective-permute-start | bytes 1572872 | tf_op jit(solution)/shard_map/ppermute | solution.py:303
  134.2 0.6 collective-permute-start.1
  134.9 1.0 slice_add_fusion.4
  135.8 3.5 %collective-permute-done.11 = f32[128,1024]{1,0:T(8,128)S(1)} collective-permute-done((f32[128,1024]{1,0:T(8,128)}, f32[128,1024]{1,0:T(8,128)S(1)}, u32[]{:S(2)}, u32[]{:S(2)}) %collective-permute-start.11) | collective-permute-done | bytes 524320 | tf_op jit(solution)/shard_map/ppermute | solution.py:303
  139.4 1.1 slice_add_fusion.8
  140.4 3.5 %collective-permute-done.27 = f32[128,1024]{1,0:T(8,128)S(1)} collective-permute-done((f32[128,1024]{1,0:T(8,128)}, f32[128,1024]{1,0:T(8,128)S(1)}, u32[]{:S(2)}, u32[]{:S(2)}) %collective-permute-start.27) | collective-permute-done | bytes 524320 | tf_op jit(solution)/shard_map/ppermute | solution.py:303
  144.0 0.1 collective-permute-start.12
  144.1 3.6 %collective-permute-start.23 = (f32[64,1024]{1,0:T(8,128)S(1)}, f32[64,1024]{1,0:T(8,128)S(1)}, u32[]{:S(2)}, u32[]{:S(2)}) collective-permute-start(f32[64,1024]{1,0:T(8,128)S(1)} %slice_add_fusion.4), channel_id=1, source_target_pairs={{0,24},{8,0},{16,8},{24,16},{32,56},{40,32},{48,40},{56,48},{64,88... | collective-permute-start | bytes 786440 | tf_op jit(solution)/shard_map/ppermute | solution.py:305
  147.7 1.0 slice_add_fusion
  148.7 0.1 collective-permute-start.28
  148.8 3.2 %collective-permute-start.14 = (f32[64,1024]{1,0:T(8,128)S(1)}, f32[64,1024]{1,0:T(8,128)S(1)}, u32[]{:S(2)}, u32[]{:S(2)}) collective-permute-start(f32[64,1024]{1,0:T(8,128)S(1)} %slice_add_fusion.8), channel_id=1, source_target_pairs={{0,96},{8,104},{16,112},{24,120},{32,0},{40,8},{48,16},{56,24},{64... | collective-permute-start | bytes 786440 | tf_op jit(solution)/shard_map/ppermute | solution.py:305
  152.0 0.1 fusion.6
  152.1 3.4 %collective-permute-start.30 = (f32[64,1024]{1,0:T(8,128)S(1)}, f32[64,1024]{1,0:T(8,128)S(1)}, u32[]{:S(2)}, u32[]{:S(2)}) collective-permute-start(f32[64,1024]{1,0:T(8,128)S(1)} %slice_add_fusion), channel_id=1, source_target_pairs={{0,24},{8,0},{16,8},{24,16},{32,56},{40,32},{48,40},{56,48},{64,88... | collective-permute-start | bytes 786440 | tf_op jit(solution)/shard_map/ppermute | solution.py:305
  155.5 1.2 collective-permute-start.2
  156.7 0.1 fusion.2
  156.8 0.6 collective-permute-done.12
  157.4 0.1 fusion.4
  157.5 1.6 collective-permute-done.28
  159.2 0.2 collective-permute-done.30
  159.4 0.1 fusion
  159.5 0.1 collective-permute-start.29
  159.6 4.2 %collective-permute-done.2 = f32[320,256]{1,0:T(8,128)S(1)} collective-permute-done((f32[320,256]{1,0:T(8,128)S(1)}, f32[320,256]{1,0:T(8,128)S(1)}, u32[]{:S(2)}, u32[]{:S(2)}) %collective-permute-start.2) | collective-permute-done | bytes 327712 | tf_op jit(solution)/shard_map/ppermute | solution.py:348
  163.9 0.1 collective-permute-start.3
  163.9 1.0 collective-permute-done.6
  165.1 2.1 %collective-permute-start.8 = (f32[32,1024]{1,0:T(8,128)S(1)}, f32[32,1024]{1,0:T(8,128)S(1)}, u32[]{:S(2)}, u32[]{:S(2)}) collective-permute-start(f32[32,1024]{1,0:T(8,128)S(1)} %pad_maximum_fusion.1), channel_id=1, source_target_pairs={{0,24},{8,0},{16,8},{24,16},{32,56},{40,32},{48,40},{56,48},{64,88... | collective-permute-start | bytes 393224 | tf_op jit(solution)/shard_map/ppermute | solution.py:303
  167.2 1.0 fusion.3
  168.3 1.1 collective-permute-start.24
  169.4 1.0 collective-permute-start.15
  170.4 0.1 fusion.1
  170.5 0.7 collective-permute-start.31
  171.2 3.4 %collective-permute-start.18 = (f32[16,1024]{1,0:T(8,128)S(1)}, f32[16,1024]{1,0:T(8,128)S(1)}, u32[]{:S(2)}, u32[]{:S(2)}) collective-permute-start(f32[16,1024]{1,0:T(8,128)S(1)} %get-tuple-element.61), channel_id=1, source_target_pairs={{0,24},{8,0},{16,8},{24,16},{32,56},{40,32},{48,40},{56,48},{64,88... | collective-permute-start | bytes 196616 | tf_op jit(solution)/shard_map/ppermute | solution.py:305
  174.6 0.1 collective-permute-start.9
  174.7 1.7 collective-permute-start.34
  176.5 0.5 collective-permute-start.25
  177.0 3.9 %collective-permute-done.9 = f32[32,1024]{1,0:T(8,128)S(1)} collective-permute-done((f32[32,1024]{1,0:T(8,128)S(1)}, f32[32,1024]{1,0:T(8,128)S(1)}, u32[]{:S(2)}, u32[]{:S(2)}) %collective-permute-start.9) | collective-permute-done | bytes 131104 | tf_op jit(solution)/shard_map/ppermute | solution.py:302
  180.9 1.8 collective-permute-done.25
  182.7 0.8 collective-permute-start.16
  183.5 5.4 %collective-permute-done.16 = f32[32,1024]{1,0:T(8,128)S(1)} collective-permute-done((f32[32,1024]{1,0:T(8,128)S(1)}, f32[32,1024]{1,0:T(8,128)S(1)}, u32[]{:S(2)}, u32[]{:S(2)}) %collective-permute-start.16) | collective-permute-done | bytes 131104 | tf_op jit(solution)/shard_map/ppermute | solution.py:302
  188.9 6.2 %collective-permute-done.32 = f32[32,1024]{1,0:T(8,128)S(1)} collective-permute-done((f32[32,1024]{1,0:T(8,128)S(1)}, f32[32,1024]{1,0:T(8,128)S(1)}, u32[]{:S(2)}, u32[]{:S(2)}) %collective-permute-start.32) | collective-permute-done | bytes 131104 | tf_op jit(solution)/shard_map/ppermute | solution.py:302
  195.1 0.1 collective-permute-start.10
  195.2 0.9 pad_maximum_fusion
  196.1 4.5 %collective-permute-done.10 = f32[16,1024]{1,0:T(8,128)S(1)} collective-permute-done((f32[16,1024]{1,0:T(8,128)S(1)}, f32[16,1024]{1,0:T(8,128)S(1)}, u32[]{:S(2)}, u32[]{:S(2)}) %collective-permute-start.10) | collective-permute-done | bytes 65568 | tf_op jit(solution)/shard_map/ppermute | solution.py:304
  200.7 5.5 %collective-permute-done.17 = f32[16,1024]{1,0:T(8,128)S(1)} collective-permute-done((f32[16,1024]{1,0:T(8,128)S(1)}, f32[16,1024]{1,0:T(8,128)S(1)}, u32[]{:S(2)}, u32[]{:S(2)}) %collective-permute-start.17) | collective-permute-done | bytes 65568 | tf_op jit(solution)/shard_map/ppermute | solution.py:304
  206.1 2.0 collective-permute-start.26
  208.2 0.1 collective-permute-start.33
  208.3 3.3 %collective-permute-done.26 = f32[16,1024]{1,0:T(8,128)S(1)} collective-permute-done((f32[16,1024]{1,0:T(8,128)S(1)}, f32[16,1024]{1,0:T(8,128)S(1)}, u32[]{:S(2)}, u32[]{:S(2)}) %collective-permute-start.26) | collective-permute-done | bytes 65568 | tf_op jit(solution)/shard_map/ppermute | solution.py:304
  211.6 2.1 collective-permute-done.33
  213.8 0.0 copy-start.7
  213.8 0.8 copy-done.7
  (85 shorter events, 0.7 us)
Async XLA Ops:
  12.0 10.8 %all-to-all-start = ((f32[8,8,128]{2,1,0:T(8,128)}), f32[8,8,128]{2,1,0:T(8,128)S(1)}, u32[]{:S(2)}, u32[]{:S(2)}) async-start(f32[8,8,128]{2,1,0:T(8,128)} %broadcast_in_dim.6), calls=%async_computation | async-start | bytes 65536 | tf_op jit(solution)/shard_map/all_to_all | solution.py:334
  22.9 0.9 copy-start.5
  35.1 95.8 %collective-permute-start.4 = (f32[128,1024]{1,0:T(8,128)}, f32[128,1024]{1,0:T(8,128)S(1)}, u32[]{:S(2)}, u32[]{:S(2)}) collective-permute-start(f32[128,1024]{1,0:T(8,128)} %get-tuple-element.29), channel_id=1, source_target_pairs={{0,96},{8,104},{16,112},{24,120},{32,0},{40,8},{48,16},{56,24},{64... | collective-permute-start | bytes 1572872 | tf_op jit(solution)/shard_map/ppermute | solution.py:303
  37.9 14.7 %copy-start.6 = (f32[1,8192]{1,0:T(1,128)S(1)}, f32[1,8192]{1,0:T(1,128)}, u32[]{:S(2)}) copy-start(f32[1,8192]{1,0:T(1,128)} %get-tuple-element.40) | copy-start | bytes 98308
  37.9 89.2 %copy-start = (f32[8192]{0:T(1024)S(1)}, f32[8192]{0:T(1024)}, u32[]{:S(2)}) copy-start(f32[8192]{0:T(1024)} %param.7) | copy-start | bytes 98308
  37.9 96.2 %copy-start.4 = (f32[256,1024]{1,0:T(8,128)S(1)}, f32[256,1024]{1,0:T(8,128)}, u32[]{:S(2)}) copy-start(f32[256,1024]{1,0:T(8,128)} %get-tuple-element.28) | copy-start | bytes 3145732
  37.9 96.9 %copy-start.3 = (f32[256,1024]{1,0:T(8,128)S(1)}, f32[256,1024]{1,0:T(8,128)}, u32[]{:S(2)}) copy-start(f32[256,1024]{1,0:T(8,128)} %get-tuple-element.34) | copy-start | bytes 3145732
  49.5 80.3 %collective-permute-start = (f32[320,256]{1,0:T(8,128)}, f32[320,256]{1,0:T(8,128)S(1)}, u32[]{:S(2)}, u32[]{:S(2)}) collective-permute-start(f32[320,256]{1,0:T(8,128)} %get-tuple-element.27), channel_id=1, source_target_pairs={{0,1},{1,0},{2,3},{3,2},{4,5},{5,4},{6,7},{7,6},{8,9},{9,8},{10,11... | collective-permute-start | bytes 983048 | tf_op jit(solution)/shard_map/ppermute | solution.py:346
  49.6 84.6 %collective-permute-start.20 = (f32[128,1024]{1,0:T(8,128)}, f32[128,1024]{1,0:T(8,128)}, u32[]{:S(2)}, u32[]{:S(2)}) collective-permute-start(f32[128,1024]{1,0:T(8,128)} %get-tuple-element.35), channel_id=1, source_target_pairs={{0,24},{8,0},{16,8},{24,16},{32,56},{40,32},{48,40},{56,48},{64,88... | collective-permute-start | bytes 1572872 | tf_op jit(solution)/shard_map/ppermute | solution.py:303
  127.2 12.2 %collective-permute-start.11 = (f32[128,1024]{1,0:T(8,128)}, f32[128,1024]{1,0:T(8,128)S(1)}, u32[]{:S(2)}, u32[]{:S(2)}) collective-permute-start(f32[128,1024]{1,0:T(8,128)} %get-tuple-element.32), channel_id=1, source_target_pairs={{0,96},{8,104},{16,112},{24,120},{32,0},{40,8},{48,16},{56,24},{64... | collective-permute-start | bytes 1572872 | tf_op jit(solution)/shard_map/ppermute | solution.py:303
  127.8 20.9 %copy-start.8 = (f32[128,1024]{1,0:T(8,128)S(1)}, f32[128,1024]{1,0:T(8,128)}, u32[]{:S(2)}) copy-start(f32[128,1024]{1,0:T(8,128)} %get-tuple-element.39) | copy-start | bytes 1572868
  127.8 20.9 %collective-permute-start.5 = (f32[128,1024]{1,0:T(8,128)}, f32[128,1024]{1,0:T(8,128)S(1)}, u32[]{:S(2)}, u32[]{:S(2)}) collective-permute-start(f32[128,1024]{1,0:T(8,128)} %get-tuple-element.30), channel_id=1, source_target_pairs={{0,32},{8,40},{16,48},{24,56},{32,64},{40,72},{48,80},{56,88},{64,... | collective-permute-start | bytes 1572872 | tf_op jit(solution)/shard_map/ppermute | solution.py:302
  129.8 22.3 %collective-permute-start.21 = (f32[128,1024]{1,0:T(8,128)}, f32[128,1024]{1,0:T(8,128)S(1)}, u32[]{:S(2)}, u32[]{:S(2)}) collective-permute-start(f32[128,1024]{1,0:T(8,128)} %get-tuple-element.36), channel_id=1, source_target_pairs={{0,8},{8,16},{16,24},{24,0},{32,40},{40,48},{48,56},{56,32},{64,72... | collective-permute-start | bytes 1572872 | tf_op jit(solution)/shard_map/ppermute | solution.py:302
  130.8 26.6 %copy-start.2 = (f32[256,1024]{1,0:T(8,128)S(1)}, f32[256,1024]{1,0:T(8,128)}, u32[]{:S(2)}) copy-start(f32[256,1024]{1,0:T(8,128)} %get-tuple-element.31) | copy-start | bytes 3145732
  130.9 13.1 %collective-permute-start.27 = (f32[128,1024]{1,0:T(8,128)}, f32[128,1024]{1,0:T(8,128)S(1)}, u32[]{:S(2)}, u32[]{:S(2)}) collective-permute-start(f32[128,1024]{1,0:T(8,128)} %get-tuple-element.38), channel_id=1, source_target_pairs={{0,24},{8,0},{16,8},{24,16},{32,56},{40,32},{48,40},{56,48},{64,88... | collective-permute-start | bytes 1572872 | tf_op jit(solution)/shard_map/ppermute | solution.py:303
  134.2 9.9 %collective-permute-start.1 = (f32[320,256]{1,0:T(8,128)S(1)}, f32[320,256]{1,0:T(8,128)S(1)}, u32[]{:S(2)}, u32[]{:S(2)}) collective-permute-start(f32[320,256]{1,0:T(8,128)S(1)} %add.169), channel_id=1, source_target_pairs={{0,2},{1,3},{2,0},{3,1},{4,6},{5,7},{6,4},{7,5},{8,10},{9,11},{10,... | collective-permute-start | bytes 983048 | tf_op jit(solution)/shard_map/ppermute | solution.py:347
  139.4 9.4 %collective-permute-start.7 = (f32[64,1024]{1,0:T(8,128)S(1)}, f32[64,1024]{1,0:T(8,128)S(1)}, u32[]{:S(2)}, u32[]{:S(2)}) collective-permute-start(f32[64,1024]{1,0:T(8,128)S(1)} %slice_add_fusion.12), channel_id=1, source_target_pairs={{0,96},{8,104},{16,112},{24,120},{32,0},{40,8},{48,16},{56,24},{64... | collective-permute-start | bytes 786440 | tf_op jit(solution)/shard_map/ppermute | solution.py:305
  139.4 20.0 %copy-start.1 = (f32[256,1024]{1,0:T(8,128)S(1)}, f32[256,1024]{1,0:T(8,128)}, u32[]{:S(2)}) copy-start(f32[256,1024]{1,0:T(8,128)} %get-tuple-element.37) | copy-start | bytes 3145732
  144.0 13.4 %collective-permute-start.12 = (f32[128,1024]{1,0:T(8,128)}, f32[128,1024]{1,0:T(8,128)S(1)}, u32[]{:S(2)}, u32[]{:S(2)}) collective-permute-start(f32[128,1024]{1,0:T(8,128)} %get-tuple-element.33), channel_id=1, source_target_pairs={{0,32},{8,40},{16,48},{24,56},{32,64},{40,72},{48,80},{56,88},{64,... | collective-permute-start | bytes 1572872 | tf_op jit(solution)/shard_map/ppermute | solution.py:302
  144.1 11.4 %collective-permute-start.23 = (f32[64,1024]{1,0:T(8,128)S(1)}, f32[64,1024]{1,0:T(8,128)S(1)}, u32[]{:S(2)}, u32[]{:S(2)}) collective-permute-start(f32[64,1024]{1,0:T(8,128)S(1)} %slice_add_fusion.4), channel_id=1, source_target_pairs={{0,24},{8,0},{16,8},{24,16},{32,56},{40,32},{48,40},{56,48},{64,88... | collective-permute-start | bytes 786440 | tf_op jit(solution)/shard_map/ppermute | solution.py:305
  148.7 10.5 %collective-permute-start.28 = (f32[128,1024]{1,0:T(8,128)S(1)}, f32[128,1024]{1,0:T(8,128)S(1)}, u32[]{:S(2)}, u32[]{:S(2)}) collective-permute-start(f32[128,1024]{1,0:T(8,128)S(1)} %copy-done.8), channel_id=1, source_target_pairs={{0,8},{8,16},{16,24},{24,0},{32,40},{40,48},{48,56},{56,32},{64,72... | collective-permute-start | bytes 1572872 | tf_op jit(solution)/shard_map/ppermute | solution.py:302
  148.8 8.6 %collective-permute-start.14 = (f32[64,1024]{1,0:T(8,128)S(1)}, f32[64,1024]{1,0:T(8,128)S(1)}, u32[]{:S(2)}, u32[]{:S(2)}) collective-permute-start(f32[64,1024]{1,0:T(8,128)S(1)} %slice_add_fusion.8), channel_id=1, source_target_pairs={{0,96},{8,104},{16,112},{24,120},{32,0},{40,8},{48,16},{56,24},{64... | collective-permute-start | bytes 786440 | tf_op jit(solution)/shard_map/ppermute | solution.py:305
  152.1 7.3 %collective-permute-start.30 = (f32[64,1024]{1,0:T(8,128)S(1)}, f32[64,1024]{1,0:T(8,128)S(1)}, u32[]{:S(2)}, u32[]{:S(2)}) collective-permute-start(f32[64,1024]{1,0:T(8,128)S(1)} %slice_add_fusion), channel_id=1, source_target_pairs={{0,24},{8,0},{16,8},{24,16},{32,56},{40,32},{48,40},{56,48},{64,88... | collective-permute-start | bytes 786440 | tf_op jit(solution)/shard_map/ppermute | solution.py:305
  155.5 8.3 %collective-permute-start.2 = (f32[320,256]{1,0:T(8,128)S(1)}, f32[320,256]{1,0:T(8,128)S(1)}, u32[]{:S(2)}, u32[]{:S(2)}) collective-permute-start(f32[320,256]{1,0:T(8,128)S(1)} %add.170), channel_id=1, source_target_pairs={{0,6},{1,7},{2,4},{3,5},{4,2},{5,3},{6,0},{7,1},{8,14},{9,15},{10,... | collective-permute-start | bytes 983048 | tf_op jit(solution)/shard_map/ppermute | solution.py:348
  157.4 7.6 %collective-permute-start.6 = (f32[64,1024]{1,0:T(8,128)S(1)}, f32[64,1024]{1,0:T(8,128)S(1)}, u32[]{:S(2)}, u32[]{:S(2)}) collective-permute-start(f32[64,1024]{1,0:T(8,128)S(1)} %get-tuple-element.48), channel_id=1, source_target_pairs={{0,32},{8,40},{16,48},{24,56},{32,64},{40,72},{48,80},{56,88},{64,... | collective-permute-start | bytes 786440 | tf_op jit(solution)/shard_map/ppermute | solution.py:304
  157.4 9.8 %collective-permute-start.22 = (f32[64,1024]{1,0:T(8,128)S(1)}, f32[64,1024]{1,0:T(8,128)S(1)}, u32[]{:S(2)}, u32[]{:S(2)}) collective-permute-start(f32[64,1024]{1,0:T(8,128)S(1)} %get-tuple-element.44), channel_id=1, source_target_pairs={{0,8},{8,16},{16,24},{24,0},{32,40},{40,48},{48,56},{56,32},{64,72... | collective-permute-start | bytes 786440 | tf_op jit(solution)/shard_map/ppermute | solution.py:304
  159.2 10.2 %collective-permute-start.13 = (f32[64,1024]{1,0:T(8,128)S(1)}, f32[64,1024]{1,0:T(8,128)S(1)}, u32[]{:S(2)}, u32[]{:S(2)}) collective-permute-start(f32[64,1024]{1,0:T(8,128)S(1)} %get-tuple-element.46), channel_id=1, source_target_pairs={{0,32},{8,40},{16,48},{24,56},{32,64},{40,72},{48,80},{56,88},{64,... | collective-permute-start | bytes 786440 | tf_op jit(solution)/shard_map/ppermute | solution.py:304
  159.5 10.9 %collective-permute-start.29 = (f32[64,1024]{1,0:T(8,128)S(1)}, f32[64,1024]{1,0:T(8,128)S(1)}, u32[]{:S(2)}, u32[]{:S(2)}) collective-permute-start(f32[64,1024]{1,0:T(8,128)S(1)} %get-tuple-element.42), channel_id=1, source_target_pairs={{0,8},{8,16},{16,24},{24,0},{32,40},{40,48},{48,56},{56,32},{64,72... | collective-permute-start | bytes 786440 | tf_op jit(solution)/shard_map/ppermute | solution.py:304
  163.9 31.2 %collective-permute-start.3 = (f32[320,256]{1,0:T(8,128)S(1)}, f32[320,256]{1,0:T(8,128)S(1)}, u32[]{:S(2)}, u32[]{:S(2)}) collective-permute-start(f32[320,256]{1,0:T(8,128)S(1)} %add.171), channel_id=1, source_target_pairs={{0,1},{1,0},{2,3},{3,2},{4,5},{5,4},{6,7},{7,6},{8,9},{9,8},{10,11... | collective-permute-start | bytes 983048 | tf_op jit(solution)/shard_map/ppermute | solution.py:349
  165.1 6.1 %collective-permute-start.8 = (f32[32,1024]{1,0:T(8,128)S(1)}, f32[32,1024]{1,0:T(8,128)S(1)}, u32[]{:S(2)}, u32[]{:S(2)}) collective-permute-start(f32[32,1024]{1,0:T(8,128)S(1)} %pad_maximum_fusion.1), channel_id=1, source_target_pairs={{0,24},{8,0},{16,8},{24,16},{32,56},{40,32},{48,40},{56,48},{64,88... | collective-permute-start | bytes 393224 | tf_op jit(solution)/shard_map/ppermute | solution.py:303
  168.3 6.4 %collective-permute-start.24 = (f32[32,1024]{1,0:T(8,128)S(1)}, f32[32,1024]{1,0:T(8,128)S(1)}, u32[]{:S(2)}, u32[]{:S(2)}) collective-permute-start(f32[32,1024]{1,0:T(8,128)S(1)} %pad_maximum_fusion.5), channel_id=1, source_target_pairs={{0,96},{8,104},{16,112},{24,120},{32,0},{40,8},{48,16},{56,24},{64... | collective-permute-start | bytes 393224 | tf_op jit(solution)/shard_map/ppermute | solution.py:303
  169.4 5.3 %collective-permute-start.15 = (f32[32,1024]{1,0:T(8,128)S(1)}, f32[32,1024]{1,0:T(8,128)S(1)}, u32[]{:S(2)}, u32[]{:S(2)}) collective-permute-start(f32[32,1024]{1,0:T(8,128)S(1)} %pad_maximum_fusion.3), channel_id=1, source_target_pairs={{0,24},{8,0},{16,8},{24,16},{32,56},{40,32},{48,40},{56,48},{64,88... | collective-permute-start | bytes 393224 | tf_op jit(solution)/shard_map/ppermute | solution.py:303
  170.5 6.0 %collective-permute-start.31 = (f32[32,1024]{1,0:T(8,128)S(1)}, f32[32,1024]{1,0:T(8,128)S(1)}, u32[]{:S(2)}, u32[]{:S(2)}) collective-permute-start(f32[32,1024]{1,0:T(8,128)S(1)} %pad_maximum_fusion.7), channel_id=1, source_target_pairs={{0,96},{8,104},{16,112},{24,120},{32,0},{40,8},{48,16},{56,24},{64... | collective-permute-start | bytes 393224 | tf_op jit(solution)/shard_map/ppermute | solution.py:303
  171.2 36.9 %collective-permute-start.18 = (f32[16,1024]{1,0:T(8,128)S(1)}, f32[16,1024]{1,0:T(8,128)S(1)}, u32[]{:S(2)}, u32[]{:S(2)}) collective-permute-start(f32[16,1024]{1,0:T(8,128)S(1)} %get-tuple-element.61), channel_id=1, source_target_pairs={{0,24},{8,0},{16,8},{24,16},{32,56},{40,32},{48,40},{56,48},{64,88... | collective-permute-start | bytes 196616 | tf_op jit(solution)/shard_map/ppermute | solution.py:305
  174.6 6.2 %collective-permute-start.9 = (f32[32,1024]{1,0:T(8,128)S(1)}, f32[32,1024]{1,0:T(8,128)S(1)}, u32[]{:S(2)}, u32[]{:S(2)}) collective-permute-start(f32[32,1024]{1,0:T(8,128)S(1)} %pad_maximum_fusion.2), channel_id=1, source_target_pairs={{0,8},{8,16},{16,24},{24,0},{32,40},{40,48},{48,56},{56,32},{64,72... | collective-permute-start | bytes 393224 | tf_op jit(solution)/shard_map/ppermute | solution.py:302
  174.7 39.0 %collective-permute-start.34 = (f32[16,1024]{1,0:T(8,128)S(1)}, f32[16,1024]{1,0:T(8,128)S(1)}, u32[]{:S(2)}, u32[]{:S(2)}) collective-permute-start(f32[16,1024]{1,0:T(8,128)S(1)} %get-tuple-element.53), channel_id=1, source_target_pairs={{0,96},{8,104},{16,112},{24,120},{32,0},{40,8},{48,16},{56,24},{64... | collective-permute-start | bytes 196616 | tf_op jit(solution)/shard_map/ppermute | solution.py:305
  176.5 6.2 %collective-permute-start.25 = (f32[32,1024]{1,0:T(8,128)S(1)}, f32[32,1024]{1,0:T(8,128)S(1)}, u32[]{:S(2)}, u32[]{:S(2)}) collective-permute-start(f32[32,1024]{1,0:T(8,128)S(1)} %pad_maximum_fusion.6), channel_id=1, source_target_pairs={{0,32},{8,40},{16,48},{24,56},{32,64},{40,72},{48,80},{56,88},{64,... | collective-permute-start | bytes 393224 | tf_op jit(solution)/shard_map/ppermute | solution.py:302
  180.9 27.4 %collective-permute-start.19 = (f32[16,1024]{1,0:T(8,128)S(1)}, f32[16,1024]{1,0:T(8,128)S(1)}, u32[]{:S(2)}, u32[]{:S(2)}) collective-permute-start(f32[16,1024]{1,0:T(8,128)S(1)} %get-tuple-element.59), channel_id=1, source_target_pairs={{0,24},{8,0},{16,8},{24,16},{32,56},{40,32},{48,40},{56,48},{64,88... | collective-permute-start | bytes 196616 | tf_op jit(solution)/shard_map/ppermute | solution.py:305
  182.7 6.2 %collective-permute-start.16 = (f32[32,1024]{1,0:T(8,128)S(1)}, f32[32,1024]{1,0:T(8,128)S(1)}, u32[]{:S(2)}, u32[]{:S(2)}) collective-permute-start(f32[32,1024]{1,0:T(8,128)S(1)} %pad_maximum_fusion.4), channel_id=1, source_target_pairs={{0,8},{8,16},{16,24},{24,0},{32,40},{40,48},{48,56},{56,32},{64,72... | collective-permute-start | bytes 393224 | tf_op jit(solution)/shard_map/ppermute | solution.py:302
  188.9 6.2 %collective-permute-start.32 = (f32[32,1024]{1,0:T(8,128)S(1)}, f32[32,1024]{1,0:T(8,128)S(1)}, u32[]{:S(2)}, u32[]{:S(2)}) collective-permute-start(f32[32,1024]{1,0:T(8,128)S(1)} %pad_maximum_fusion.8), channel_id=1, source_target_pairs={{0,32},{8,40},{16,48},{24,56},{32,64},{40,72},{48,80},{56,88},{64,... | collective-permute-start | bytes 393224 | tf_op jit(solution)/shard_map/ppermute | solution.py:302
  195.1 18.7 %collective-permute-start.35 = (f32[16,1024]{1,0:T(8,128)S(1)}, f32[16,1024]{1,0:T(8,128)S(1)}, u32[]{:S(2)}, u32[]{:S(2)}) collective-permute-start(f32[16,1024]{1,0:T(8,128)S(1)} %get-tuple-element.51), channel_id=1, source_target_pairs={{0,96},{8,104},{16,112},{24,120},{32,0},{40,8},{48,16},{56,24},{64... | collective-permute-start | bytes 196616 | tf_op jit(solution)/shard_map/ppermute | solution.py:305
  195.1 5.5 %collective-permute-start.10 = (f32[16,1024]{1,0:T(8,128)S(1)}, f32[16,1024]{1,0:T(8,128)S(1)}, u32[]{:S(2)}, u32[]{:S(2)}) collective-permute-start(f32[16,1024]{1,0:T(8,128)S(1)} %slice_add_fusion.30), channel_id=1, source_target_pairs={{0,8},{8,16},{16,24},{24,0},{32,40},{40,48},{48,56},{56,32},{64,72... | collective-permute-start | bytes 196616 | tf_op jit(solution)/shard_map/ppermute | solution.py:304
  200.6 5.5 %collective-permute-start.17 = (f32[16,1024]{1,0:T(8,128)S(1)}, f32[16,1024]{1,0:T(8,128)S(1)}, u32[]{:S(2)}, u32[]{:S(2)}) collective-permute-start(f32[16,1024]{1,0:T(8,128)S(1)} %slice_add_fusion.28), channel_id=1, source_target_pairs={{0,8},{8,16},{16,24},{24,0},{32,40},{40,48},{48,56},{56,32},{64,72... | collective-permute-start | bytes 196616 | tf_op jit(solution)/shard_map/ppermute | solution.py:304
  206.1 5.5 %collective-permute-start.26 = (f32[16,1024]{1,0:T(8,128)S(1)}, f32[16,1024]{1,0:T(8,128)S(1)}, u32[]{:S(2)}, u32[]{:S(2)}) collective-permute-start(f32[16,1024]{1,0:T(8,128)S(1)} %slice_add_fusion.22), channel_id=1, source_target_pairs={{0,32},{8,40},{16,48},{24,56},{32,64},{40,72},{48,80},{56,88},{64,... | collective-permute-start | bytes 196616 | tf_op jit(solution)/shard_map/ppermute | solution.py:304
  208.2 5.5 %collective-permute-start.33 = (f32[16,1024]{1,0:T(8,128)S(1)}, f32[16,1024]{1,0:T(8,128)S(1)}, u32[]{:S(2)}, u32[]{:S(2)}) collective-permute-start(f32[16,1024]{1,0:T(8,128)S(1)} %slice_add_fusion.20), channel_id=1, source_target_pairs={{0,32},{8,40},{16,48},{24,56},{32,64},{40,72},{48,80},{56,88},{64,... | collective-permute-start | bytes 196616 | tf_op jit(solution)/shard_map/ppermute | solution.py:304
  213.8 0.8 copy-start.7

commit v2 on v0

v2 whole, which is shorter than its diff:
```python
import functools
import math

import jax
import jax.numpy as jnp
from jax import lax
from jax.experimental import pallas as pl
from jax.experimental.pallas import tpu as pltpu
from jax.sharding import PartitionSpec as P

F32 = jnp.float32
BF16 = jnp.bfloat16
STUDENT_C = 10.0 * math.log2(math.e)
TEACHER_C = 25.0
EPS = 1e-06
PARTS = 4
CALLS = 2
STAT_TILE = 1024
STAT_SUB = 256
SUB = 512

_KEEP = {0: (0, 3), 1: (0, 1), 2: (0, 3), 3: (0, 1)}
_SEND = {0: (1, 2), 1: (3, 2), 2: (1, 2), 3: (3, 2)}


def blocks_of(part):
    outer = _KEEP[part] + _SEND[part]
    if part < 2:
        return [(a, b) for a in outer for b in outer]
    return [(b, a) for a in outer for b in outer]


def block_start(kx, ky):
    place = lax.axis_index("batch")
    x, y = lax.div(place, 4), lax.rem(place, 4)
    return pl.multiple_of(lax.bitwise_xor(x, kx) * 64 + lax.bitwise_xor(y, ky) * 16, 16)


def stats_kernel(
    f_ref, c_ref, dir_hbm, t_hbm, ub_ref, ut_ref, inv_ref, colsum_ref, stat_ref,
    dbuf, tbuf, sacc, macc, tacc, dsem, tsem,
):
    rows = f_ref.shape[0]
    protos = dbuf.shape[1]
    tiles = protos // STAT_TILE

    def copies(n):
        cols = pl.ds(pl.multiple_of(n * STAT_TILE, STAT_TILE), STAT_TILE)
        return (
            pltpu.make_async_copy(dir_hbm.at[:, cols], dbuf.at[:, cols], dsem.at[n]),
            pltpu.make_async_copy(t_hbm.at[:, cols], tbuf.at[:, cols], tsem.at[n]),
        )

    for n in range(tiles):
        for copy in copies(n):
            copy.start()
    zf = f_ref[...].astype(F32)
    inv = 1.0 / jnp.sqrt(jnp.sum(zf * zf, axis=-1, keepdims=True) + EPS)
    ub = (zf * inv).astype(BF16)
    ub_ref[...] = ub
    ut_ref[...] = ub.T
    sacc[...] = jnp.zeros_like(sacc)
    macc[...] = jnp.full_like(macc, -1e30)
    tacc[...] = jnp.zeros_like(tacc)
    colsum_ref[...] = jnp.zeros_like(colsum_ref)

    @pl.loop(0, tiles)
    def _(n):
        for copy in copies(n):
            copy.wait()
        cols = pl.ds(pl.multiple_of(n * STAT_TILE, STAT_TILE), STAT_TILE)
        d = dbuf[:, cols].astype(F32)
        inv_col = 1.0 / jnp.sqrt(jnp.sum(d * d, axis=0, keepdims=True) + EPS)
        inv_ref[:, cols] = inv_col
        wb = (d * inv_col).astype(BF16)
        part = None
        for k in range(STAT_TILE // STAT_SUB):
            s = jnp.dot(
                ub_ref[...], wb[:, k * STAT_SUB : (k + 1) * STAT_SUB], preferred_element_type=F32
            )
            e = jnp.exp2(s * STUDENT_C)
            for m in range(STAT_SUB // 128):
                lane = e[:, m * 128 : (m + 1) * 128]
                part = lane if part is None else part + lane
        sacc[...] += part
        t = tbuf[:, cols].astype(F32)
        colsum_ref[pl.ds(n, 1), :] = jnp.sum(t, axis=0, keepdims=True)
        diff = t - c_ref[:, cols]
        lanes = [diff[:, m * 128 : (m + 1) * 128] for m in range(STAT_TILE // 128)]
        old = macc[...]
        top = functools.reduce(jnp.maximum, lanes, old)
        total = tacc[...] * jnp.exp((old - top) * TEACHER_C)
        for lane in lanes:
            total += jnp.exp((lane - top) * TEACHER_C)
        macc[...] = top
        tacc[...] = total

    stat_ref[...] = jnp.zeros_like(stat_ref)
    for r in range(rows // 128):
        stat_ref[r : r + 1, :] = jnp.sum(sacc[r * 128 : (r + 1) * 128, :].T, axis=0, keepdims=True)
    tops = macc[...].T
    best = jnp.max(tops, axis=0, keepdims=True)
    stat_ref[5:6, :] = best
    stat_ref[6:7, :] = jnp.sum(
        tacc[...].T * jnp.exp((tops - best) * TEACHER_C), axis=0, keepdims=True
    )


def weight_kernel(images, call, *refs):
    refs = list(refs)
    take = lambda n: [refs.pop(0) for _ in range(n)]
    first, last = call == 0, call == CALLS - 1
    ub_ref, ut_ref, dir_ref, inv_ref, t_ref, c_ref = take(6)
    stat_ref, colsum_ref = take(2) if first else (None, None)
    arow, brow, mrow, before_ref = take(4) if not first else (None,) * 4
    (f_ref,) = take(1) if last else (None,)
    keep_refs, send_refs = take(PARTS), take(PARTS)
    fouts = take(2 if last else 1)
    rows = ub_ref.shape[0]
    img = rows // 10
    if first:
        arow, brow, mrow = take(3)
        scale = 1.0 / (0.1 * 18.0 * images)
        stat = stat_ref[...]
        sums = jnp.sum(stat, axis=0)
        top = jnp.max(stat[:, 5:6, :], axis=0)
        ttot = jnp.sum(stat[:, 6:7, :] * jnp.exp((stat[:, 5:6, :] - top) * TEACHER_C), axis=0)
        packed = jnp.concatenate([sums[0:5], top, ttot, jnp.zeros((121, 128), F32)], axis=0).T
        for r in range(5):
            arow[r * 128 : (r + 1) * 128, :] = jnp.broadcast_to(
                (scale if r == 0 else 2.0 * scale) / packed[:, r : r + 1], (128, 128)
            )
        mrow[...] = jnp.broadcast_to(packed[:, 5:6], (128, 128))
        brow[...] = jnp.broadcast_to(scale / packed[:, 6:7], (128, 128))
    ub = ub_ref[...]
    protos = dir_ref.shape[1]
    width = protos // PARTS // CALLS
    wide = lambda v: jnp.concatenate([v] * (SUB // 128), axis=1)
    total = None
    for part in range(PARTS):
        ut = jnp.concatenate(
            [ut_ref[pl.ds(block_start(kx, ky), 16), :] for kx, ky in blocks_of(part)], axis=0
        )
        base = (part * CALLS + call) * width
        for at in range(0, width, SUB):
            cols, mine = slice(at, at + SUB), slice(base + at, base + at + SUB)
            inv = inv_ref[:, mine]
            wb = (dir_ref[:, mine].astype(F32) * inv).astype(BF16)
            s = jnp.dot(ub, wb, preferred_element_type=F32)
            diff = t_ref[:, mine].astype(F32) - c_ref[:, mine]
            t = jnp.exp((diff - wide(mrow[...])) * TEACHER_C) * wide(brow[...])
            t0, t1 = t[:img], t[img:]
            both = t0 + t1
            rounded = []
            for j in range(10):
                r = slice(j * img, (j + 1) * img)
                target = t1 if j == 0 else t0 if j == 1 else both
                rounded.append(
                    (jnp.exp2(s[r] * STUDENT_C) * wide(arow[r, :]) - target).astype(BF16)
                )
            g = jnp.concatenate(rounded, axis=0)
            gw = jnp.dot(ut, g, preferred_element_type=F32)
            term = lax.dot_general(g, wb, (((1,), (1,)), ((), ())), preferred_element_type=F32)
            total = term if total is None else total + term
            ds = []
            dots = jnp.zeros((16, SUB), F32)
            for n, (kx, ky) in enumerate(blocks_of(part)):
                d = dir_ref[pl.ds(block_start(kx, ky), 16), mine].astype(F32)
                ds.append(d)
                dots += gw[n * 16 : (n + 1) * 16] * d
            factor = jnp.sum(dots, axis=0, keepdims=True) * inv * inv * inv
            for n in range(16):
                ref, row = (keep_refs[part], n * 16) if n < 8 else (send_refs[part], (n - 8) * 16)
                ref[row : row + 16, cols] = gw[n * 16 : (n + 1) * 16] * inv - ds[n] * factor
    if first:
        send_refs[0][128:136, :] = colsum_ref[...]
    else:
        total = before_ref[...] + total
    if not last:
        fouts[0][...] = total
        return
    (acc,) = take(1)
    zf = f_ref[...].astype(F32)
    inv = 1.0 / jnp.sqrt(jnp.sum(zf * zf, axis=-1, keepdims=True) + EPS)
    unit = zf * inv
    acc[...] = (total - unit * jnp.sum(total * unit, axis=-1, keepdims=True)) * inv
    half = rows // 2
    core = lax.rem(lax.axis_index("proto"), 2)
    fouts[0][...] = acc[pl.ds(pl.multiple_of(core * half, 8), half), :]
    fouts[1][...] = acc[pl.ds(pl.multiple_of((1 - core) * half, 8), half), :]


def final_kernel(images, c_ref, cs_ref, csgot_ref, mine_ref, other_ref, *refs):
    keeps, gots = refs[: PARTS * CALLS], refs[PARTS * CALLS : PARTS * CALLS + PARTS]
    feat_ref, dir_ref, center_ref = refs[PARTS * CALLS + PARTS :]
    half = mine_ref.shape[0]
    core = lax.rem(lax.axis_index("proto"), 2)
    feat_ref[pl.ds(pl.multiple_of(core * half, 8), half), :] = mine_ref[...]
    feat_ref[pl.ds(pl.multiple_of((1 - core) * half, 8), half), :] = other_ref[...]
    width = keeps[0].shape[1]
    for part in range(PARTS):
        for call in range(CALLS):
            n = part * CALLS + call
            got = gots[part][call * 16 : (call + 1) * 16, :]
            dir_ref[:, n * width : (n + 1) * width] = keeps[n][...] + got
    cs = cs_ref[...] + csgot_ref[...]
    for n in range(8):
        cols = slice(n * STAT_TILE, (n + 1) * STAT_TILE)
        center_ref[:, cols] = 0.9 * c_ref[:, cols] + 0.1 * cs[n : n + 1, :] / (2.0 * images)


IN_VMEM = pl.BlockSpec(memory_space=pltpu.VMEM)


def params(mib):
    return pltpu.CompilerParams(vmem_limit_bytes=mib * 1024 * 1024)


def stats_call(f, dirs, teach, center):
    rows, dim = f.shape
    protos = dirs.shape[1]
    trows = teach.shape[0]
    tiles = protos // STAT_TILE
    return pl.pallas_call(
        stats_kernel,
        in_specs=[IN_VMEM, IN_VMEM] + [pl.BlockSpec(memory_space=pltpu.HBM)] * 2,
        out_specs=[IN_VMEM] * 5,
        scratch_shapes=[
            pltpu.VMEM((dim, protos), BF16),
            pltpu.VMEM((trows, protos), BF16),
            pltpu.VMEM((rows, 128), F32),
            pltpu.VMEM((trows, 128), F32),
            pltpu.VMEM((trows, 128), F32),
            pltpu.SemaphoreType.DMA((tiles,)),
            pltpu.SemaphoreType.DMA((tiles,)),
        ],
        out_shape=[
            jax.ShapeDtypeStruct((rows, dim), BF16),
            jax.ShapeDtypeStruct((dim, rows), BF16),
            jax.ShapeDtypeStruct((1, protos), F32),
            jax.ShapeDtypeStruct((8, STAT_TILE), F32),
            jax.ShapeDtypeStruct((8, 128), F32),
        ],
        compiler_params=params(53),
        cost_estimate=pl.CostEstimate(
            flops=2 * rows * dim * protos,
            bytes_accessed=2 * (dim + trows) * protos,
            transcendentals=(rows + trows) * protos,
        ),
        name="stats",
    )(f, center, dirs, teach)


def weight_call(images, call, ub, ut, dirs, inv, teach, center, extra):
    rows, dim = ub.shape
    protos = dirs.shape[1]
    trows = teach.shape[0]
    width = protos // PARTS // CALLS
    first, last = call == 0, call == CALLS - 1
    shape = lambda *dims: jax.ShapeDtypeStruct(dims, F32)
    outs = [shape(128, width)] * PARTS
    outs += [shape(136 if first and part == 0 else 128, width) for part in range(PARTS)]
    outs += [shape(rows // 2, dim)] * 2 if last else [shape(rows, dim)]
    outs += [shape(rows, 128), shape(trows, 128), shape(trows, 128)] if first else []
    args = [ub, ut, dirs, inv, teach, center, *extra]
    out = pl.pallas_call(
        functools.partial(weight_kernel, images, call),
        in_specs=[IN_VMEM] * len(args),
        out_specs=[IN_VMEM] * len(outs),
        scratch_shapes=[pltpu.VMEM((rows, dim), F32)] if last else [],
        out_shape=outs,
        compiler_params=params(8),
        cost_estimate=pl.CostEstimate(
            flops=6 * rows * dim * protos // CALLS,
            bytes_accessed=(2 * (dim + trows) + 4 * dim) * protos // CALLS,
            transcendentals=(rows + trows) * protos // CALLS,
        ),
        name="weights",
    )(*args)
    return out[:PARTS], out[PARTS : 2 * PARTS], out[2 * PARTS :]


def final_call(images, center, cs, csgot, mine, other, keeps, gots):
    half, dim = mine.shape
    protos = center.shape[1]
    args = [center, cs, csgot, mine, other, *keeps, *gots]
    return pl.pallas_call(
        functools.partial(final_kernel, images),
        in_specs=[IN_VMEM] * len(args),
        out_specs=[IN_VMEM] * 3,
        out_shape=[
            jax.ShapeDtypeStruct((2 * half, dim), F32),
            jax.ShapeDtypeStruct((16, protos), F32),
            jax.ShapeDtypeStruct((1, protos), F32),
        ],
        compiler_params=params(8),
        name="final",
    )(*args)


def pairs_x(k):
    return [(x * 4 + y, (x ^ k) * 4 + y) for x in range(4) for y in range(4)]


def pairs_y(k):
    return [(x * 4 + y, x * 4 + (y ^ k)) for x in range(4) for y in range(4)]


X1, X3, Y1, Y3 = pairs_x(1), pairs_x(3), pairs_y(1), pairs_y(3)
ORDER = [(X1, X3, Y1, Y3), (X3, X1, Y3, Y1), (Y1, Y3, X1, X3), (Y3, Y1, X3, X1)]


def on_device(features, teacher_logits, directions, center):
    crops, img, dim = features.shape
    images = img * lax.axis_size("batch")
    protos = directions.shape[1]
    rows = crops * img
    f = features.reshape(rows, dim)
    teach = teacher_logits.reshape(-1, protos)
    cent = center.reshape(1, protos)
    ub, ut, inv, colsum, stat = stats_call(f, directions, teach, cent)
    stats = lax.all_to_all(jnp.broadcast_to(stat, (8, 8, 128)), "proto", 0, 0)
    keeps, sends, extra = [], [], [stats, colsum]
    for call in range(CALLS):
        if call == CALLS - 1:
            extra = extra + [f]
        keep, send, rest = weight_call(images, call, ub, ut, directions, inv, teach, cent, extra)
        factors = rest[1:] if call == 0 else factors
        extra = [*factors, rest[0]]
        keeps.append(keep)
        sends.append([lax.ppermute(send[p], "batch", ORDER[p][0]) for p in range(PARTS)])
    fkeep, fsend = rest
    cs, before = colsum, None
    got = [[None] * CALLS for _ in range(PARTS)]
    for call in range(CALLS):
        for part in range(PARTS):
            block = sends[call][part]
            if before is not None:
                block, _ = lax.optimization_barrier((block, before))
            before = block
            got[part][call] = block[:128]
            if call == 0 and part == 0:
                cs = cs + block[128:]
    fsend, _ = lax.optimization_barrier((fsend, before))
    keeps = [[keeps[call][part] for call in range(CALLS)] for part in range(PARTS)]
    for n in (1, 2, 3):
        size = 128 >> n
        arrived, before = [], None
        for part in range(PARTS):
            out = [keeps[part][c][size:] + got[part][c][size:] for c in range(CALLS)]
            out += [cs] if part == 0 else []
            keeps[part] = [keeps[part][c][:size] + got[part][c][:size] for c in range(CALLS)]
            block = lax.ppermute(jnp.concatenate(out, axis=0), "batch", ORDER[part][n])
            if before is not None:
                block, _ = lax.optimization_barrier((block, before))
            before = block
            arrived.append(block)
            got[part] = [block[c * size : (c + 1) * size] for c in range(CALLS)]
        if n < 3:
            cs = cs + arrived[0][CALLS * size :]
    total = fkeep + lax.ppermute(fsend, "proto", [(i, i ^ 1) for i in range(8)])
    total = total + lax.ppermute(total, "proto", [(i, i ^ 2) for i in range(8)])
    total = total + lax.ppermute(total, "proto", [(i, i ^ 6) for i in range(8)])
    other = lax.ppermute(total, "proto", [(i, i ^ 1) for i in range(8)])
    keeps = [keeps[part][call] for part in range(PARTS) for call in range(CALLS)]
    csgot = arrived[0][CALLS * 16 :]
    grad_features, grad_directions, new_center = final_call(
        images, cent, cs, csgot, total, other, keeps, arrived
    )
    return (
        grad_features.reshape(crops, img, dim),
        grad_directions,
        new_center.reshape(protos),
    )


def solution(mesh):
    in_specs = (P(None, "batch", None), P(None, "batch", "proto"), P(None, "proto"), P("proto"))
    out_specs = (P(None, "batch", None), P("batch", "proto"), P("proto"))
    return jax.shard_map(
        on_device, mesh=mesh, in_specs=in_specs, out_specs=out_specs, check_vma=False
    )
```

time: 316 us -> 100 us (0.32)
  blocking collectives: 105 us -> 10.6 us
  waiting for transfers between devices: 114 us -> 34.5 us
  other arithmetic: 45.3 us -> 1.42 us
  starting transfers between devices: 0.08 us -> 28.6 us
  matrix products: 26 us -> 0 us
  Pallas kernels: 0 us -> 22.3 us
  between operations: 14.2 us -> 0.9 us
  local copies, waits for them, and re-layouts: 11.9 us -> 0.77 us
    psum x2 -> x0, waiting for transfers between devices: 114 us -> none  [the longest x1 114 us: on_device(): grad_all = lax.psum(full_local, 'batch')]
    psum x2 -> x0, blocking collectives: 88.1 us -> none  [the longest x1 75.1 us: on_device(): col_sums = lax.psum(col_local, 'batch')]
    ppermute x0 -> x24, waiting for transfers between devices: none -> 34.5 us  [the longest x12 20 us: on_device(): block = lax.ppermute(jnp.concatenate(out, axis=0), 'batch', ORDER[part][n])]
    ppermute x0 -> x24, starting transfers between devices: none -> 28.6 us  [the longest x8 13.3 us: on_device(): lax.ppermute(send[p], 'batch', ORDER[p][0])]
    dot_general x3 -> x0, matrix products: 26 us -> none  [the longest x1 12.4 us: on_device(): jnp.einsum('cbd,dp->cbp', unit_b, weight_b, preferred_element_type=jnp.fl...]
    pallas_call x0 -> x4, Pallas kernels: none -> 22.3 us  [the longest x2 11.7 us: weight_call(): pl.pallas_call(functools.partial(weight_kernel, images, call), in_specs=[...]
    reduce_sum x5 -> x0, other arithmetic: 20.8 us -> none  [the longest x1 9.33 us: on_device(): jnp.sum(s_exp, axis=-1, keepdims=True)]
    pmax x1 -> x0, blocking collectives: 16.4 us -> none  [on_device(): s_top, t_top = lax.pmax((s_loc, t_loc), 'proto')]
  transfers between devices with their start and end apart: 2 -> 24, of which waited for: 1 -> 12; matrix products, arithmetic and copies ran while one was open for 5% -> 1% of each run, Pallas kernels for 0% -> 6%
where the time goes in v2:
time: 100 us; the launch traced here: 99.2 us
  waiting for transfers between devices  34.5 us (34%)
  starting transfers between devices  28.6 us (29%)
  Pallas kernels  22.3 us (22%)
  blocking collectives  10.6 us (11%)
  other arithmetic  1.42 us (1%)
    ppermute x12, waiting for transfers between devices, on_device(): block = lax.ppermute(jnp.concatenate(out, axis=0), 'batch', ORDER[part][n])  20 us
    ppermute x8, starting transfers between devices, on_device(): lax.ppermute(send[p], 'batch', ORDER[p][0])  13.3 us
    ppermute x12, starting transfers between devices, on_device(): block = lax.ppermute(jnp.concatenate(out, axis=0), 'batch', ORDER[part][n])  13.3 us
    ppermute x8, waiting for transfers between devices, on_device(): lax.ppermute(send[p], 'batch', ORDER[p][0])  12.9 us
    pallas_call x2, Pallas kernels, weight_call(): pl.pallas_call(functools.partial(weight_kernel, images, call), in_specs=[...  11.7 us
    all_to_all x1, blocking collectives, on_device(): stats = lax.all_to_all(jnp.broadcast_to(stat, (8, 8, 128)), 'proto', 0, 0)  10.6 us
    pallas_call x1, Pallas kernels, stats_call(): pl.pallas_call(stats_kernel, in_specs=[IN_VMEM, IN_VMEM] + [pl.BlockSpec(...  9.5 us
  transfers between devices with their start and end apart: 24, of which 12 were waited for; matrix products, arithmetic and copies ran while one was open for 1% of the time, Pallas kernels for 6%

profile of v2, /device:TPU:0, one launch (start us, length us, event | category | flops | bytes accessed | tf_op | source)
XLA Modules:
  0.0 99.2 jit_solution(16958862855343130081)
XLA Ops:
  0.6 0.7 copy-done
  1.4 9.5 %stats.1 = (bf16[640,256]{1,0:T(8,128)(2,1)S(1)}, bf16[256,640]{1,0:T(8,128)(2,1)S(1)}, f32[1,8192]{1,0:T(1,128)S(1)}, f32[8,1024]{1,0:T(8,128)S(1)}, f32[8,128]{1,0:T(8,128)S(1)}) custom-call(bf16[640,256]{1,0:T(8,128)(2,1)} %bitcast.12, f32[1,8192]{1,0:T(1,128)S(1)} %bitcast.5, bf16[256,8192]{1,0:T(8,128)(2,1)} %refs_2_.3, bf16[128,8192]{1,0:T(8,128)(2,1)} %bitcast.9), custom_call_target="tpu_custom_call" | custom-call | flops 2684354560 | bytes 6291456 | tf_op jit(solution)/shard_map/stats/pallas_call | solution.py:224
  10.9 10.6 %all_to_all.5.refs_6_ = f32[8,8,128]{2,1,0:T(8,128)S(1)} all-to-all(f32[8,8,128]{2,1,0:T(8,128)S(1)} %broadcast_in_dim.3), channel_id=1, replica_groups=mesh['batch'=16,'proto'=8] {'proto'}, dimensions={0} | all-to-all | bytes 65536 | tf_op jit(solution)/shard_map/all_to_all | solution.py:322
  21.6 5.7 %weights.2 = (f32[128,1024]{1,0:T(8,128)S(1)}, f32[128,1024]{1,0:T(8,128)S(1)}, f32[128,1024]{1,0:T(8,128)S(1)}, f32[128,1024]{1,0:T(8,128)S(1)}, f32[136,1024]{...) custom-call(bf16[640,256]{1,0:T(8,128)(2,1)S(1)} %get-tuple-element., ...), custom_call_target="tpu_custom_call" | custom-call | flops 4026531840 | bytes 7340032 | tf_op jit(solution)/shard_map/weights/pallas_call | solution.py:266
  27.3 1.6 %collective-permute-start = (f32[136,1024]{1,0:T(8,128)S(1)}, f32[136,1024]{1,0:T(8,128)S(1)}, u32[]{:S(2)}, u32[]{:S(2)}) collective-permute-start(f32[136,1024]{1,0:T(8,128)S(1)} %get-tuple-element.55), channel_id=1, source_target_pairs={{0,32},{8,40},{16,48},{24,56},{32,0},{40,8},{48,16},{56,24},{64,96... | collective-permute-start | bytes 1671176 | tf_op jit(solution)/shard_map/ppermute | solution.py:331
  28.9 2.1 %collective-permute-start.4 = (f32[128,1024]{1,0:T(8,128)S(1)}, f32[128,1024]{1,0:T(8,128)S(1)}, u32[]{:S(2)}, u32[]{:S(2)}) collective-permute-start(f32[128,1024]{1,0:T(8,128)S(1)} %get-tuple-element.65), channel_id=1, source_target_pairs={{0,96},{8,104},{16,112},{24,120},{32,64},{40,72},{48,80},{56,88},{... | collective-permute-start | bytes 1572872 | tf_op jit(solution)/shard_map/ppermute | solution.py:331
  31.0 1.6 %collective-permute-start.3 = (f32[128,1024]{1,0:T(8,128)S(1)}, f32[128,1024]{1,0:T(8,128)S(1)}, u32[]{:S(2)}, u32[]{:S(2)}) collective-permute-start(f32[128,1024]{1,0:T(8,128)S(1)} %get-tuple-element.64), channel_id=1, source_target_pairs={{0,8},{8,0},{16,24},{24,16},{32,40},{40,32},{48,56},{56,48},{64,72... | collective-permute-start | bytes 1572872 | tf_op jit(solution)/shard_map/ppermute | solution.py:331
  32.5 2.2 %collective-permute-start.2 = (f32[128,1024]{1,0:T(8,128)S(1)}, f32[128,1024]{1,0:T(8,128)S(1)}, u32[]{:S(2)}, u32[]{:S(2)}) collective-permute-start(f32[128,1024]{1,0:T(8,128)S(1)} %get-tuple-element.63), channel_id=1, source_target_pairs={{0,24},{8,16},{16,8},{24,0},{32,56},{40,48},{48,40},{56,32},{64,88... | collective-permute-start | bytes 1572872 | tf_op jit(solution)/shard_map/ppermute | solution.py:331
  34.7 6.0 %weights.3 = (f32[128,1024]{1,0:T(8,128)S(1)}, f32[128,1024]{1,0:T(8,128)S(1)}, f32[128,1024]{1,0:T(8,128)S(1)}, f32[128,1024]{1,0:T(8,128)S(1)}, f32[128,1024]{...) custom-call(bf16[640,256]{1,0:T(8,128)(2,1)S(1)} %get-tuple-element., ...), custom_call_target="tpu_custom_call" | custom-call | flops 4026531840 | bytes 7340032 | tf_op jit(solution)/shard_map/weights/pallas_call | solution.py:266
  40.7 0.7 collective-permute-start.1
  41.4 2.0 %collective-permute-done.4 = f32[128,1024]{1,0:T(8,128)S(1)} collective-permute-done((f32[128,1024]{1,0:T(8,128)S(1)}, f32[128,1024]{1,0:T(8,128)S(1)}, u32[]{:S(2)}, u32[]{:S(2)}) %collective-permute-start.4) | collective-permute-done | bytes 524320 | tf_op jit(solution)/shard_map/ppermute | solution.py:331
  43.4 3.0 %collective-permute-start.8 = (f32[128,1024]{1,0:T(8,128)S(1)}, f32[128,1024]{1,0:T(8,128)S(1)}, u32[]{:S(2)}, u32[]{:S(2)}) collective-permute-start(f32[128,1024]{1,0:T(8,128)S(1)} %get-tuple-element.72), channel_id=1, source_target_pairs={{0,24},{8,16},{16,8},{24,0},{32,56},{40,48},{48,40},{56,32},{64,88... | collective-permute-start | bytes 1572872 | tf_op jit(solution)/shard_map/ppermute | solution.py:331
  46.4 0.0 collective-permute-done
  46.4 0.2 collective-permute-start.9
  46.6 0.0 collective-permute-done.3
  46.6 2.1 %collective-permute-start.10 = (f32[128,1024]{1,0:T(8,128)S(1)}, f32[128,1024]{1,0:T(8,128)S(1)}, u32[]{:S(2)}, u32[]{:S(2)}) collective-permute-start(f32[128,1024]{1,0:T(8,128)S(1)} %get-tuple-element.74), channel_id=1, source_target_pairs={{0,96},{8,104},{16,112},{24,120},{32,64},{40,72},{48,80},{56,88},{... | collective-permute-start | bytes 1572872 | tf_op jit(solution)/shard_map/ppermute | solution.py:331
  48.7 0.1 slice_add_fusion.12
  48.7 0.1 slice_add_fusion.8
  48.8 0.0 collective-permute-done.2
  48.8 4.5 %collective-permute-done.1 = f32[128,1024]{1,0:T(8,128)S(1)} collective-permute-done((f32[128,1024]{1,0:T(8,128)S(1)}, f32[128,1024]{1,0:T(8,128)S(1)}, u32[]{:S(2)}, u32[]{:S(2)}) %collective-permute-start.1) | collective-permute-done | bytes 524320 | tf_op jit(solution)/shard_map/ppermute | solution.py:331
  53.3 0.1 slice_add_fusion.4
  53.3 0.1 slice_add_fusion.14
  53.4 6.4 %collective-permute-done.10 = f32[128,1024]{1,0:T(8,128)S(1)} collective-permute-done((f32[128,1024]{1,0:T(8,128)S(1)}, f32[128,1024]{1,0:T(8,128)S(1)}, u32[]{:S(2)}, u32[]{:S(2)}) %collective-permute-start.10) | collective-permute-done | bytes 524320 | tf_op jit(solution)/shard_map/ppermute | solution.py:331
  59.8 0.0 collective-permute-done.9
  59.8 0.1 slice_add_fusion.10
  59.9 0.1 slice_add_fusion.6
  60.0 0.0 collective-permute-done.8
  60.0 0.1 collective-permute-start.15
  60.2 0.9 collective-permute-start.17
  61.1 0.1 slice_add_fusion
  61.2 2.2 %collective-permute-start.5 = (f32[136,1024]{1,0:T(8,128)S(1)}, f32[136,1024]{1,0:T(8,128)S(1)}, u32[]{:S(2)}, u32[]{:S(2)}) collective-permute-start(f32[136,1024]{1,0:T(8,128)S(1)} %pad_maximum_fusion), channel_id=1, source_target_pairs={{0,96},{8,104},{16,112},{24,120},{32,64},{40,72},{48,80},{56,88},{... | collective-permute-start | bytes 1671176 | tf_op jit(solution)/shard_map/ppermute | solution.py:353
  63.4 0.1 slice_add_fusion.2
  63.5 0.9 collective-permute-start.19
  64.5 0.0 collective-permute-start.11
  64.5 1.6 %collective-permute-done.11 = f32[320,256]{1,0:T(8,128)S(1)} collective-permute-done((f32[320,256]{1,0:T(8,128)S(1)}, f32[320,256]{1,0:T(8,128)S(1)}, u32[]{:S(2)}, u32[]{:S(2)}) %collective-permute-start.11) | collective-permute-done | bytes 327712 | tf_op jit(solution)/shard_map/ppermute | solution.py:361
  66.2 0.6 collective-permute-start.12
  66.8 4.5 %collective-permute-done.15 = f32[128,1024]{1,0:T(8,128)S(1)} collective-permute-done((f32[128,1024]{1,0:T(8,128)S(1)}, f32[128,1024]{1,0:T(8,128)S(1)}, u32[]{:S(2)}, u32[]{:S(2)}) %collective-permute-start.15) | collective-permute-done | bytes 524320 | tf_op jit(solution)/shard_map/ppermute | solution.py:353
  71.3 3.3 %collective-permute-done.5 = f32[136,1024]{1,0:T(8,128)S(1)} collective-permute-done((f32[136,1024]{1,0:T(8,128)S(1)}, f32[136,1024]{1,0:T(8,128)S(1)}, u32[]{:S(2)}, u32[]{:S(2)}) %collective-permute-start.5) | collective-permute-done | bytes 557088 | tf_op jit(solution)/shard_map/ppermute | solution.py:353
  74.6 0.0 collective-permute-done.17
  74.6 0.0 collective-permute-done.19
  74.6 0.1 slice_add_fusion.24
  74.7 2.1 %collective-permute-start.16 = (f32[64,1024]{1,0:T(8,128)S(1)}, f32[64,1024]{1,0:T(8,128)S(1)}, u32[]{:S(2)}, u32[]{:S(2)}) collective-permute-start(f32[64,1024]{1,0:T(8,128)S(1)} %pad_maximum_fusion.5), channel_id=1, source_target_pairs={{0,24},{8,16},{16,8},{24,0},{32,56},{40,48},{48,40},{56,32},{64,88... | collective-permute-start | bytes 786440 | tf_op jit(solution)/shard_map/ppermute | solution.py:353
  76.8 0.1 slice_add_fusion.20
  76.9 1.2 %collective-permute-start.18 = (f32[64,1024]{1,0:T(8,128)S(1)}, f32[64,1024]{1,0:T(8,128)S(1)}, u32[]{:S(2)}, u32[]{:S(2)}) collective-permute-start(f32[64,1024]{1,0:T(8,128)S(1)} %pad_maximum_fusion.6), channel_id=1, source_target_pairs={{0,32},{8,40},{16,48},{24,56},{32,0},{40,8},{48,16},{56,24},{64,96... | collective-permute-start | bytes 786440 | tf_op jit(solution)/shard_map/ppermute | solution.py:353
  78.1 0.1 slice_add_fusion.29
  78.2 0.3 collective-permute-start.6
  78.5 0.1 slice_add_fusion.16
  78.6 1.5 %collective-permute-start.20 = (f32[64,1024]{1,0:T(8,128)S(1)}, f32[64,1024]{1,0:T(8,128)S(1)}, u32[]{:S(2)}, u32[]{:S(2)}) collective-permute-start(f32[64,1024]{1,0:T(8,128)S(1)} %pad_maximum_fusion.7), channel_id=1, source_target_pairs={{0,96},{8,104},{16,112},{24,120},{32,64},{40,72},{48,80},{56,88},{... | collective-permute-start | bytes 786440 | tf_op jit(solution)/shard_map/ppermute | solution.py:353
  80.1 0.0 collective-permute-done.12
  80.1 1.2 %collective-permute-start.13 = (f32[320,256]{1,0:T(8,128)S(1)}, f32[320,256]{1,0:T(8,128)S(1)}, u32[]{:S(2)}, u32[]{:S(2)}) collective-permute-start(f32[320,256]{1,0:T(8,128)S(1)} %add.176), channel_id=1, source_target_pairs={{0,6},{1,7},{2,4},{3,5},{4,2},{5,3},{6,0},{7,1},{8,14},{9,15},{10,... | collective-permute-start | bytes 983048 | tf_op jit(solution)/shard_map/ppermute | solution.py:363
  81.4 1.0 collective-permute-done.16
  82.3 3.1 %collective-permute-done.6 = f32[72,1024]{1,0:T(8,128)S(1)} collective-permute-done((f32[72,1024]{1,0:T(8,128)S(1)}, f32[72,1024]{1,0:T(8,128)S(1)}, u32[]{:S(2)}, u32[]{:S(2)}) %collective-permute-start.6) | collective-permute-done | bytes 294944 | tf_op jit(solution)/shard_map/ppermute | solution.py:353
  85.4 2.3 %collective-permute-done.20 = f32[64,1024]{1,0:T(8,128)S(1)} collective-permute-done((f32[64,1024]{1,0:T(8,128)S(1)}, f32[64,1024]{1,0:T(8,128)S(1)}, u32[]{:S(2)}, u32[]{:S(2)}) %collective-permute-start.20) | collective-permute-done | bytes 262176 | tf_op jit(solution)/shard_map/ppermute | solution.py:353
  87.7 1.5 %collective-permute-start.22 = (f32[32,1024]{1,0:T(8,128)S(1)}, f32[32,1024]{1,0:T(8,128)S(1)}, u32[]{:S(2)}, u32[]{:S(2)}) collective-permute-start(f32[32,1024]{1,0:T(8,128)S(1)} %pad_maximum_fusion.10), channel_id=1, source_target_pairs={{0,96},{8,104},{16,112},{24,120},{32,64},{40,72},{48,80},{56,88},{... | collective-permute-start | bytes 393224 | tf_op jit(solution)/shard_map/ppermute | solution.py:353
  89.3 1.9 %collective-permute-start.21 = (f32[32,1024]{1,0:T(8,128)S(1)}, f32[32,1024]{1,0:T(8,128)S(1)}, u32[]{:S(2)}, u32[]{:S(2)}) collective-permute-start(f32[32,1024]{1,0:T(8,128)S(1)} %pad_maximum_fusion.9), channel_id=1, source_target_pairs={{0,8},{8,0},{16,24},{24,16},{32,40},{40,32},{48,56},{56,48},{64,72... | collective-permute-start | bytes 393224 | tf_op jit(solution)/shard_map/ppermute | solution.py:353
  91.2 0.7 collective-permute-start.7
  92.0 0.1 collective-permute-start.14
  92.1 0.1 collective-permute-start.23
  92.2 2.1 %collective-permute-done.21.refs_9_ = f32[32,1024]{1,0:T(8,128)S(1)} collective-permute-done((f32[32,1024]{1,0:T(8,128)S(1)}, f32[32,1024]{1,0:T(8,128)S(1)}, u32[]{:S(2)}, u32[]{:S(2)}) %collective-permute-start.21) | collective-permute-done | bytes 131104 | tf_op jit(solution)/shard_map/ppermute | solution.py:353
  94.3 3.5 %collective-permute-done.7.refs_8_ = f32[40,1024]{1,0:T(8,128)S(1)} collective-permute-done((f32[40,1024]{1,0:T(8,128)S(1)}, f32[40,1024]{1,0:T(8,128)S(1)}, u32[]{:S(2)}, u32[]{:S(2)}) %collective-permute-start.7) | collective-permute-done | bytes 163872 | tf_op jit(solution)/shard_map/ppermute | solution.py:353
  97.8 0.0 collective-permute-done.22.refs_10_
  97.8 0.2 collective-permute-done.23.refs_11_
  98.1 0.0 collective-permute-done.14.other_ref
  98.1 1.1 %final.1 = (f32[640,256]{1,0:T(8,128)}, f32[16,8192]{1,0:T(8,128)}, f32[1,8192]{1,0:T(1,128)}) custom-call(f32[1,8192]{1,0:T(1,128)S(1)} %bitcast.8, f32[8,1024]{1,0:T(8,128)S(1)} %slice_add_fusion.48.cs_ref, f32[8,1024]{1,0:T(8,128)S(1)} %slice.468.csgot_ref, f32[320,256]{1,0:T(8,128)S(1)} %add.177.mine_ref, ...), custom_call_target="tpu_custom_call" | custom-call | tf_op jit(solution)/shard_map/final/pallas_call | solution.py:287
  (33 shorter events, 0.6 us)
Async XLA Ops:
  0.6 0.8 copy-start
  1.4 20.2 %copy-start.1 = (bf16[256,8192]{1,0:T(8,128)(2,1)S(1)}, bf16[256,8192]{1,0:T(8,128)(2,1)}, u32[]{:S(2)}) copy-start(bf16[256,8192]{1,0:T(8,128)(2,1)} %refs_2_.3) | copy-start | bytes 12582916
  1.4 20.2 %copy-start.2 = (bf16[2,64,8192]{2,1,0:T(8,128)(2,1)S(1)}, bf16[2,64,8192]{2,1,0:T(8,128)(2,1)}, u32[]{:S(2)}) copy-start(bf16[2,64,8192]{2,1,0:T(8,128)(2,1)} %param.5) | copy-start | bytes 6291460
  21.6 13.2 %copy-start.3 = (bf16[10,64,256]{2,1,0:T(8,128)(2,1)S(1)}, bf16[10,64,256]{2,1,0:T(8,128)(2,1)}, u32[]{:S(2)}) copy-start(bf16[10,64,256]{2,1,0:T(8,128)(2,1)} %param.4) | copy-start | bytes 983044
  27.3 19.1 %collective-permute-start = (f32[136,1024]{1,0:T(8,128)S(1)}, f32[136,1024]{1,0:T(8,128)S(1)}, u32[]{:S(2)}, u32[]{:S(2)}) collective-permute-start(f32[136,1024]{1,0:T(8,128)S(1)} %get-tuple-element.55), channel_id=1, source_target_pairs={{0,32},{8,40},{16,48},{24,56},{32,0},{40,8},{48,16},{56,24},{64,96... | collective-permute-start | bytes 1671176 | tf_op jit(solution)/shard_map/ppermute | solution.py:331
  28.9 14.5 %collective-permute-start.4 = (f32[128,1024]{1,0:T(8,128)S(1)}, f32[128,1024]{1,0:T(8,128)S(1)}, u32[]{:S(2)}, u32[]{:S(2)}) collective-permute-start(f32[128,1024]{1,0:T(8,128)S(1)} %get-tuple-element.65), channel_id=1, source_target_pairs={{0,96},{8,104},{16,112},{24,120},{32,64},{40,72},{48,80},{56,88},{... | collective-permute-start | bytes 1572872 | tf_op jit(solution)/shard_map/ppermute | solution.py:331
  31.0 15.6 %collective-permute-start.3 = (f32[128,1024]{1,0:T(8,128)S(1)}, f32[128,1024]{1,0:T(8,128)S(1)}, u32[]{:S(2)}, u32[]{:S(2)}) collective-permute-start(f32[128,1024]{1,0:T(8,128)S(1)} %get-tuple-element.64), channel_id=1, source_target_pairs={{0,8},{8,0},{16,24},{24,16},{32,40},{40,32},{48,56},{56,48},{64,72... | collective-permute-start | bytes 1572872 | tf_op jit(solution)/shard_map/ppermute | solution.py:331
  32.5 16.3 %collective-permute-start.2 = (f32[128,1024]{1,0:T(8,128)S(1)}, f32[128,1024]{1,0:T(8,128)S(1)}, u32[]{:S(2)}, u32[]{:S(2)}) collective-permute-start(f32[128,1024]{1,0:T(8,128)S(1)} %get-tuple-element.63), channel_id=1, source_target_pairs={{0,24},{8,16},{16,8},{24,0},{32,56},{40,48},{48,40},{56,32},{64,88... | collective-permute-start | bytes 1572872 | tf_op jit(solution)/shard_map/ppermute | solution.py:331
  40.7 12.6 %collective-permute-start.1 = (f32[128,1024]{1,0:T(8,128)S(1)}, f32[128,1024]{1,0:T(8,128)S(1)}, u32[]{:S(2)}, u32[]{:S(2)}) collective-permute-start(f32[128,1024]{1,0:T(8,128)S(1)} %get-tuple-element.62), channel_id=1, source_target_pairs={{0,32},{8,40},{16,48},{24,56},{32,0},{40,8},{48,16},{56,24},{64,96... | collective-permute-start | bytes 1572872 | tf_op jit(solution)/shard_map/ppermute | solution.py:331
  43.4 16.6 %collective-permute-start.8 = (f32[128,1024]{1,0:T(8,128)S(1)}, f32[128,1024]{1,0:T(8,128)S(1)}, u32[]{:S(2)}, u32[]{:S(2)}) collective-permute-start(f32[128,1024]{1,0:T(8,128)S(1)} %get-tuple-element.72), channel_id=1, source_target_pairs={{0,24},{8,16},{16,8},{24,0},{32,56},{40,48},{48,40},{56,32},{64,88... | collective-permute-start | bytes 1572872 | tf_op jit(solution)/shard_map/ppermute | solution.py:331
  46.4 13.4 %collective-permute-start.9 = (f32[128,1024]{1,0:T(8,128)S(1)}, f32[128,1024]{1,0:T(8,128)S(1)}, u32[]{:S(2)}, u32[]{:S(2)}) collective-permute-start(f32[128,1024]{1,0:T(8,128)S(1)} %get-tuple-element.73), channel_id=1, source_target_pairs={{0,8},{8,0},{16,24},{24,16},{32,40},{40,32},{48,56},{56,48},{64,72... | collective-permute-start | bytes 1572872 | tf_op jit(solution)/shard_map/ppermute | solution.py:331
  46.6 13.3 %collective-permute-start.10 = (f32[128,1024]{1,0:T(8,128)S(1)}, f32[128,1024]{1,0:T(8,128)S(1)}, u32[]{:S(2)}, u32[]{:S(2)}) collective-permute-start(f32[128,1024]{1,0:T(8,128)S(1)} %get-tuple-element.74), channel_id=1, source_target_pairs={{0,96},{8,104},{16,112},{24,120},{32,64},{40,72},{48,80},{56,88},{... | collective-permute-start | bytes 1572872 | tf_op jit(solution)/shard_map/ppermute | solution.py:331
  60.0 11.2 %collective-permute-start.15 = (f32[128,1024]{1,0:T(8,128)S(1)}, f32[128,1024]{1,0:T(8,128)S(1)}, u32[]{:S(2)}, u32[]{:S(2)}) collective-permute-start(f32[128,1024]{1,0:T(8,128)S(1)} %pad_maximum_fusion.1), channel_id=1, source_target_pairs={{0,32},{8,40},{16,48},{24,56},{32,0},{40,8},{48,16},{56,24},{64,96... | collective-permute-start | bytes 1572872 | tf_op jit(solution)/shard_map/ppermute | solution.py:353
  60.2 14.4 %collective-permute-start.17 = (f32[128,1024]{1,0:T(8,128)S(1)}, f32[128,1024]{1,0:T(8,128)S(1)}, u32[]{:S(2)}, u32[]{:S(2)}) collective-permute-start(f32[128,1024]{1,0:T(8,128)S(1)} %pad_maximum_fusion.2), channel_id=1, source_target_pairs={{0,24},{8,16},{16,8},{24,0},{32,56},{40,48},{48,40},{56,32},{64,88... | collective-permute-start | bytes 1572872 | tf_op jit(solution)/shard_map/ppermute | solution.py:353
  61.2 13.3 %collective-permute-start.5 = (f32[136,1024]{1,0:T(8,128)S(1)}, f32[136,1024]{1,0:T(8,128)S(1)}, u32[]{:S(2)}, u32[]{:S(2)}) collective-permute-start(f32[136,1024]{1,0:T(8,128)S(1)} %pad_maximum_fusion), channel_id=1, source_target_pairs={{0,96},{8,104},{16,112},{24,120},{32,64},{40,72},{48,80},{56,88},{... | collective-permute-start | bytes 1671176 | tf_op jit(solution)/shard_map/ppermute | solution.py:353
  63.5 11.0 %collective-permute-start.19 = (f32[128,1024]{1,0:T(8,128)S(1)}, f32[128,1024]{1,0:T(8,128)S(1)}, u32[]{:S(2)}, u32[]{:S(2)}) collective-permute-start(f32[128,1024]{1,0:T(8,128)S(1)} %pad_maximum_fusion.3), channel_id=1, source_target_pairs={{0,8},{8,0},{16,24},{24,16},{32,40},{40,32},{48,56},{56,48},{64,72... | collective-permute-start | bytes 1572872 | tf_op jit(solution)/shard_map/ppermute | solution.py:353
  64.5 1.6 %collective-permute-start.11 = (f32[320,256]{1,0:T(8,128)S(1)}, f32[320,256]{1,0:T(8,128)S(1)}, u32[]{:S(2)}, u32[]{:S(2)}) collective-permute-start(f32[320,256]{1,0:T(8,128)S(1)} %get-tuple-element.78), channel_id=1, source_target_pairs={{0,1},{1,0},{2,3},{3,2},{4,5},{5,4},{6,7},{7,6},{8,9},{9,8},{10,11... | collective-permute-start | bytes 983048 | tf_op jit(solution)/shard_map/ppermute | solution.py:361
  66.2 13.9 %collective-permute-start.12 = (f32[320,256]{1,0:T(8,128)S(1)}, f32[320,256]{1,0:T(8,128)S(1)}, u32[]{:S(2)}, u32[]{:S(2)}) collective-permute-start(f32[320,256]{1,0:T(8,128)S(1)} %add.175), channel_id=1, source_target_pairs={{0,2},{1,3},{2,0},{3,1},{4,6},{5,7},{6,4},{7,5},{8,10},{9,11},{10,... | collective-permute-start | bytes 983048 | tf_op jit(solution)/shard_map/ppermute | solution.py:362
  74.7 7.7 %collective-permute-start.16 = (f32[64,1024]{1,0:T(8,128)S(1)}, f32[64,1024]{1,0:T(8,128)S(1)}, u32[]{:S(2)}, u32[]{:S(2)}) collective-permute-start(f32[64,1024]{1,0:T(8,128)S(1)} %pad_maximum_fusion.5), channel_id=1, source_target_pairs={{0,24},{8,16},{16,8},{24,0},{32,56},{40,48},{48,40},{56,32},{64,88... | collective-permute-start | bytes 786440 | tf_op jit(solution)/shard_map/ppermute | solution.py:353
  76.9 8.5 %collective-permute-start.18 = (f32[64,1024]{1,0:T(8,128)S(1)}, f32[64,1024]{1,0:T(8,128)S(1)}, u32[]{:S(2)}, u32[]{:S(2)}) collective-permute-start(f32[64,1024]{1,0:T(8,128)S(1)} %pad_maximum_fusion.6), channel_id=1, source_target_pairs={{0,32},{8,40},{16,48},{24,56},{32,0},{40,8},{48,16},{56,24},{64,96... | collective-permute-start | bytes 786440 | tf_op jit(solution)/shard_map/ppermute | solution.py:353
  78.2 7.2 %collective-permute-start.6 = (f32[72,1024]{1,0:T(8,128)S(1)}, f32[72,1024]{1,0:T(8,128)S(1)}, u32[]{:S(2)}, u32[]{:S(2)}) collective-permute-start(f32[72,1024]{1,0:T(8,128)S(1)} %pad_maximum_fusion.4), channel_id=1, source_target_pairs={{0,8},{8,0},{16,24},{24,16},{32,40},{40,32},{48,56},{56,48},{64,72... | collective-permute-start | bytes 884744 | tf_op jit(solution)/shard_map/ppermute | solution.py:353
  78.6 9.1 %collective-permute-start.20 = (f32[64,1024]{1,0:T(8,128)S(1)}, f32[64,1024]{1,0:T(8,128)S(1)}, u32[]{:S(2)}, u32[]{:S(2)}) collective-permute-start(f32[64,1024]{1,0:T(8,128)S(1)} %pad_maximum_fusion.7), channel_id=1, source_target_pairs={{0,96},{8,104},{16,112},{24,120},{32,64},{40,72},{48,80},{56,88},{... | collective-permute-start | bytes 786440 | tf_op jit(solution)/shard_map/ppermute | solution.py:353
  80.1 11.8 %collective-permute-start.13 = (f32[320,256]{1,0:T(8,128)S(1)}, f32[320,256]{1,0:T(8,128)S(1)}, u32[]{:S(2)}, u32[]{:S(2)}) collective-permute-start(f32[320,256]{1,0:T(8,128)S(1)} %add.176), channel_id=1, source_target_pairs={{0,6},{1,7},{2,4},{3,5},{4,2},{5,3},{6,0},{7,1},{8,14},{9,15},{10,... | collective-permute-start | bytes 983048 | tf_op jit(solution)/shard_map/ppermute | solution.py:363
  87.7 10.1 %collective-permute-start.22 = (f32[32,1024]{1,0:T(8,128)S(1)}, f32[32,1024]{1,0:T(8,128)S(1)}, u32[]{:S(2)}, u32[]{:S(2)}) collective-permute-start(f32[32,1024]{1,0:T(8,128)S(1)} %pad_maximum_fusion.10), channel_id=1, source_target_pairs={{0,96},{8,104},{16,112},{24,120},{32,64},{40,72},{48,80},{56,88},{... | collective-permute-start | bytes 393224 | tf_op jit(solution)/shard_map/ppermute | solution.py:353
  89.3 5.0 %collective-permute-start.21 = (f32[32,1024]{1,0:T(8,128)S(1)}, f32[32,1024]{1,0:T(8,128)S(1)}, u32[]{:S(2)}, u32[]{:S(2)}) collective-permute-start(f32[32,1024]{1,0:T(8,128)S(1)} %pad_maximum_fusion.9), channel_id=1, source_target_pairs={{0,8},{8,0},{16,24},{24,16},{32,40},{40,32},{48,56},{56,48},{64,72... | collective-permute-start | bytes 393224 | tf_op jit(solution)/shard_map/ppermute | solution.py:353
  91.2 6.6 %collective-permute-start.7 = (f32[40,1024]{1,0:T(8,128)S(1)}, f32[40,1024]{1,0:T(8,128)S(1)}, u32[]{:S(2)}, u32[]{:S(2)}) collective-permute-start(f32[40,1024]{1,0:T(8,128)S(1)} %pad_maximum_fusion.8), channel_id=1, source_target_pairs={{0,24},{8,16},{16,8},{24,0},{32,56},{40,48},{48,40},{56,32},{64,88... | collective-permute-start | bytes 491528 | tf_op jit(solution)/shard_map/ppermute | solution.py:353
  92.0 6.1 %collective-permute-start.14 = (f32[320,256]{1,0:T(8,128)S(1)}, f32[320,256]{1,0:T(8,128)S(1)}, u32[]{:S(2)}, u32[]{:S(2)}) collective-permute-start(f32[320,256]{1,0:T(8,128)S(1)} %add.177.mine_ref), channel_id=1, source_target_pairs={{0,1},{1,0},{2,3},{3,2},{4,5},{5,4},{6,7},{7,6},{8,9},{9,8},{10,11... | collective-permute-start | bytes 983048 | tf_op jit(solution)/shard_map/ppermute | solution.py:364
  92.1 6.0 %collective-permute-start.23 = (f32[32,1024]{1,0:T(8,128)S(1)}, f32[32,1024]{1,0:T(8,128)S(1)}, u32[]{:S(2)}, u32[]{:S(2)}) collective-permute-start(f32[32,1024]{1,0:T(8,128)S(1)} %pad_maximum_fusion.11), channel_id=1, source_target_pairs={{0,32},{8,40},{16,48},{24,56},{32,0},{40,8},{48,16},{56,24},{64,96... | collective-permute-start | bytes 393224 | tf_op jit(solution)/shard_map/ppermute | solution.py:353

commit v3 on v2

--- a/solution.py
+++ b/solution.py
@@ -11,12 +11,12 @@
 F32 = jnp.float32
 BF16 = jnp.bfloat16
 STUDENT_C = 10.0 * math.log2(math.e)
-TEACHER_C = 25.0
+TEACHER_C = 25.0 * math.log2(math.e)
 EPS = 1e-06
 PARTS = 4
 CALLS = 2
 STAT_TILE = 1024
-STAT_SUB = 256
+STAT_SUB = 1024
 SUB = 512
 
 _KEEP = {0: (0, 3), 1: (0, 1), 2: (0, 3), 3: (0, 1)}
@@ -84,14 +84,16 @@
                 part = lane if part is None else part + lane
         sacc[...] += part
         t = tbuf[:, cols].astype(F32)
-        colsum_ref[pl.ds(n, 1), :] = jnp.sum(t, axis=0, keepdims=True)
+        ones = jnp.ones((8, tbuf.shape[0]), BF16)
+        sums = jnp.dot(ones, tbuf[:, cols], preferred_element_type=F32)
+        colsum_ref[pl.ds(n, 1), :] = sums[:1]
         diff = t - c_ref[:, cols]
         lanes = [diff[:, m * 128 : (m + 1) * 128] for m in range(STAT_TILE // 128)]
         old = macc[...]
         top = functools.reduce(jnp.maximum, lanes, old)
-        total = tacc[...] * jnp.exp((old - top) * TEACHER_C)
+        total = tacc[...] * jnp.exp2((old - top) * TEACHER_C)
         for lane in lanes:
-            total += jnp.exp((lane - top) * TEACHER_C)
+            total += jnp.exp2((lane - top) * TEACHER_C)
         macc[...] = top
         tacc[...] = total
 
@@ -102,7 +104,7 @@
     best = jnp.max(tops, axis=0, keepdims=True)
     stat_ref[5:6, :] = best
     stat_ref[6:7, :] = jnp.sum(
-        tacc[...].T * jnp.exp((tops - best) * TEACHER_C), axis=0, keepdims=True
+        tacc[...].T * jnp.exp2((tops - best) * TEACHER_C), axis=0, keepdims=True
     )
 
 
@@ -124,7 +126,7 @@
         stat = stat_ref[...]
         sums = jnp.sum(stat, axis=0)
         top = jnp.max(stat[:, 5:6, :], axis=0)
-        ttot = jnp.sum(stat[:, 6:7, :] * jnp.exp((stat[:, 5:6, :] - top) * TEACHER_C), axis=0)
+        ttot = jnp.sum(stat[:, 6:7, :] * jnp.exp2((stat[:, 5:6, :] - top) * TEACHER_C), axis=0)
         packed = jnp.concatenate([sums[0:5], top, ttot, jnp.zeros((121, 128), F32)], axis=0).T
         for r in range(5):
             arow[r * 128 : (r + 1) * 128, :] = jnp.broadcast_to(
@@ -148,7 +150,7 @@
             wb = (dir_ref[:, mine].astype(F32) * inv).astype(BF16)
             s = jnp.dot(ub, wb, preferred_element_type=F32)
             diff = t_ref[:, mine].astype(F32) - c_ref[:, mine]
-            t = jnp.exp((diff - wide(mrow[...])) * TEACHER_C) * wide(brow[...])
+            t = jnp.exp2((diff - wide(mrow[...])) * TEACHER_C) * wide(brow[...])
             t0, t1 = t[:img], t[img:]
             both = t0 + t1
             rounded = []
@@ -340,8 +342,9 @@
             before = block
             got[part][call] = block[:128]
             if call == 0 and part == 0:
+                fsend, _ = lax.optimization_barrier((fsend, block))
+            if call == 0 and part == 0:
                 cs = cs + block[128:]
-    fsend, _ = lax.optimization_barrier((fsend, before))
     keeps = [[keeps[call][part] for call in range(CALLS)] for part in range(PARTS)]
     for n in (1, 2, 3):
         size = 128 >> n

time: 100 us -> 99.4 us (level)
  starting transfers between devices: 28.6 us -> 25.4 us
  waiting for transfers between devices: 34.5 us -> 37.7 us
    ppermute x12, starting transfers between devices: 13.3 us -> 10.4 us  [on_device(): block = lax.ppermute(jnp.concatenate(out, axis=0), 'batch', ORDER[part][n])]
    ppermute x8, waiting for transfers between devices: 12.9 us -> 15.8 us  [on_device(): lax.ppermute(send[p], 'batch', ORDER[p][0])]
  transfers between devices with their start and end apart: 24 -> 24, of which waited for: 12 -> 15; matrix products, arithmetic and copies ran while one was open for 1% -> 1% of each run, Pallas kernels for 6% -> 6%
where the time goes in v3:
time: 99.4 us; the launch traced here: 98.6 us
  waiting for transfers between devices  37.7 us (38%)
  starting transfers between devices  25.4 us (26%)
  Pallas kernels  21.7 us (22%)
  blocking collectives  10.6 us (11%)
  other arithmetic  1.45 us (1%)
    ppermute x12, waiting for transfers between devices, on_device(): block = lax.ppermute(jnp.concatenate(out, axis=0), 'batch', ORDER[part][n])  20.3 us
    ppermute x8, waiting for transfers between devices, on_device(): lax.ppermute(send[p], 'batch', ORDER[p][0])  15.8 us
    ppermute x8, starting transfers between devices, on_device(): lax.ppermute(send[p], 'batch', ORDER[p][0])  13 us
    pallas_call x2, Pallas kernels, weight_call(): pl.pallas_call(functools.partial(weight_kernel, images, call), in_specs=[...  11.7 us
    all_to_all x1, blocking collectives, on_device(): stats = lax.all_to_all(jnp.broadcast_to(stat, (8, 8, 128)), 'proto', 0, 0)  10.6 us
    ppermute x12, starting transfers between devices, on_device(): block = lax.ppermute(jnp.concatenate(out, axis=0), 'batch', ORDER[part][n])  10.4 us
    pallas_call x1, Pallas kernels, stats_call(): pl.pallas_call(stats_kernel, in_specs=[IN_VMEM, IN_VMEM] + [pl.BlockSpec(...  8.89 us
  transfers between devices with their start and end apart: 24, of which 15 were waited for; matrix products, arithmetic and copies ran while one was open for 1% of the time, Pallas kernels for 6%

profile of v3, /device:TPU:0, one launch (start us, length us, event | category | flops | bytes accessed | tf_op | source)
XLA Modules:
  0.0 98.6 jit_solution(9563516505812956263)
XLA Ops:
  0.6 0.7 copy-done
  1.4 8.9 %stats.1 = (bf16[640,256]{1,0:T(8,128)(2,1)S(1)}, bf16[256,640]{1,0:T(8,128)(2,1)S(1)}, f32[1,8192]{1,0:T(1,128)S(1)}, f32[8,1024]{1,0:T(8,128)S(1)}, f32[8,128]{1,0:T(8,128)S(1)}) custom-call(bf16[640,256]{1,0:T(8,128)(2,1)} %bitcast.12, f32[1,8192]{1,0:T(1,128)S(1)} %bitcast.5, bf16[256,8192]{1,0:T(8,128)(2,1)} %refs_2_.3, bf16[128,8192]{1,0:T(8,128)(2,1)} %bitcast.9), custom_call_target="tpu_custom_call" | custom-call | flops 2684354560 | bytes 6291456 | tf_op jit(solution)/shard_map/stats/pallas_call | solution.py:226
  10.3 10.6 %all_to_all.5.refs_6_ = f32[8,8,128]{2,1,0:T(8,128)S(1)} all-to-all(f32[8,8,128]{2,1,0:T(8,128)S(1)} %broadcast_in_dim.3), channel_id=1, replica_groups=mesh['batch'=16,'proto'=8] {'proto'}, dimensions={0} | all-to-all | bytes 65536 | tf_op jit(solution)/shard_map/all_to_all | solution.py:324
  21.0 5.7 %weights.2 = (f32[128,1024]{1,0:T(8,128)S(1)}, f32[128,1024]{1,0:T(8,128)S(1)}, f32[128,1024]{1,0:T(8,128)S(1)}, f32[128,1024]{1,0:T(8,128)S(1)}, f32[136,1024]{...) custom-call(bf16[640,256]{1,0:T(8,128)(2,1)S(1)} %get-tuple-element., ...), custom_call_target="tpu_custom_call" | custom-call | flops 4026531840 | bytes 7340032 | tf_op jit(solution)/shard_map/weights/pallas_call | solution.py:268
  26.7 3.1 %collective-permute-start.2 = (f32[128,1024]{1,0:T(8,128)S(1)}, f32[128,1024]{1,0:T(8,128)S(1)}, u32[]{:S(2)}, u32[]{:S(2)}) collective-permute-start(f32[128,1024]{1,0:T(8,128)S(1)} %get-tuple-element.63), channel_id=1, source_target_pairs={{0,24},{8,16},{16,8},{24,0},{32,56},{40,48},{48,40},{56,32},{64,88... | collective-permute-start | bytes 1572872 | tf_op jit(solution)/shard_map/ppermute | solution.py:333
  29.8 0.2 collective-permute-start.3
  29.9 2.7 %collective-permute-start.4 = (f32[128,1024]{1,0:T(8,128)S(1)}, f32[128,1024]{1,0:T(8,128)S(1)}, u32[]{:S(2)}, u32[]{:S(2)}) collective-permute-start(f32[128,1024]{1,0:T(8,128)S(1)} %get-tuple-element.65), channel_id=1, source_target_pairs={{0,96},{8,104},{16,112},{24,120},{32,64},{40,72},{48,80},{56,88},{... | collective-permute-start | bytes 1572872 | tf_op jit(solution)/shard_map/ppermute | solution.py:333
  32.7 0.2 collective-permute-start
  32.9 6.0 %weights.3 = (f32[128,1024]{1,0:T(8,128)S(1)}, f32[128,1024]{1,0:T(8,128)S(1)}, f32[128,1024]{1,0:T(8,128)S(1)}, f32[128,1024]{1,0:T(8,128)S(1)}, f32[128,1024]{...) custom-call(bf16[640,256]{1,0:T(8,128)(2,1)S(1)} %get-tuple-element., ...), custom_call_target="tpu_custom_call" | custom-call | flops 4026531840 | bytes 7340032 | tf_op jit(solution)/shard_map/weights/pallas_call | solution.py:268
  38.9 1.9 %collective-permute-start.1 = (f32[128,1024]{1,0:T(8,128)S(1)}, f32[128,1024]{1,0:T(8,128)S(1)}, u32[]{:S(2)}, u32[]{:S(2)}) collective-permute-start(f32[128,1024]{1,0:T(8,128)S(1)} %get-tuple-element.62), channel_id=1, source_target_pairs={{0,32},{8,40},{16,48},{24,56},{32,0},{40,8},{48,16},{56,24},{64,96... | collective-permute-start | bytes 1572872 | tf_op jit(solution)/shard_map/ppermute | solution.py:333
  40.8 3.5 %collective-permute-done.4 = f32[128,1024]{1,0:T(8,128)S(1)} collective-permute-done((f32[128,1024]{1,0:T(8,128)S(1)}, f32[128,1024]{1,0:T(8,128)S(1)}, u32[]{:S(2)}, u32[]{:S(2)}) %collective-permute-start.4) | collective-permute-done | bytes 524320 | tf_op jit(solution)/shard_map/ppermute | solution.py:333
  44.3 2.7 %collective-permute-start.12 = (f32[128,1024]{1,0:T(8,128)S(1)}, f32[128,1024]{1,0:T(8,128)S(1)}, u32[]{:S(2)}, u32[]{:S(2)}) collective-permute-start(f32[128,1024]{1,0:T(8,128)S(1)} %get-tuple-element.75), channel_id=1, source_target_pairs={{0,96},{8,104},{16,112},{24,120},{32,64},{40,72},{48,80},{56,88},{... | collective-permute-start | bytes 1572872 | tf_op jit(solution)/shard_map/ppermute | solution.py:333
  47.1 1.2 %collective-permute-done = f32[136,1024]{1,0:T(8,128)S(1)} collective-permute-done((f32[136,1024]{1,0:T(8,128)S(1)}, f32[136,1024]{1,0:T(8,128)S(1)}, u32[]{:S(2)}, u32[]{:S(2)}) %collective-permute-start) | collective-permute-done | bytes 557088 | tf_op jit(solution)/shard_map/ppermute | solution.py:333
  48.2 1.9 %collective-permute-start.15 = (f32[128,1024]{1,0:T(8,128)S(1)}, f32[128,1024]{1,0:T(8,128)S(1)}, u32[]{:S(2)}, u32[]{:S(2)}) collective-permute-start(f32[128,1024]{1,0:T(8,128)S(1)} %get-tuple-element.81), channel_id=1, source_target_pairs={{0,8},{8,0},{16,24},{24,16},{32,40},{40,32},{48,56},{56,48},{64,72... | collective-permute-start | bytes 1572872 | tf_op jit(solution)/shard_map/ppermute | solution.py:333
  50.1 0.0 collective-permute-done.3
  50.1 0.2 collective-permute-start.18
  50.3 0.0 collective-permute-done.2
  50.4 7.2 %collective-permute-done.1 = f32[128,1024]{1,0:T(8,128)S(1)} collective-permute-done((f32[128,1024]{1,0:T(8,128)S(1)}, f32[128,1024]{1,0:T(8,128)S(1)}, u32[]{:S(2)}, u32[]{:S(2)}) %collective-permute-start.1) | collective-permute-done | bytes 524320 | tf_op jit(solution)/shard_map/ppermute | solution.py:333
  57.5 0.1 slice_add_fusion.12
  57.6 0.2 collective-permute-done.12
  57.8 0.1 slice_add_fusion.10
  57.9 0.2 collective-permute-start.13
  58.1 0.1 slice_add_fusion.8
  58.2 0.9 collective-permute-done.15
  59.0 0.1 slice_add_fusion.6
  59.1 0.9 collective-permute-start.16
  60.0 0.1 slice_add_fusion.4
  60.1 0.1 slice_add_fusion.14
  60.2 2.8 %collective-permute-done.18 = f32[128,1024]{1,0:T(8,128)S(1)} collective-permute-done((f32[128,1024]{1,0:T(8,128)S(1)}, f32[128,1024]{1,0:T(8,128)S(1)}, u32[]{:S(2)}, u32[]{:S(2)}) %collective-permute-start.18) | collective-permute-done | bytes 524320 | tf_op jit(solution)/shard_map/ppermute | solution.py:333
  63.0 0.1 slice_add_fusion
  63.1 0.1 collective-permute-start.5
  63.2 0.1 slice_add_fusion.2
  63.4 0.1 collective-permute-start.19
  63.5 0.1 collective-permute-start.8
  63.5 1.6 %collective-permute-done.8 = f32[320,256]{1,0:T(8,128)S(1)} collective-permute-done((f32[320,256]{1,0:T(8,128)S(1)}, f32[320,256]{1,0:T(8,128)S(1)}, u32[]{:S(2)}, u32[]{:S(2)}) %collective-permute-start.8) | collective-permute-done | bytes 327712 | tf_op jit(solution)/shard_map/ppermute | solution.py:364
  65.2 0.7 collective-permute-start.9
  65.9 3.9 %collective-permute-done.13 = f32[128,1024]{1,0:T(8,128)S(1)} collective-permute-done((f32[128,1024]{1,0:T(8,128)S(1)}, f32[128,1024]{1,0:T(8,128)S(1)}, u32[]{:S(2)}, u32[]{:S(2)}) %collective-permute-start.13) | collective-permute-done | bytes 524320 | tf_op jit(solution)/shard_map/ppermute | solution.py:356
  69.8 4.2 %collective-permute-done.5 = f32[136,1024]{1,0:T(8,128)S(1)} collective-permute-done((f32[136,1024]{1,0:T(8,128)S(1)}, f32[136,1024]{1,0:T(8,128)S(1)}, u32[]{:S(2)}, u32[]{:S(2)}) %collective-permute-start.5) | collective-permute-done | bytes 557088 | tf_op jit(solution)/shard_map/ppermute | solution.py:356
  74.0 0.1 slice_add_fusion.24
  74.1 1.7 %collective-permute-start.14 = (f32[64,1024]{1,0:T(8,128)S(1)}, f32[64,1024]{1,0:T(8,128)S(1)}, u32[]{:S(2)}, u32[]{:S(2)}) collective-permute-start(f32[64,1024]{1,0:T(8,128)S(1)} %pad_maximum_fusion.5), channel_id=1, source_target_pairs={{0,24},{8,16},{16,8},{24,0},{32,56},{40,48},{48,40},{56,32},{64,88... | collective-permute-start | bytes 786440 | tf_op jit(solution)/shard_map/ppermute | solution.py:356
  75.8 0.1 slice_add_fusion.20
  75.9 1.2 %collective-permute-start.17 = (f32[64,1024]{1,0:T(8,128)S(1)}, f32[64,1024]{1,0:T(8,128)S(1)}, u32[]{:S(2)}, u32[]{:S(2)}) collective-permute-start(f32[64,1024]{1,0:T(8,128)S(1)} %pad_maximum_fusion.6), channel_id=1, source_target_pairs={{0,32},{8,40},{16,48},{24,56},{32,0},{40,8},{48,16},{56,24},{64,96... | collective-permute-start | bytes 786440 | tf_op jit(solution)/shard_map/ppermute | solution.py:356
  77.1 0.1 slice_add_fusion.29
  77.2 0.4 collective-permute-start.6
  77.6 0.1 slice_add_fusion.16
  77.7 1.5 %collective-permute-start.20 = (f32[64,1024]{1,0:T(8,128)S(1)}, f32[64,1024]{1,0:T(8,128)S(1)}, u32[]{:S(2)}, u32[]{:S(2)}) collective-permute-start(f32[64,1024]{1,0:T(8,128)S(1)} %pad_maximum_fusion.7), channel_id=1, source_target_pairs={{0,96},{8,104},{16,112},{24,120},{32,64},{40,72},{48,80},{56,88},{... | collective-permute-start | bytes 786440 | tf_op jit(solution)/shard_map/ppermute | solution.py:356
  79.1 0.0 collective-permute-done.9
  79.2 1.2 %collective-permute-start.10 = (f32[320,256]{1,0:T(8,128)S(1)}, f32[320,256]{1,0:T(8,128)S(1)}, u32[]{:S(2)}, u32[]{:S(2)}) collective-permute-start(f32[320,256]{1,0:T(8,128)S(1)} %add.176), channel_id=1, source_target_pairs={{0,6},{1,7},{2,4},{3,5},{4,2},{5,3},{6,0},{7,1},{8,14},{9,15},{10,... | collective-permute-start | bytes 983048 | tf_op jit(solution)/shard_map/ppermute | solution.py:366
  80.4 1.3 %collective-permute-done.14 = f32[64,1024]{1,0:T(8,128)S(1)} collective-permute-done((f32[64,1024]{1,0:T(8,128)S(1)}, f32[64,1024]{1,0:T(8,128)S(1)}, u32[]{:S(2)}, u32[]{:S(2)}) %collective-permute-start.14) | collective-permute-done | bytes 262176 | tf_op jit(solution)/shard_map/ppermute | solution.py:356
  81.7 2.5 %collective-permute-done.6 = f32[72,1024]{1,0:T(8,128)S(1)} collective-permute-done((f32[72,1024]{1,0:T(8,128)S(1)}, f32[72,1024]{1,0:T(8,128)S(1)}, u32[]{:S(2)}, u32[]{:S(2)}) %collective-permute-start.6) | collective-permute-done | bytes 294944 | tf_op jit(solution)/shard_map/ppermute | solution.py:356
  84.3 0.0 collective-permute-done.17
  84.3 2.5 %collective-permute-done.20 = f32[64,1024]{1,0:T(8,128)S(1)} collective-permute-done((f32[64,1024]{1,0:T(8,128)S(1)}, f32[64,1024]{1,0:T(8,128)S(1)}, u32[]{:S(2)}, u32[]{:S(2)}) %collective-permute-start.20) | collective-permute-done | bytes 262176 | tf_op jit(solution)/shard_map/ppermute | solution.py:356
  86.8 1.5 %collective-permute-start.22 = (f32[32,1024]{1,0:T(8,128)S(1)}, f32[32,1024]{1,0:T(8,128)S(1)}, u32[]{:S(2)}, u32[]{:S(2)}) collective-permute-start(f32[32,1024]{1,0:T(8,128)S(1)} %pad_maximum_fusion.10), channel_id=1, source_target_pairs={{0,96},{8,104},{16,112},{24,120},{32,64},{40,72},{48,80},{56,88},{... | collective-permute-start | bytes 393224 | tf_op jit(solution)/shard_map/ppermute | solution.py:356
  88.3 1.8 %collective-permute-start.21 = (f32[32,1024]{1,0:T(8,128)S(1)}, f32[32,1024]{1,0:T(8,128)S(1)}, u32[]{:S(2)}, u32[]{:S(2)}) collective-permute-start(f32[32,1024]{1,0:T(8,128)S(1)} %pad_maximum_fusion.9), channel_id=1, source_target_pairs={{0,8},{8,0},{16,24},{24,16},{32,40},{40,32},{48,56},{56,48},{64,72... | collective-permute-start | bytes 393224 | tf_op jit(solution)/shard_map/ppermute | solution.py:356
  90.2 1.0 %collective-permute-start.7 = (f32[40,1024]{1,0:T(8,128)S(1)}, f32[40,1024]{1,0:T(8,128)S(1)}, u32[]{:S(2)}, u32[]{:S(2)}) collective-permute-start(f32[40,1024]{1,0:T(8,128)S(1)} %pad_maximum_fusion.8), channel_id=1, source_target_pairs={{0,24},{8,16},{16,8},{24,0},{32,56},{40,48},{48,40},{56,32},{64,88... | collective-permute-start | bytes 491528 | tf_op jit(solution)/shard_map/ppermute | solution.py:356
  91.3 0.0 collective-permute-done.10
  91.3 0.1 collective-permute-start.11
  91.5 0.1 collective-permute-start.23
  91.6 1.8 %collective-permute-done.21.refs_9_ = f32[32,1024]{1,0:T(8,128)S(1)} collective-permute-done((f32[32,1024]{1,0:T(8,128)S(1)}, f32[32,1024]{1,0:T(8,128)S(1)}, u32[]{:S(2)}, u32[]{:S(2)}) %collective-permute-start.21) | collective-permute-done | bytes 131104 | tf_op jit(solution)/shard_map/ppermute | solution.py:356
  93.4 3.5 %collective-permute-done.7.refs_8_ = f32[40,1024]{1,0:T(8,128)S(1)} collective-permute-done((f32[40,1024]{1,0:T(8,128)S(1)}, f32[40,1024]{1,0:T(8,128)S(1)}, u32[]{:S(2)}, u32[]{:S(2)}) %collective-permute-start.7) | collective-permute-done | bytes 163872 | tf_op jit(solution)/shard_map/ppermute | solution.py:356
  96.8 0.0 collective-permute-done.22.refs_10_
  96.8 0.6 collective-permute-done.23.refs_11_
  97.4 0.0 collective-permute-done.11.other_ref
  97.4 1.1 %final.1 = (f32[640,256]{1,0:T(8,128)}, f32[16,8192]{1,0:T(8,128)}, f32[1,8192]{1,0:T(1,128)}) custom-call(f32[1,8192]{1,0:T(1,128)S(1)} %bitcast.8, f32[8,1024]{1,0:T(8,128)S(1)} %slice_add_fusion.48.cs_ref, f32[8,1024]{1,0:T(8,128)S(1)} %slice.468.csgot_ref, f32[320,256]{1,0:T(8,128)S(1)} %add.177.mine_ref, ...), custom_call_target="tpu_custom_call" | custom-call | tf_op jit(solution)/shard_map/final/pallas_call | solution.py:289
  (33 shorter events, 0.6 us)
Async XLA Ops:
  0.6 0.8 copy-start
  1.4 19.6 %copy-start.1 = (bf16[256,8192]{1,0:T(8,128)(2,1)S(1)}, bf16[256,8192]{1,0:T(8,128)(2,1)}, u32[]{:S(2)}) copy-start(bf16[256,8192]{1,0:T(8,128)(2,1)} %refs_2_.3) | copy-start | bytes 12582916
  1.4 19.6 %copy-start.2 = (bf16[2,64,8192]{2,1,0:T(8,128)(2,1)S(1)}, bf16[2,64,8192]{2,1,0:T(8,128)(2,1)}, u32[]{:S(2)}) copy-start(bf16[2,64,8192]{2,1,0:T(8,128)(2,1)} %param.5) | copy-start | bytes 6291460
  20.9 12.0 %copy-start.3 = (bf16[10,64,256]{2,1,0:T(8,128)(2,1)S(1)}, bf16[10,64,256]{2,1,0:T(8,128)(2,1)}, u32[]{:S(2)}) copy-start(bf16[10,64,256]{2,1,0:T(8,128)(2,1)} %param.4) | copy-start | bytes 983044
  26.7 23.7 %collective-permute-start.2 = (f32[128,1024]{1,0:T(8,128)S(1)}, f32[128,1024]{1,0:T(8,128)S(1)}, u32[]{:S(2)}, u32[]{:S(2)}) collective-permute-start(f32[128,1024]{1,0:T(8,128)S(1)} %get-tuple-element.63), channel_id=1, source_target_pairs={{0,24},{8,16},{16,8},{24,0},{32,56},{40,48},{48,40},{56,32},{64,88... | collective-permute-start | bytes 1572872 | tf_op jit(solution)/shard_map/ppermute | solution.py:333
  29.8 20.3 %collective-permute-start.3 = (f32[128,1024]{1,0:T(8,128)S(1)}, f32[128,1024]{1,0:T(8,128)S(1)}, u32[]{:S(2)}, u32[]{:S(2)}) collective-permute-start(f32[128,1024]{1,0:T(8,128)S(1)} %get-tuple-element.64), channel_id=1, source_target_pairs={{0,8},{8,0},{16,24},{24,16},{32,40},{40,32},{48,56},{56,48},{64,72... | collective-permute-start | bytes 1572872 | tf_op jit(solution)/shard_map/ppermute | solution.py:333
  29.9 14.4 %collective-permute-start.4 = (f32[128,1024]{1,0:T(8,128)S(1)}, f32[128,1024]{1,0:T(8,128)S(1)}, u32[]{:S(2)}, u32[]{:S(2)}) collective-permute-start(f32[128,1024]{1,0:T(8,128)S(1)} %get-tuple-element.65), channel_id=1, source_target_pairs={{0,96},{8,104},{16,112},{24,120},{32,64},{40,72},{48,80},{56,88},{... | collective-permute-start | bytes 1572872 | tf_op jit(solution)/shard_map/ppermute | solution.py:333
  32.7 15.6 %collective-permute-start = (f32[136,1024]{1,0:T(8,128)S(1)}, f32[136,1024]{1,0:T(8,128)S(1)}, u32[]{:S(2)}, u32[]{:S(2)}) collective-permute-start(f32[136,1024]{1,0:T(8,128)S(1)} %get-tuple-element.55), channel_id=1, source_target_pairs={{0,32},{8,40},{16,48},{24,56},{32,0},{40,8},{48,16},{56,24},{64,96... | collective-permute-start | bytes 1671176 | tf_op jit(solution)/shard_map/ppermute | solution.py:333
  38.9 18.6 %collective-permute-start.1 = (f32[128,1024]{1,0:T(8,128)S(1)}, f32[128,1024]{1,0:T(8,128)S(1)}, u32[]{:S(2)}, u32[]{:S(2)}) collective-permute-start(f32[128,1024]{1,0:T(8,128)S(1)} %get-tuple-element.62), channel_id=1, source_target_pairs={{0,32},{8,40},{16,48},{24,56},{32,0},{40,8},{48,16},{56,24},{64,96... | collective-permute-start | bytes 1572872 | tf_op jit(solution)/shard_map/ppermute | solution.py:333
  44.3 13.5 %collective-permute-start.12 = (f32[128,1024]{1,0:T(8,128)S(1)}, f32[128,1024]{1,0:T(8,128)S(1)}, u32[]{:S(2)}, u32[]{:S(2)}) collective-permute-start(f32[128,1024]{1,0:T(8,128)S(1)} %get-tuple-element.75), channel_id=1, source_target_pairs={{0,96},{8,104},{16,112},{24,120},{32,64},{40,72},{48,80},{56,88},{... | collective-permute-start | bytes 1572872 | tf_op jit(solution)/shard_map/ppermute | solution.py:333
  48.2 10.8 %collective-permute-start.15 = (f32[128,1024]{1,0:T(8,128)S(1)}, f32[128,1024]{1,0:T(8,128)S(1)}, u32[]{:S(2)}, u32[]{:S(2)}) collective-permute-start(f32[128,1024]{1,0:T(8,128)S(1)} %get-tuple-element.81), channel_id=1, source_target_pairs={{0,8},{8,0},{16,24},{24,16},{32,40},{40,32},{48,56},{56,48},{64,72... | collective-permute-start | bytes 1572872 | tf_op jit(solution)/shard_map/ppermute | solution.py:333
  50.1 12.9 %collective-permute-start.18 = (f32[128,1024]{1,0:T(8,128)S(1)}, f32[128,1024]{1,0:T(8,128)S(1)}, u32[]{:S(2)}, u32[]{:S(2)}) collective-permute-start(f32[128,1024]{1,0:T(8,128)S(1)} %get-tuple-element.87), channel_id=1, source_target_pairs={{0,24},{8,16},{16,8},{24,0},{32,56},{40,48},{48,40},{56,32},{64,88... | collective-permute-start | bytes 1572872 | tf_op jit(solution)/shard_map/ppermute | solution.py:333
  57.9 11.9 %collective-permute-start.13 = (f32[128,1024]{1,0:T(8,128)S(1)}, f32[128,1024]{1,0:T(8,128)S(1)}, u32[]{:S(2)}, u32[]{:S(2)}) collective-permute-start(f32[128,1024]{1,0:T(8,128)S(1)} %pad_maximum_fusion.1), channel_id=1, source_target_pairs={{0,32},{8,40},{16,48},{24,56},{32,0},{40,8},{48,16},{56,24},{64,96... | collective-permute-start | bytes 1572872 | tf_op jit(solution)/shard_map/ppermute | solution.py:356
  59.1 14.8 %collective-permute-start.16 = (f32[128,1024]{1,0:T(8,128)S(1)}, f32[128,1024]{1,0:T(8,128)S(1)}, u32[]{:S(2)}, u32[]{:S(2)}) collective-permute-start(f32[128,1024]{1,0:T(8,128)S(1)} %pad_maximum_fusion.2), channel_id=1, source_target_pairs={{0,24},{8,16},{16,8},{24,0},{32,56},{40,48},{48,40},{56,32},{64,88... | collective-permute-start | bytes 1572872 | tf_op jit(solution)/shard_map/ppermute | solution.py:356
  63.1 10.8 %collective-permute-start.5 = (f32[136,1024]{1,0:T(8,128)S(1)}, f32[136,1024]{1,0:T(8,128)S(1)}, u32[]{:S(2)}, u32[]{:S(2)}) collective-permute-start(f32[136,1024]{1,0:T(8,128)S(1)} %pad_maximum_fusion), channel_id=1, source_target_pairs={{0,96},{8,104},{16,112},{24,120},{32,64},{40,72},{48,80},{56,88},{... | collective-permute-start | bytes 1671176 | tf_op jit(solution)/shard_map/ppermute | solution.py:356
  63.4 10.6 %collective-permute-start.19 = (f32[128,1024]{1,0:T(8,128)S(1)}, f32[128,1024]{1,0:T(8,128)S(1)}, u32[]{:S(2)}, u32[]{:S(2)}) collective-permute-start(f32[128,1024]{1,0:T(8,128)S(1)} %pad_maximum_fusion.3), channel_id=1, source_target_pairs={{0,8},{8,0},{16,24},{24,16},{32,40},{40,32},{48,56},{56,48},{64,72... | collective-permute-start | bytes 1572872 | tf_op jit(solution)/shard_map/ppermute | solution.py:356
  63.5 1.7 %collective-permute-start.8 = (f32[320,256]{1,0:T(8,128)S(1)}, f32[320,256]{1,0:T(8,128)S(1)}, u32[]{:S(2)}, u32[]{:S(2)}) collective-permute-start(f32[320,256]{1,0:T(8,128)S(1)} %get-tuple-element.72), channel_id=1, source_target_pairs={{0,1},{1,0},{2,3},{3,2},{4,5},{5,4},{6,7},{7,6},{8,9},{9,8},{10,11... | collective-permute-start | bytes 983048 | tf_op jit(solution)/shard_map/ppermute | solution.py:364
  65.2 13.9 %collective-permute-start.9 = (f32[320,256]{1,0:T(8,128)S(1)}, f32[320,256]{1,0:T(8,128)S(1)}, u32[]{:S(2)}, u32[]{:S(2)}) collective-permute-start(f32[320,256]{1,0:T(8,128)S(1)} %add.175), channel_id=1, source_target_pairs={{0,2},{1,3},{2,0},{3,1},{4,6},{5,7},{6,4},{7,5},{8,10},{9,11},{10,... | collective-permute-start | bytes 983048 | tf_op jit(solution)/shard_map/ppermute | solution.py:365
  74.1 7.7 %collective-permute-start.14 = (f32[64,1024]{1,0:T(8,128)S(1)}, f32[64,1024]{1,0:T(8,128)S(1)}, u32[]{:S(2)}, u32[]{:S(2)}) collective-permute-start(f32[64,1024]{1,0:T(8,128)S(1)} %pad_maximum_fusion.5), channel_id=1, source_target_pairs={{0,24},{8,16},{16,8},{24,0},{32,56},{40,48},{48,40},{56,32},{64,88... | collective-permute-start | bytes 786440 | tf_op jit(solution)/shard_map/ppermute | solution.py:356
  75.9 8.4 %collective-permute-start.17 = (f32[64,1024]{1,0:T(8,128)S(1)}, f32[64,1024]{1,0:T(8,128)S(1)}, u32[]{:S(2)}, u32[]{:S(2)}) collective-permute-start(f32[64,1024]{1,0:T(8,128)S(1)} %pad_maximum_fusion.6), channel_id=1, source_target_pairs={{0,32},{8,40},{16,48},{24,56},{32,0},{40,8},{48,16},{56,24},{64,96... | collective-permute-start | bytes 786440 | tf_op jit(solution)/shard_map/ppermute | solution.py:356
  77.2 7.0 %collective-permute-start.6 = (f32[72,1024]{1,0:T(8,128)S(1)}, f32[72,1024]{1,0:T(8,128)S(1)}, u32[]{:S(2)}, u32[]{:S(2)}) collective-permute-start(f32[72,1024]{1,0:T(8,128)S(1)} %pad_maximum_fusion.4), channel_id=1, source_target_pairs={{0,8},{8,0},{16,24},{24,16},{32,40},{40,32},{48,56},{56,48},{64,72... | collective-permute-start | bytes 884744 | tf_op jit(solution)/shard_map/ppermute | solution.py:356
  77.7 9.1 %collective-permute-start.20 = (f32[64,1024]{1,0:T(8,128)S(1)}, f32[64,1024]{1,0:T(8,128)S(1)}, u32[]{:S(2)}, u32[]{:S(2)}) collective-permute-start(f32[64,1024]{1,0:T(8,128)S(1)} %pad_maximum_fusion.7), channel_id=1, source_target_pairs={{0,96},{8,104},{16,112},{24,120},{32,64},{40,72},{48,80},{56,88},{... | collective-permute-start | bytes 786440 | tf_op jit(solution)/shard_map/ppermute | solution.py:356
  79.2 12.1 %collective-permute-start.10 = (f32[320,256]{1,0:T(8,128)S(1)}, f32[320,256]{1,0:T(8,128)S(1)}, u32[]{:S(2)}, u32[]{:S(2)}) collective-permute-start(f32[320,256]{1,0:T(8,128)S(1)} %add.176), channel_id=1, source_target_pairs={{0,6},{1,7},{2,4},{3,5},{4,2},{5,3},{6,0},{7,1},{8,14},{9,15},{10,... | collective-permute-start | bytes 983048 | tf_op jit(solution)/shard_map/ppermute | solution.py:366
  86.8 10.0 %collective-permute-start.22 = (f32[32,1024]{1,0:T(8,128)S(1)}, f32[32,1024]{1,0:T(8,128)S(1)}, u32[]{:S(2)}, u32[]{:S(2)}) collective-permute-start(f32[32,1024]{1,0:T(8,128)S(1)} %pad_maximum_fusion.10), channel_id=1, source_target_pairs={{0,96},{8,104},{16,112},{24,120},{32,64},{40,72},{48,80},{56,88},{... | collective-permute-start | bytes 393224 | tf_op jit(solution)/shard_map/ppermute | solution.py:356
  88.3 5.0 %collective-permute-start.21 = (f32[32,1024]{1,0:T(8,128)S(1)}, f32[32,1024]{1,0:T(8,128)S(1)}, u32[]{:S(2)}, u32[]{:S(2)}) collective-permute-start(f32[32,1024]{1,0:T(8,128)S(1)} %pad_maximum_fusion.9), channel_id=1, source_target_pairs={{0,8},{8,0},{16,24},{24,16},{32,40},{40,32},{48,56},{56,48},{64,72... | collective-permute-start | bytes 393224 | tf_op jit(solution)/shard_map/ppermute | solution.py:356
  90.2 6.6 %collective-permute-start.7 = (f32[40,1024]{1,0:T(8,128)S(1)}, f32[40,1024]{1,0:T(8,128)S(1)}, u32[]{:S(2)}, u32[]{:S(2)}) collective-permute-start(f32[40,1024]{1,0:T(8,128)S(1)} %pad_maximum_fusion.8), channel_id=1, source_target_pairs={{0,24},{8,16},{16,8},{24,0},{32,56},{40,48},{48,40},{56,32},{64,88... | collective-permute-start | bytes 491528 | tf_op jit(solution)/shard_map/ppermute | solution.py:356
  91.3 6.1 %collective-permute-start.11 = (f32[320,256]{1,0:T(8,128)S(1)}, f32[320,256]{1,0:T(8,128)S(1)}, u32[]{:S(2)}, u32[]{:S(2)}) collective-permute-start(f32[320,256]{1,0:T(8,128)S(1)} %add.177.mine_ref), channel_id=1, source_target_pairs={{0,1},{1,0},{2,3},{3,2},{4,5},{5,4},{6,7},{7,6},{8,9},{9,8},{10,11... | collective-permute-start | bytes 983048 | tf_op jit(solution)/shard_map/ppermute | solution.py:367
  91.5 6.0 %collective-permute-start.23 = (f32[32,1024]{1,0:T(8,128)S(1)}, f32[32,1024]{1,0:T(8,128)S(1)}, u32[]{:S(2)}, u32[]{:S(2)}) collective-permute-start(f32[32,1024]{1,0:T(8,128)S(1)} %pad_maximum_fusion.11), channel_id=1, source_target_pairs={{0,32},{8,40},{16,48},{24,56},{32,0},{40,8},{48,16},{56,24},{64,96... | collective-permute-start | bytes 393224 | tf_op jit(solution)/shard_map/ppermute | solution.py:356

commit v4 on v3

--- a/solution.py
+++ b/solution.py
@@ -37,8 +37,8 @@
 
 
 def stats_kernel(
-    f_ref, c_ref, dir_hbm, t_hbm, ub_ref, ut_ref, inv_ref, colsum_ref, stat_ref,
-    dbuf, tbuf, sacc, macc, tacc, dsem, tsem,
+    f_hbm, c_hbm, dir_hbm, t_hbm, ub_ref, ut_ref, inv_ref, colsum_ref, stat_ref,
+    f_ref, c_ref, dbuf, tbuf, sacc, macc, tacc, fsem, csem, dsem, tsem,
 ):
     rows = f_ref.shape[0]
     protos = dbuf.shape[1]
@@ -51,9 +51,15 @@
             pltpu.make_async_copy(t_hbm.at[:, cols], tbuf.at[:, cols], tsem.at[n]),
         )
 
+    f_copy = pltpu.make_async_copy(f_hbm, f_ref, fsem)
+    c_copy = pltpu.make_async_copy(c_hbm, c_ref, csem)
+    f_copy.start()
     for n in range(tiles):
         for copy in copies(n):
             copy.start()
+        if n == 0:
+            c_copy.start()
+    f_copy.wait()
     zf = f_ref[...].astype(F32)
     inv = 1.0 / jnp.sqrt(jnp.sum(zf * zf, axis=-1, keepdims=True) + EPS)
     ub = (zf * inv).astype(BF16)
@@ -63,6 +69,8 @@
     macc[...] = jnp.full_like(macc, -1e30)
     tacc[...] = jnp.zeros_like(tacc)
     colsum_ref[...] = jnp.zeros_like(colsum_ref)
+
+    c_copy.wait()
 
     @pl.loop(0, tiles)
     def _(n):
@@ -225,14 +233,18 @@
     tiles = protos // STAT_TILE
     return pl.pallas_call(
         stats_kernel,
-        in_specs=[IN_VMEM, IN_VMEM] + [pl.BlockSpec(memory_space=pltpu.HBM)] * 2,
+        in_specs=[pl.BlockSpec(memory_space=pltpu.HBM)] * 4,
         out_specs=[IN_VMEM] * 5,
         scratch_shapes=[
+            pltpu.VMEM((rows, dim), BF16),
+            pltpu.VMEM((1, protos), F32),
             pltpu.VMEM((dim, protos), BF16),
             pltpu.VMEM((trows, protos), BF16),
             pltpu.VMEM((rows, 128), F32),
             pltpu.VMEM((trows, 128), F32),
             pltpu.VMEM((trows, 128), F32),
+            pltpu.SemaphoreType.DMA,
+            pltpu.SemaphoreType.DMA,
             pltpu.SemaphoreType.DMA((tiles,)),
             pltpu.SemaphoreType.DMA((tiles,)),
         ],

time: 99.4 us -> 98.1 us (0.987)
  Pallas kernels: 21.7 us -> 20.4 us
    pallas_call x1, Pallas kernels: 8.89 us -> 7.63 us  [stats_call(): pl.pallas_call(stats_kernel, in_specs=[pl.BlockSpec(memory_space=pltpu.HB...]
where the time goes in v4:
time: 98.1 us; the launch traced here: 97.3 us
  waiting for transfers between devices  37.7 us (38%)
  starting transfers between devices  25.4 us (26%)
  Pallas kernels  20.4 us (21%)
  blocking collectives  10.6 us (11%)
  other arithmetic  1.45 us (1%)
    ppermute x12, waiting for transfers between devices, on_device(): block = lax.ppermute(jnp.concatenate(out, axis=0), 'batch', ORDER[part][n])  20.3 us
    ppermute x8, waiting for transfers between devices, on_device(): lax.ppermute(send[p], 'batch', ORDER[p][0])  15.7 us
    ppermute x8, starting transfers between devices, on_device(): lax.ppermute(send[p], 'batch', ORDER[p][0])  13 us
    pallas_call x2, Pallas kernels, weight_call(): pl.pallas_call(functools.partial(weight_kernel, images, call), in_specs=[...  11.7 us
    all_to_all x1, blocking collectives, on_device(): stats = lax.all_to_all(jnp.broadcast_to(stat, (8, 8, 128)), 'proto', 0, 0)  10.6 us
    ppermute x12, starting transfers between devices, on_device(): block = lax.ppermute(jnp.concatenate(out, axis=0), 'batch', ORDER[part][n])  10.4 us
    pallas_call x1, Pallas kernels, stats_call(): pl.pallas_call(stats_kernel, in_specs=[pl.BlockSpec(memory_space=pltpu.HB...  7.63 us
  transfers between devices with their start and end apart: 24, of which 15 were waited for; matrix products, arithmetic and copies ran while one was open for 1% of the time, Pallas kernels for 6%

profile of v4, /device:TPU:0, one launch (start us, length us, event | category | flops | bytes accessed | tf_op | source)
XLA Modules:
  0.0 97.3 jit_solution(16311844595303589542)
XLA Ops:
  0.6 0.7 copy-done
  1.4 7.6 %stats.1 = (bf16[640,256]{1,0:T(8,128)(2,1)S(1)}, bf16[256,640]{1,0:T(8,128)(2,1)S(1)}, f32[1,8192]{1,0:T(1,128)S(1)}, f32[8,1024]{1,0:T(8,128)S(1)}, f32[8,128]{1,0:T(8,128)S(1)}) custom-call(bf16[640,256]{1,0:T(8,128)(2,1)} %bitcast.12, f32[1,8192]{1,0:T(1,128)S(1)} %bitcast.5, bf16[256,8192]{1,0:T(8,128)(2,1)} %refs_2_.3, bf16[128,8192]{1,0:T(8,128)(2,1)} %bitcast.9), custom_call_target="tpu_custom_call" | custom-call | flops 2684354560 | bytes 6291456 | tf_op jit(solution)/shard_map/stats/pallas_call | solution.py:234
  9.0 10.6 %all_to_all.5.refs_6_ = f32[8,8,128]{2,1,0:T(8,128)S(1)} all-to-all(f32[8,8,128]{2,1,0:T(8,128)S(1)} %broadcast_in_dim.3), channel_id=1, replica_groups=mesh['batch'=16,'proto'=8] {'proto'}, dimensions={0} | all-to-all | bytes 65536 | tf_op jit(solution)/shard_map/all_to_all | solution.py:336
  19.7 5.7 %weights.2 = (f32[128,1024]{1,0:T(8,128)S(1)}, f32[128,1024]{1,0:T(8,128)S(1)}, f32[128,1024]{1,0:T(8,128)S(1)}, f32[128,1024]{1,0:T(8,128)S(1)}, f32[136,1024]{...) custom-call(bf16[640,256]{1,0:T(8,128)(2,1)S(1)} %get-tuple-element., ...), custom_call_target="tpu_custom_call" | custom-call | flops 4026531840 | bytes 7340032 | tf_op jit(solution)/shard_map/weights/pallas_call | solution.py:280
  25.4 3.1 %collective-permute-start.2 = (f32[128,1024]{1,0:T(8,128)S(1)}, f32[128,1024]{1,0:T(8,128)S(1)}, u32[]{:S(2)}, u32[]{:S(2)}) collective-permute-start(f32[128,1024]{1,0:T(8,128)S(1)} %get-tuple-element.63), channel_id=1, source_target_pairs={{0,24},{8,16},{16,8},{24,0},{32,56},{40,48},{48,40},{56,32},{64,88... | collective-permute-start | bytes 1572872 | tf_op jit(solution)/shard_map/ppermute | solution.py:345
  28.5 0.2 collective-permute-start.3
  28.7 2.8 %collective-permute-start.4 = (f32[128,1024]{1,0:T(8,128)S(1)}, f32[128,1024]{1,0:T(8,128)S(1)}, u32[]{:S(2)}, u32[]{:S(2)}) collective-permute-start(f32[128,1024]{1,0:T(8,128)S(1)} %get-tuple-element.65), channel_id=1, source_target_pairs={{0,96},{8,104},{16,112},{24,120},{32,64},{40,72},{48,80},{56,88},{... | collective-permute-start | bytes 1572872 | tf_op jit(solution)/shard_map/ppermute | solution.py:345
  31.4 0.2 collective-permute-start
  31.6 6.0 %weights.3 = (f32[128,1024]{1,0:T(8,128)S(1)}, f32[128,1024]{1,0:T(8,128)S(1)}, f32[128,1024]{1,0:T(8,128)S(1)}, f32[128,1024]{1,0:T(8,128)S(1)}, f32[128,1024]{...) custom-call(bf16[640,256]{1,0:T(8,128)(2,1)S(1)} %get-tuple-element., ...), custom_call_target="tpu_custom_call" | custom-call | flops 4026531840 | bytes 7340032 | tf_op jit(solution)/shard_map/weights/pallas_call | solution.py:280
  37.6 1.9 %collective-permute-start.1 = (f32[128,1024]{1,0:T(8,128)S(1)}, f32[128,1024]{1,0:T(8,128)S(1)}, u32[]{:S(2)}, u32[]{:S(2)}) collective-permute-start(f32[128,1024]{1,0:T(8,128)S(1)} %get-tuple-element.62), channel_id=1, source_target_pairs={{0,32},{8,40},{16,48},{24,56},{32,0},{40,8},{48,16},{56,24},{64,96... | collective-permute-start | bytes 1572872 | tf_op jit(solution)/shard_map/ppermute | solution.py:345
  39.5 3.5 %collective-permute-done.4 = f32[128,1024]{1,0:T(8,128)S(1)} collective-permute-done((f32[128,1024]{1,0:T(8,128)S(1)}, f32[128,1024]{1,0:T(8,128)S(1)}, u32[]{:S(2)}, u32[]{:S(2)}) %collective-permute-start.4) | collective-permute-done | bytes 524320 | tf_op jit(solution)/shard_map/ppermute | solution.py:345
  43.0 2.8 %collective-permute-start.12 = (f32[128,1024]{1,0:T(8,128)S(1)}, f32[128,1024]{1,0:T(8,128)S(1)}, u32[]{:S(2)}, u32[]{:S(2)}) collective-permute-start(f32[128,1024]{1,0:T(8,128)S(1)} %get-tuple-element.75), channel_id=1, source_target_pairs={{0,96},{8,104},{16,112},{24,120},{32,64},{40,72},{48,80},{56,88},{... | collective-permute-start | bytes 1572872 | tf_op jit(solution)/shard_map/ppermute | solution.py:345
  45.8 1.2 %collective-permute-done = f32[136,1024]{1,0:T(8,128)S(1)} collective-permute-done((f32[136,1024]{1,0:T(8,128)S(1)}, f32[136,1024]{1,0:T(8,128)S(1)}, u32[]{:S(2)}, u32[]{:S(2)}) %collective-permute-start) | collective-permute-done | bytes 557088 | tf_op jit(solution)/shard_map/ppermute | solution.py:345
  47.0 1.9 %collective-permute-start.15 = (f32[128,1024]{1,0:T(8,128)S(1)}, f32[128,1024]{1,0:T(8,128)S(1)}, u32[]{:S(2)}, u32[]{:S(2)}) collective-permute-start(f32[128,1024]{1,0:T(8,128)S(1)} %get-tuple-element.81), channel_id=1, source_target_pairs={{0,8},{8,0},{16,24},{24,16},{32,40},{40,32},{48,56},{56,48},{64,72... | collective-permute-start | bytes 1572872 | tf_op jit(solution)/shard_map/ppermute | solution.py:345
  48.9 0.0 collective-permute-done.3
  48.9 0.2 collective-permute-start.18
  49.1 0.0 collective-permute-done.2
  49.1 7.2 %collective-permute-done.1 = f32[128,1024]{1,0:T(8,128)S(1)} collective-permute-done((f32[128,1024]{1,0:T(8,128)S(1)}, f32[128,1024]{1,0:T(8,128)S(1)}, u32[]{:S(2)}, u32[]{:S(2)}) %collective-permute-start.1) | collective-permute-done | bytes 524320 | tf_op jit(solution)/shard_map/ppermute | solution.py:345
  56.2 0.1 slice_add_fusion.12
  56.3 0.2 collective-permute-done.12
  56.5 0.1 slice_add_fusion.10
  56.6 0.2 collective-permute-start.13
  56.8 0.1 slice_add_fusion.8
  56.9 0.9 collective-permute-done.15
  57.8 0.1 slice_add_fusion.6
  57.9 0.9 collective-permute-start.16
  58.8 0.1 slice_add_fusion.4
  58.8 0.1 slice_add_fusion.14
  58.9 2.8 %collective-permute-done.18 = f32[128,1024]{1,0:T(8,128)S(1)} collective-permute-done((f32[128,1024]{1,0:T(8,128)S(1)}, f32[128,1024]{1,0:T(8,128)S(1)}, u32[]{:S(2)}, u32[]{:S(2)}) %collective-permute-start.18) | collective-permute-done | bytes 524320 | tf_op jit(solution)/shard_map/ppermute | solution.py:345
  61.7 0.1 slice_add_fusion
  61.9 0.1 collective-permute-start.5
  62.0 0.1 slice_add_fusion.2
  62.1 0.1 collective-permute-start.19
  62.2 0.1 collective-permute-start.8
  62.3 1.6 %collective-permute-done.8 = f32[320,256]{1,0:T(8,128)S(1)} collective-permute-done((f32[320,256]{1,0:T(8,128)S(1)}, f32[320,256]{1,0:T(8,128)S(1)}, u32[]{:S(2)}, u32[]{:S(2)}) %collective-permute-start.8) | collective-permute-done | bytes 327712 | tf_op jit(solution)/shard_map/ppermute | solution.py:376
  63.9 0.6 collective-permute-start.9
  64.6 3.9 %collective-permute-done.13 = f32[128,1024]{1,0:T(8,128)S(1)} collective-permute-done((f32[128,1024]{1,0:T(8,128)S(1)}, f32[128,1024]{1,0:T(8,128)S(1)}, u32[]{:S(2)}, u32[]{:S(2)}) %collective-permute-start.13) | collective-permute-done | bytes 524320 | tf_op jit(solution)/shard_map/ppermute | solution.py:368
  68.5 4.2 %collective-permute-done.5 = f32[136,1024]{1,0:T(8,128)S(1)} collective-permute-done((f32[136,1024]{1,0:T(8,128)S(1)}, f32[136,1024]{1,0:T(8,128)S(1)}, u32[]{:S(2)}, u32[]{:S(2)}) %collective-permute-start.5) | collective-permute-done | bytes 557088 | tf_op jit(solution)/shard_map/ppermute | solution.py:368
  72.7 0.0 collective-permute-done.16
  72.7 0.0 collective-permute-done.19
  72.7 0.1 slice_add_fusion.24
  72.8 1.7 %collective-permute-start.14 = (f32[64,1024]{1,0:T(8,128)S(1)}, f32[64,1024]{1,0:T(8,128)S(1)}, u32[]{:S(2)}, u32[]{:S(2)}) collective-permute-start(f32[64,1024]{1,0:T(8,128)S(1)} %pad_maximum_fusion.5), channel_id=1, source_target_pairs={{0,24},{8,16},{16,8},{24,0},{32,56},{40,48},{48,40},{56,32},{64,88... | collective-permute-start | bytes 786440 | tf_op jit(solution)/shard_map/ppermute | solution.py:368
  74.6 0.1 slice_add_fusion.20
  74.7 1.2 %collective-permute-start.17 = (f32[64,1024]{1,0:T(8,128)S(1)}, f32[64,1024]{1,0:T(8,128)S(1)}, u32[]{:S(2)}, u32[]{:S(2)}) collective-permute-start(f32[64,1024]{1,0:T(8,128)S(1)} %pad_maximum_fusion.6), channel_id=1, source_target_pairs={{0,32},{8,40},{16,48},{24,56},{32,0},{40,8},{48,16},{56,24},{64,96... | collective-permute-start | bytes 786440 | tf_op jit(solution)/shard_map/ppermute | solution.py:368
  75.9 0.1 slice_add_fusion.29
  76.0 0.4 collective-permute-start.6
  76.3 0.1 slice_add_fusion.16
  76.4 1.5 %collective-permute-start.20 = (f32[64,1024]{1,0:T(8,128)S(1)}, f32[64,1024]{1,0:T(8,128)S(1)}, u32[]{:S(2)}, u32[]{:S(2)}) collective-permute-start(f32[64,1024]{1,0:T(8,128)S(1)} %pad_maximum_fusion.7), channel_id=1, source_target_pairs={{0,96},{8,104},{16,112},{24,120},{32,64},{40,72},{48,80},{56,88},{... | collective-permute-start | bytes 786440 | tf_op jit(solution)/shard_map/ppermute | solution.py:368
  77.9 0.0 collective-permute-done.9
  77.9 1.2 %collective-permute-start.10 = (f32[320,256]{1,0:T(8,128)S(1)}, f32[320,256]{1,0:T(8,128)S(1)}, u32[]{:S(2)}, u32[]{:S(2)}) collective-permute-start(f32[320,256]{1,0:T(8,128)S(1)} %add.176), channel_id=1, source_target_pairs={{0,6},{1,7},{2,4},{3,5},{4,2},{5,3},{6,0},{7,1},{8,14},{9,15},{10,... | collective-permute-start | bytes 983048 | tf_op jit(solution)/shard_map/ppermute | solution.py:378
  79.2 1.3 %collective-permute-done.14 = f32[64,1024]{1,0:T(8,128)S(1)} collective-permute-done((f32[64,1024]{1,0:T(8,128)S(1)}, f32[64,1024]{1,0:T(8,128)S(1)}, u32[]{:S(2)}, u32[]{:S(2)}) %collective-permute-start.14) | collective-permute-done | bytes 262176 | tf_op jit(solution)/shard_map/ppermute | solution.py:368
  80.5 2.5 %collective-permute-done.6 = f32[72,1024]{1,0:T(8,128)S(1)} collective-permute-done((f32[72,1024]{1,0:T(8,128)S(1)}, f32[72,1024]{1,0:T(8,128)S(1)}, u32[]{:S(2)}, u32[]{:S(2)}) %collective-permute-start.6) | collective-permute-done | bytes 294944 | tf_op jit(solution)/shard_map/ppermute | solution.py:368
  83.0 0.0 collective-permute-done.17
  83.0 2.5 %collective-permute-done.20 = f32[64,1024]{1,0:T(8,128)S(1)} collective-permute-done((f32[64,1024]{1,0:T(8,128)S(1)}, f32[64,1024]{1,0:T(8,128)S(1)}, u32[]{:S(2)}, u32[]{:S(2)}) %collective-permute-start.20) | collective-permute-done | bytes 262176 | tf_op jit(solution)/shard_map/ppermute | solution.py:368
  85.5 1.5 %collective-permute-start.22 = (f32[32,1024]{1,0:T(8,128)S(1)}, f32[32,1024]{1,0:T(8,128)S(1)}, u32[]{:S(2)}, u32[]{:S(2)}) collective-permute-start(f32[32,1024]{1,0:T(8,128)S(1)} %pad_maximum_fusion.10), channel_id=1, source_target_pairs={{0,96},{8,104},{16,112},{24,120},{32,64},{40,72},{48,80},{56,88},{... | collective-permute-start | bytes 393224 | tf_op jit(solution)/shard_map/ppermute | solution.py:368
  87.1 1.8 %collective-permute-start.21 = (f32[32,1024]{1,0:T(8,128)S(1)}, f32[32,1024]{1,0:T(8,128)S(1)}, u32[]{:S(2)}, u32[]{:S(2)}) collective-permute-start(f32[32,1024]{1,0:T(8,128)S(1)} %pad_maximum_fusion.9), channel_id=1, source_target_pairs={{0,8},{8,0},{16,24},{24,16},{32,40},{40,32},{48,56},{56,48},{64,72... | collective-permute-start | bytes 393224 | tf_op jit(solution)/shard_map/ppermute | solution.py:368
  89.0 1.0 %collective-permute-start.7 = (f32[40,1024]{1,0:T(8,128)S(1)}, f32[40,1024]{1,0:T(8,128)S(1)}, u32[]{:S(2)}, u32[]{:S(2)}) collective-permute-start(f32[40,1024]{1,0:T(8,128)S(1)} %pad_maximum_fusion.8), channel_id=1, source_target_pairs={{0,24},{8,16},{16,8},{24,0},{32,56},{40,48},{48,40},{56,32},{64,88... | collective-permute-start | bytes 491528 | tf_op jit(solution)/shard_map/ppermute | solution.py:368
  90.0 0.1 collective-permute-start.11
  90.2 0.1 collective-permute-start.23
  90.3 1.8 %collective-permute-done.21.refs_9_ = f32[32,1024]{1,0:T(8,128)S(1)} collective-permute-done((f32[32,1024]{1,0:T(8,128)S(1)}, f32[32,1024]{1,0:T(8,128)S(1)}, u32[]{:S(2)}, u32[]{:S(2)}) %collective-permute-start.21) | collective-permute-done | bytes 131104 | tf_op jit(solution)/shard_map/ppermute | solution.py:368
  92.1 3.5 %collective-permute-done.7.refs_8_ = f32[40,1024]{1,0:T(8,128)S(1)} collective-permute-done((f32[40,1024]{1,0:T(8,128)S(1)}, f32[40,1024]{1,0:T(8,128)S(1)}, u32[]{:S(2)}, u32[]{:S(2)}) %collective-permute-start.7) | collective-permute-done | bytes 163872 | tf_op jit(solution)/shard_map/ppermute | solution.py:368
  95.6 0.6 collective-permute-done.23.refs_11_
  96.2 0.0 collective-permute-done.11.other_ref
  96.2 1.1 %final.1 = (f32[640,256]{1,0:T(8,128)}, f32[16,8192]{1,0:T(8,128)}, f32[1,8192]{1,0:T(1,128)}) custom-call(f32[1,8192]{1,0:T(1,128)S(1)} %bitcast.8, f32[8,1024]{1,0:T(8,128)S(1)} %slice_add_fusion.48.cs_ref, f32[8,1024]{1,0:T(8,128)S(1)} %slice.468.csgot_ref, f32[320,256]{1,0:T(8,128)S(1)} %add.177.mine_ref, ...), custom_call_target="tpu_custom_call" | custom-call | tf_op jit(solution)/shard_map/final/pallas_call | solution.py:301
  (33 shorter events, 0.6 us)
Async XLA Ops:
  0.6 0.8 copy-start
  1.4 18.3 %copy-start.1 = (bf16[256,8192]{1,0:T(8,128)(2,1)S(1)}, bf16[256,8192]{1,0:T(8,128)(2,1)}, u32[]{:S(2)}) copy-start(bf16[256,8192]{1,0:T(8,128)(2,1)} %refs_2_.3) | copy-start | bytes 12582916
  1.4 18.3 %copy-start.2 = (bf16[2,64,8192]{2,1,0:T(8,128)(2,1)S(1)}, bf16[2,64,8192]{2,1,0:T(8,128)(2,1)}, u32[]{:S(2)}) copy-start(bf16[2,64,8192]{2,1,0:T(8,128)(2,1)} %param.5) | copy-start | bytes 6291460
  19.7 11.9 %copy-start.3 = (bf16[10,64,256]{2,1,0:T(8,128)(2,1)S(1)}, bf16[10,64,256]{2,1,0:T(8,128)(2,1)}, u32[]{:S(2)}) copy-start(bf16[10,64,256]{2,1,0:T(8,128)(2,1)} %param.4) | copy-start | bytes 983044
  25.4 23.7 %collective-permute-start.2 = (f32[128,1024]{1,0:T(8,128)S(1)}, f32[128,1024]{1,0:T(8,128)S(1)}, u32[]{:S(2)}, u32[]{:S(2)}) collective-permute-start(f32[128,1024]{1,0:T(8,128)S(1)} %get-tuple-element.63), channel_id=1, source_target_pairs={{0,24},{8,16},{16,8},{24,0},{32,56},{40,48},{48,40},{56,32},{64,88... | collective-permute-start | bytes 1572872 | tf_op jit(solution)/shard_map/ppermute | solution.py:345
  28.5 20.4 %collective-permute-start.3 = (f32[128,1024]{1,0:T(8,128)S(1)}, f32[128,1024]{1,0:T(8,128)S(1)}, u32[]{:S(2)}, u32[]{:S(2)}) collective-permute-start(f32[128,1024]{1,0:T(8,128)S(1)} %get-tuple-element.64), channel_id=1, source_target_pairs={{0,8},{8,0},{16,24},{24,16},{32,40},{40,32},{48,56},{56,48},{64,72... | collective-permute-start | bytes 1572872 | tf_op jit(solution)/shard_map/ppermute | solution.py:345
  28.7 14.4 %collective-permute-start.4 = (f32[128,1024]{1,0:T(8,128)S(1)}, f32[128,1024]{1,0:T(8,128)S(1)}, u32[]{:S(2)}, u32[]{:S(2)}) collective-permute-start(f32[128,1024]{1,0:T(8,128)S(1)} %get-tuple-element.65), channel_id=1, source_target_pairs={{0,96},{8,104},{16,112},{24,120},{32,64},{40,72},{48,80},{56,88},{... | collective-permute-start | bytes 1572872 | tf_op jit(solution)/shard_map/ppermute | solution.py:345
  31.4 15.6 %collective-permute-start = (f32[136,1024]{1,0:T(8,128)S(1)}, f32[136,1024]{1,0:T(8,128)S(1)}, u32[]{:S(2)}, u32[]{:S(2)}) collective-permute-start(f32[136,1024]{1,0:T(8,128)S(1)} %get-tuple-element.55), channel_id=1, source_target_pairs={{0,32},{8,40},{16,48},{24,56},{32,0},{40,8},{48,16},{56,24},{64,96... | collective-permute-start | bytes 1671176 | tf_op jit(solution)/shard_map/ppermute | solution.py:345
  37.6 18.6 %collective-permute-start.1 = (f32[128,1024]{1,0:T(8,128)S(1)}, f32[128,1024]{1,0:T(8,128)S(1)}, u32[]{:S(2)}, u32[]{:S(2)}) collective-permute-start(f32[128,1024]{1,0:T(8,128)S(1)} %get-tuple-element.62), channel_id=1, source_target_pairs={{0,32},{8,40},{16,48},{24,56},{32,0},{40,8},{48,16},{56,24},{64,96... | collective-permute-start | bytes 1572872 | tf_op jit(solution)/shard_map/ppermute | solution.py:345
  43.0 13.5 %collective-permute-start.12 = (f32[128,1024]{1,0:T(8,128)S(1)}, f32[128,1024]{1,0:T(8,128)S(1)}, u32[]{:S(2)}, u32[]{:S(2)}) collective-permute-start(f32[128,1024]{1,0:T(8,128)S(1)} %get-tuple-element.75), channel_id=1, source_target_pairs={{0,96},{8,104},{16,112},{24,120},{32,64},{40,72},{48,80},{56,88},{... | collective-permute-start | bytes 1572872 | tf_op jit(solution)/shard_map/ppermute | solution.py:345
  47.0 10.8 %collective-permute-start.15 = (f32[128,1024]{1,0:T(8,128)S(1)}, f32[128,1024]{1,0:T(8,128)S(1)}, u32[]{:S(2)}, u32[]{:S(2)}) collective-permute-start(f32[128,1024]{1,0:T(8,128)S(1)} %get-tuple-element.81), channel_id=1, source_target_pairs={{0,8},{8,0},{16,24},{24,16},{32,40},{40,32},{48,56},{56,48},{64,72... | collective-permute-start | bytes 1572872 | tf_op jit(solution)/shard_map/ppermute | solution.py:345
  48.9 12.9 %collective-permute-start.18 = (f32[128,1024]{1,0:T(8,128)S(1)}, f32[128,1024]{1,0:T(8,128)S(1)}, u32[]{:S(2)}, u32[]{:S(2)}) collective-permute-start(f32[128,1024]{1,0:T(8,128)S(1)} %get-tuple-element.87), channel_id=1, source_target_pairs={{0,24},{8,16},{16,8},{24,0},{32,56},{40,48},{48,40},{56,32},{64,88... | collective-permute-start | bytes 1572872 | tf_op jit(solution)/shard_map/ppermute | solution.py:345
  56.6 11.9 %collective-permute-start.13 = (f32[128,1024]{1,0:T(8,128)S(1)}, f32[128,1024]{1,0:T(8,128)S(1)}, u32[]{:S(2)}, u32[]{:S(2)}) collective-permute-start(f32[128,1024]{1,0:T(8,128)S(1)} %pad_maximum_fusion.1), channel_id=1, source_target_pairs={{0,32},{8,40},{16,48},{24,56},{32,0},{40,8},{48,16},{56,24},{64,96... | collective-permute-start | bytes 1572872 | tf_op jit(solution)/shard_map/ppermute | solution.py:368
  57.9 14.8 %collective-permute-start.16 = (f32[128,1024]{1,0:T(8,128)S(1)}, f32[128,1024]{1,0:T(8,128)S(1)}, u32[]{:S(2)}, u32[]{:S(2)}) collective-permute-start(f32[128,1024]{1,0:T(8,128)S(1)} %pad_maximum_fusion.2), channel_id=1, source_target_pairs={{0,24},{8,16},{16,8},{24,0},{32,56},{40,48},{48,40},{56,32},{64,88... | collective-permute-start | bytes 1572872 | tf_op jit(solution)/shard_map/ppermute | solution.py:368
  61.9 10.8 %collective-permute-start.5 = (f32[136,1024]{1,0:T(8,128)S(1)}, f32[136,1024]{1,0:T(8,128)S(1)}, u32[]{:S(2)}, u32[]{:S(2)}) collective-permute-start(f32[136,1024]{1,0:T(8,128)S(1)} %pad_maximum_fusion), channel_id=1, source_target_pairs={{0,96},{8,104},{16,112},{24,120},{32,64},{40,72},{48,80},{56,88},{... | collective-permute-start | bytes 1671176 | tf_op jit(solution)/shard_map/ppermute | solution.py:368
  62.1 10.6 %collective-permute-start.19 = (f32[128,1024]{1,0:T(8,128)S(1)}, f32[128,1024]{1,0:T(8,128)S(1)}, u32[]{:S(2)}, u32[]{:S(2)}) collective-permute-start(f32[128,1024]{1,0:T(8,128)S(1)} %pad_maximum_fusion.3), channel_id=1, source_target_pairs={{0,8},{8,0},{16,24},{24,16},{32,40},{40,32},{48,56},{56,48},{64,72... | collective-permute-start | bytes 1572872 | tf_op jit(solution)/shard_map/ppermute | solution.py:368
  62.2 1.7 %collective-permute-start.8 = (f32[320,256]{1,0:T(8,128)S(1)}, f32[320,256]{1,0:T(8,128)S(1)}, u32[]{:S(2)}, u32[]{:S(2)}) collective-permute-start(f32[320,256]{1,0:T(8,128)S(1)} %get-tuple-element.72), channel_id=1, source_target_pairs={{0,1},{1,0},{2,3},{3,2},{4,5},{5,4},{6,7},{7,6},{8,9},{9,8},{10,11... | collective-permute-start | bytes 983048 | tf_op jit(solution)/shard_map/ppermute | solution.py:376
  63.9 14.0 %collective-permute-start.9 = (f32[320,256]{1,0:T(8,128)S(1)}, f32[320,256]{1,0:T(8,128)S(1)}, u32[]{:S(2)}, u32[]{:S(2)}) collective-permute-start(f32[320,256]{1,0:T(8,128)S(1)} %add.175), channel_id=1, source_target_pairs={{0,2},{1,3},{2,0},{3,1},{4,6},{5,7},{6,4},{7,5},{8,10},{9,11},{10,... | collective-permute-start | bytes 983048 | tf_op jit(solution)/shard_map/ppermute | solution.py:377
  72.8 7.7 %collective-permute-start.14 = (f32[64,1024]{1,0:T(8,128)S(1)}, f32[64,1024]{1,0:T(8,128)S(1)}, u32[]{:S(2)}, u32[]{:S(2)}) collective-permute-start(f32[64,1024]{1,0:T(8,128)S(1)} %pad_maximum_fusion.5), channel_id=1, source_target_pairs={{0,24},{8,16},{16,8},{24,0},{32,56},{40,48},{48,40},{56,32},{64,88... | collective-permute-start | bytes 786440 | tf_op jit(solution)/shard_map/ppermute | solution.py:368
  74.7 8.4 %collective-permute-start.17 = (f32[64,1024]{1,0:T(8,128)S(1)}, f32[64,1024]{1,0:T(8,128)S(1)}, u32[]{:S(2)}, u32[]{:S(2)}) collective-permute-start(f32[64,1024]{1,0:T(8,128)S(1)} %pad_maximum_fusion.6), channel_id=1, source_target_pairs={{0,32},{8,40},{16,48},{24,56},{32,0},{40,8},{48,16},{56,24},{64,96... | collective-permute-start | bytes 786440 | tf_op jit(solution)/shard_map/ppermute | solution.py:368
  76.0 7.0 %collective-permute-start.6 = (f32[72,1024]{1,0:T(8,128)S(1)}, f32[72,1024]{1,0:T(8,128)S(1)}, u32[]{:S(2)}, u32[]{:S(2)}) collective-permute-start(f32[72,1024]{1,0:T(8,128)S(1)} %pad_maximum_fusion.4), channel_id=1, source_target_pairs={{0,8},{8,0},{16,24},{24,16},{32,40},{40,32},{48,56},{56,48},{64,72... | collective-permute-start | bytes 884744 | tf_op jit(solution)/shard_map/ppermute | solution.py:368
  76.4 9.1 %collective-permute-start.20 = (f32[64,1024]{1,0:T(8,128)S(1)}, f32[64,1024]{1,0:T(8,128)S(1)}, u32[]{:S(2)}, u32[]{:S(2)}) collective-permute-start(f32[64,1024]{1,0:T(8,128)S(1)} %pad_maximum_fusion.7), channel_id=1, source_target_pairs={{0,96},{8,104},{16,112},{24,120},{32,64},{40,72},{48,80},{56,88},{... | collective-permute-start | bytes 786440 | tf_op jit(solution)/shard_map/ppermute | solution.py:368
  77.9 12.1 %collective-permute-start.10 = (f32[320,256]{1,0:T(8,128)S(1)}, f32[320,256]{1,0:T(8,128)S(1)}, u32[]{:S(2)}, u32[]{:S(2)}) collective-permute-start(f32[320,256]{1,0:T(8,128)S(1)} %add.176), channel_id=1, source_target_pairs={{0,6},{1,7},{2,4},{3,5},{4,2},{5,3},{6,0},{7,1},{8,14},{9,15},{10,... | collective-permute-start | bytes 983048 | tf_op jit(solution)/shard_map/ppermute | solution.py:378
  85.5 10.0 %collective-permute-start.22 = (f32[32,1024]{1,0:T(8,128)S(1)}, f32[32,1024]{1,0:T(8,128)S(1)}, u32[]{:S(2)}, u32[]{:S(2)}) collective-permute-start(f32[32,1024]{1,0:T(8,128)S(1)} %pad_maximum_fusion.10), channel_id=1, source_target_pairs={{0,96},{8,104},{16,112},{24,120},{32,64},{40,72},{48,80},{56,88},{... | collective-permute-start | bytes 393224 | tf_op jit(solution)/shard_map/ppermute | solution.py:368
  87.1 5.0 %collective-permute-start.21 = (f32[32,1024]{1,0:T(8,128)S(1)}, f32[32,1024]{1,0:T(8,128)S(1)}, u32[]{:S(2)}, u32[]{:S(2)}) collective-permute-start(f32[32,1024]{1,0:T(8,128)S(1)} %pad_maximum_fusion.9), channel_id=1, source_target_pairs={{0,8},{8,0},{16,24},{24,16},{32,40},{40,32},{48,56},{56,48},{64,72... | collective-permute-start | bytes 393224 | tf_op jit(solution)/shard_map/ppermute | solution.py:368
  89.0 6.6 %collective-permute-start.7 = (f32[40,1024]{1,0:T(8,128)S(1)}, f32[40,1024]{1,0:T(8,128)S(1)}, u32[]{:S(2)}, u32[]{:S(2)}) collective-permute-start(f32[40,1024]{1,0:T(8,128)S(1)} %pad_maximum_fusion.8), channel_id=1, source_target_pairs={{0,24},{8,16},{16,8},{24,0},{32,56},{40,48},{48,40},{56,32},{64,88... | collective-permute-start | bytes 491528 | tf_op jit(solution)/shard_map/ppermute | solution.py:368
  90.0 6.1 %collective-permute-start.11 = (f32[320,256]{1,0:T(8,128)S(1)}, f32[320,256]{1,0:T(8,128)S(1)}, u32[]{:S(2)}, u32[]{:S(2)}) collective-permute-start(f32[320,256]{1,0:T(8,128)S(1)} %add.177.mine_ref), channel_id=1, source_target_pairs={{0,1},{1,0},{2,3},{3,2},{4,5},{5,4},{6,7},{7,6},{8,9},{9,8},{10,11... | collective-permute-start | bytes 983048 | tf_op jit(solution)/shard_map/ppermute | solution.py:379
  90.2 6.0 %collective-permute-start.23 = (f32[32,1024]{1,0:T(8,128)S(1)}, f32[32,1024]{1,0:T(8,128)S(1)}, u32[]{:S(2)}, u32[]{:S(2)}) collective-permute-start(f32[32,1024]{1,0:T(8,128)S(1)} %pad_maximum_fusion.11), channel_id=1, source_target_pairs={{0,32},{8,40},{16,48},{24,56},{32,0},{40,8},{48,16},{56,24},{64,96... | collective-permute-start | bytes 393224 | tf_op jit(solution)/shard_map/ppermute | solution.py:368
